TPU v7x, 32 devices: a whole 2x2x4 slice. The times are simulated.
32 devices in a mesh: grp: 2 (over y), sp: 4 (over z), ch: 4 (over x, core).
Axes of the slice: x: 2, y: 2, z: 4, core: 2. Of those that a mesh axis runs over, the one named last changes fastest.
Arguments:
- state_field: bfloat16 [512, 768, 1440], P(('grp', 'ch'), 'sp'), parts along dimension 0, may hold values from -6 to 6
- spectral_weight: bfloat16 [2, 256, 256, 256], P(None, 'sp', 'ch'), may hold values from -0.5 to 0.5
- mode_gain: float32 [256, 320], P('ch'), may hold values from 0.5 to 2
- bypass_weight: bfloat16 [256, 256], replicated, may hold values from -0.375 to 0.375
Outputs:
- block_output: bfloat16 [512, 768, 1440], P(('grp', 'ch'), 'sp'), parts along dimension 0
There are 2 independent parts, one for each index of `grp`. A program takes and returns all parts, laid end to end along the dimension named above; an argument that names none is the same for every part. Nothing has to cross between parts.
All inputs are finite; a program needn't handle non-finite values.
Results may differ from a plain program's by a relative error of at most 0.0069.
Values may be sent and summed in bfloat16 or wider, within the bound.
No kernel may reach another device: no remote copies, remote signals or barrier semaphores. Data moves between devices by JAX's collectives and lax.ppermute only.
A program may use at most 576 MiB of HBM per device.

v0:
```python
import math

import jax
import jax.numpy as jnp
from jax import lax
from jax.sharding import PartitionSpec as P

LAT = 768
LON = 1440
M = 256
L = 320


def make_tables():
    lon_index = jnp.arange(LON, dtype=jnp.int32)
    mode_index = jnp.arange(M, dtype=jnp.int32)
    phase_lon = jnp.mod(lon_index[:, None] * mode_index[None, :], LON).astype(jnp.float32) * (
        2.0 * math.pi / LON
    )
    fwd_lon = jnp.stack([jnp.cos(phase_lon), -jnp.sin(phase_lon)], axis=1).astype(jnp.bfloat16)
    mode_weight = jnp.where(mode_index == 0, 1.0, 2.0).astype(jnp.float32)
    inv_lon = jnp.stack(
        [mode_weight[:, None] * jnp.cos(phase_lon).T, -mode_weight[:, None] * jnp.sin(phase_lon).T],
        axis=0,
    ).astype(jnp.bfloat16)
    lat_index = jnp.arange(LAT, dtype=jnp.int32)
    wave_index = jnp.arange(L, dtype=jnp.int32)
    wave_number = jnp.where(wave_index < L // 2, wave_index, wave_index - L)
    phase_lat = jnp.mod(lat_index[:, None] * wave_number[None, :], LAT).astype(jnp.float32) * (
        2.0 * math.pi / LAT
    )
    fwd_lat = jnp.stack([jnp.cos(phase_lat), jnp.sin(phase_lat)], axis=1).astype(jnp.bfloat16)
    inv_lat = jnp.stack([jnp.cos(phase_lat).T, jnp.sin(phase_lat).T], axis=1).astype(jnp.bfloat16)
    return (fwd_lon, inv_lon, fwd_lat, inv_lat)


def mix_modes(weights, inputs):
    out_real = jnp.einsum(
        "mcd,cmk->dmk", weights[0], inputs[:, 0], preferred_element_type=jnp.float32
    ) - jnp.einsum("mcd,cmk->dmk", weights[1], inputs[:, 1], preferred_element_type=jnp.float32)
    out_imag = jnp.einsum(
        "mcd,cmk->dmk", weights[1], inputs[:, 0], preferred_element_type=jnp.float32
    ) + jnp.einsum("mcd,cmk->dmk", weights[0], inputs[:, 1], preferred_element_type=jnp.float32)
    return jnp.stack([out_real, out_imag], axis=1)


def body(state_field, spectral_weight, mode_gain, bypass_weight):
    fwd_lon, inv_lon, fwd_lat, inv_lat = make_tables()
    chan_count = state_field.shape[0]
    band_rows = state_field.shape[1]
    flat_field = state_field.reshape(chan_count * band_rows, LON)
    lon_spectrum = (
        jnp.dot(flat_field, fwd_lon.reshape(LON, 2 * M), preferred_element_type=jnp.float32)
        .astype(jnp.bfloat16)
        .reshape(chan_count, band_rows, 2, M)
    )
    all_latitudes = lax.all_to_all(lon_spectrum, "sp", split_axis=3, concat_axis=1, tiled=True)
    lat_parts = jnp.einsum(
        "clrm,lsk->crmsk", all_latitudes, fwd_lat, preferred_element_type=jnp.float32
    )
    real_part = lat_parts[:, 0, :, 0] + lat_parts[:, 1, :, 1]
    imag_part = lat_parts[:, 1, :, 0] - lat_parts[:, 0, :, 1]
    modes_in = jnp.stack([real_part, imag_part], axis=1).astype(jnp.bfloat16)
    weight_rows = lax.all_to_all(spectral_weight, "ch", split_axis=3, concat_axis=2, tiled=True)
    all_inputs = lax.all_gather(modes_in, "ch", axis=0, tiled=True)
    mixed = mix_modes(weight_rows, all_inputs)
    scaled = (mixed * mode_gain[:, None, None, :]).astype(jnp.bfloat16)
    back_parts = jnp.einsum("drmk,ksl->drmsl", scaled, inv_lat, preferred_element_type=jnp.float32)
    back_real = back_parts[:, 0, :, 0] - back_parts[:, 1, :, 1]
    back_imag = back_parts[:, 0, :, 1] + back_parts[:, 1, :, 0]
    lat_field = (jnp.stack([back_real, back_imag], axis=1) * (1.0 / LAT)).astype(jnp.bfloat16)
    band_spectrum = lax.all_to_all(lat_field, "sp", split_axis=3, concat_axis=2, tiled=True)
    spectral_out = jnp.einsum(
        "drml,rmx->dlx", band_spectrum, inv_lon, preferred_element_type=jnp.float32
    ) * (1.0 / LON)
    out_width = bypass_weight.shape[1] // lax.axis_size("ch")
    own_columns = lax.dynamic_slice_in_dim(
        bypass_weight, lax.axis_index("ch") * out_width, out_width, 1
    )
    weight_rows = own_columns
    bypass = jnp.einsum(
        "cd,clx->dlx",
        weight_rows,
        lax.all_gather(state_field, "ch", axis=0, tiled=True),
        preferred_element_type=jnp.float32,
    ).astype(jnp.bfloat16)
    return jax.nn.gelu(spectral_out + bypass.astype(jnp.float32), approximate=False).astype(
        jnp.bfloat16
    )


def solution(mesh):
    in_specs = (P(("grp", "ch"), "sp", None), P(None, "sp", "ch", None), P("ch", None), P())
    out_specs = P(("grp", "ch"), "sp", None)
    return jax.shard_map(body, mesh=mesh, in_specs=in_specs, out_specs=out_specs, check_vma=False)
```

profile of v0, /device:TPU:0, one launch (start us, length us, event | category | flops | bytes accessed | tf_op | source)
XLA Modules:
  0.0 1884.5 jit_solution(16320505254363975959)
XLA Ops:
  6.5 0.0 copy-start
  6.5 6.5 negate_convert_fusion
  13.0 0.1 maximum_bitcast_fusion
  13.1 0.1 copy.156
  13.3 26.2 %fusion.12 = bf16[12288,512]{0,1:T(8,128)(2,1)} fusion(bf16[1440,512]{1,0:T(8,128)(2,1)S(1)} %bitcast.128, bf16[12288,1440]{1,0:T(8,128)(2,1)} %bitcast.123), kind=kOutput, calls=%fused_computation.25 | convolution fusion | flops 18125684736 | bytes 49446912 | tf_op jit(solution)/shard_map/dot_general | solution.py:53
  39.5 25.6 %reshape.429 = bf16[64,192,2,256]{1,0,3,2:T(8,128)(2,1)} reshape(bf16[12288,512]{0,1:T(8,128)(2,1)} %fusion.12) | data formatting | bytes 25165824 | tf_op jit(solution)/shard_map/reshape | solution.py:55
  65.1 14.1 copy.120
  79.2 7.0 all-to-all-start
  86.2 0.2 all-gather.3.cloned.1.call-start
  86.5 4.7 cosine_convert_fusion.2
  91.2 359.6 %all-to-all-done = bf16[64,192,2,256]{1,0,2,3:T(8,128)(2,1)} async-done(((bf16[64,192,2,256]{1,0,2,3:T(8,128)(2,1)}), bf16[64,192,2,256]{1,0,2,3:T(8,128)(2,1)}, u32[]{:S(2)}, u32[]{:S(2)}) %all-to-all-start) | async-done | bytes 12582944 | tf_op jit(solution)/shard_map/all_to_all | solution.py:57
  450.8 22.1 %copy.122 = bf16[64,4,192,2,64]{2,1,4,3,0:T(4,128)(2,1)} copy(bf16[64,4,192,2,64]{2,0,3,4,1:T(8,128)(2,1)} %bitcast.4) | data formatting | bytes 25165824 | tf_op jit(solution)/shard_map/all_to_all | solution.py:57
  472.9 28.5 %reshape.422 = bf16[64,768,2,64,1]{1,3,2,0,4:T(8,128)(2,1)} reshape(bf16[64,4,192,2,64]{2,1,4,3,0:T(4,128)(2,1)} %copy.122) | data formatting | bytes 25165824 | tf_op jit(solution)/shard_map/all_to_all | solution.py:57
  501.4 17.8 fusion.17
  519.3 6.1 fusion.26
  525.4 6.0 fusion.25
  531.4 3.8 pad_maximum_fusion
  535.2 0.0 all-gather.3.cloned.1.call-update
  535.2 0.3 all-gather.5.cloned.1.call-start
  535.5 34.8 %copy.138 = bf16[64,192,1440]{2,0,1:T(8,128)(2,1)} copy(bf16[64,192,1440]{2,1,0:T(8,128)(2,1)} %param.4) | data formatting | bytes 70778880 | tf_op args[0]
  570.3 0.0 all-gather.5.cloned.1.call-update
  570.3 13.0 copy.125
  583.3 9.5 reshape.431
  592.8 4.9 all-to-all-start.1
  597.7 4.7 cosine_convert_fusion.1
  602.4 88.7 %all-to-all-done.1 = bf16[4,2,262144]{2,1,0:T(2,128)(2,1)} async-done(((bf16[4,2,262144]{2,1,0:T(2,128)(2,1)}), bf16[4,2,262144]{2,1,0:T(2,128)(2,1)}, u32[]{:S(2)}, u32[]{:S(2)}) %all-to-all-start.1) | async-done | bytes 4194336 | tf_op jit(solution)/shard_map/all_to_all | solution.py:64
  691.2 9.3 reshape.432
  700.4 11.2 copy.164
  711.7 5.2 fusion.61
  716.9 6.0 squeeze.11
  722.9 7.0 squeeze.9
  729.8 3.4 all-gather.3.cloned.1.call-done
  733.3 23.4 %slice_bitcast_fusion.2 = (bf16[256,64,320]{2,1,0:T(8,128)(2,1)}, bf16[256,64,320]{2,1,0:T(8,128)(2,1)}) fusion(bf16[256,2,64,320]{3,2,0,1:T(8,128)(2,1)} %all-gather.3.cloned.1.call-done), kind=kLoop, calls=%fused_computation.32 | loop fusion | bytes 41943040 | tf_op jit(solution)/shard_map/squeeze | solution.py:40
  756.6 19.3 %copy.127 = bf16[256,64,320]{0,2,1:T(8,128)(2,1)} copy(bf16[256,64,320]{2,1,0:T(8,128)(2,1)} %get-tuple-element.6) | data formatting | bytes 20971520 | tf_op jit(solution)/shard_map/squeeze | solution.py:39
  775.9 18.6 copy.128
  794.5 14.1 fusion.63
  808.6 13.9 fusion.62
  822.5 14.0 add_bitcast_fusion
  836.5 0.0 copy-start.2
  836.5 12.0 subtract_bitcast_fusion
  848.5 0.0 copy-done.2
  848.5 8.8 fusion.19
  857.3 37.0 %fusion.23 = f32[64,2,64,2,768]{4,2,3,1,0:T(8,128)} fusion(bf16[64,2,64,320,1]{3,0,2,1,4:T(8,128)(2,1)} %fusion.19, bf16[320,1,768]{2,0,1:T(8,128)(2,1)S(1)} %get-tuple-element.10, bf16[320,1,768]{2,0,1:T(8,128)(2,1)S(1)} %get-tuple-element.9), kind=kOutput, calls=%fused_computation.47 | convolution fusion | flops 8055029760 | bytes 56557568 | tf_op jit(solution)/shard_map/drmk,ksl->drmsl/dot_general | solution.py:68
  894.3 10.6 fusion.13
  904.9 9.5 fusion.15
  914.4 7.1 fusion.11
  921.5 35.4 %copy.134 = bf16[64,2,64,768]{2,0,1,3:T(8,128)(2,1)} copy(bf16[64,2,64,768]{3,2,0,1:T(8,128)(2,1)} %fusion.11) | data formatting | bytes 25165824 | tf_op jit(solution)/shard_map/convert_element_type | solution.py:71
  956.8 37.4 %reshape.433 = bf16[4,2,786432]{2,1,0:T(2,128)(2,1)} reshape(bf16[768,2,64,64]{3,2,1,0:T(8,128)(2,1)} %bitcast.121) | data formatting | bytes 25165824
  994.2 6.6 all-to-all-start.2
  1000.8 6.5 multiply_convert_fusion
  1007.4 267.2 %all-to-all-done.2 = bf16[4,2,786432]{2,1,0:T(2,128)(2,1)} async-done(((bf16[4,2,786432]{2,1,0:T(2,128)(2,1)}), bf16[4,2,786432]{2,1,0:T(2,128)(2,1)}, u32[]{:S(2)}, u32[]{:S(2)}) %all-to-all-start.2) | async-done | bytes 12582944 | tf_op jit(solution)/shard_map/all_to_all | solution.py:72
  1274.5 37.0 %reshape.434 = bf16[768,2,64,64]{3,2,1,0:T(8,128)(2,1)} reshape(bf16[4,2,786432]{2,1,0:T(2,128)(2,1)} %all-to-all-done.2) | data formatting | bytes 25165824
  1311.6 31.4 %copy.135 = bf16[64,2,64,4,192]{4,2,3,1,0:T(8,128)(2,1)} copy(bf16[64,2,64,4,192]{2,0,1,4,3:T(8,128)(2,1)} %bitcast.122) | data formatting | bytes 25165824 | tf_op jit(solution)/shard_map/all_to_all | solution.py:72
  1343.0 264.7 %all-gather.5.cloned.1.call-done = bf16[256,192,1440]{2,0,1:T(8,128)(2,1)} async-done(((bf16[64,192,1440]{2,0,1:T(8,128)(2,1)}), bf16[256,192,1440]{2,0,1:T(8,128)(2,1)}) %all-gather.5.cloned.1.call-update) | async-done | bytes 141557776 | tf_op jit(solution)/shard_map/all_gather | solution.py:84
  1607.7 0.0 copy-done
  1607.7 62.0 %fusion.53 = bf16[64,192,1440]{2,0,1:T(8,128)(2,1)} fusion(bf16[256,192,1440]{2,0,1:T(8,128)(2,1)} %all-gather.5.cloned.1.call-done, bf16[256,256]{1,0:T(8,128)(2,1)S(1)} %copy-done, s32[]{:T(128)S(6)} %select_n.109), kind=kOutput, calls=%fused_computation.99 | convolution fusion | flops 9059696640 | bytes 177012736 | tf_op jit(solution)/shard_map/cd,clx->dlx/dot_general | solution.py:81
  1669.6 0.0 copy-start.1
  1669.6 207.9 %fusion.2 = bf16[64,192,1440]{2,1,0:T(8,128)(2,1)} fusion(bf16[64,192,1440]{2,0,1:T(8,128)(2,1)} %fusion.53, bf16[64,2,256,192]{3,2,1,0:T(8,128)(2,1)} %bitcast.127, bf16[1,256,1440]{1,2,0:T(8,128)(2,1)S(1)} %get-tuple-element.15, bf16[1,256,1440]{1,2,0:T(8,128)(2,1)S(1)} %get-tuple-element.16), kind=kOutput, calls=%fused_computation.3 | convolution fusion | flops 19323371520 | bytes 84836352 | tf_op jit(solution)/shard_map/drml,rmx->dlx/dot_general | solution.py:73
  1877.5 0.0 copy-done.1
  (3 shorter events, 0.0 us)
Async XLA Ops:
  6.5 1601.1 %copy-start = (bf16[256,256]{1,0:T(8,128)(2,1)S(1)}, bf16[256,256]{1,0:T(8,128)(2,1)}, u32[]{:S(2)}) copy-start(bf16[256,256]{1,0:T(8,128)(2,1)} %param.7) | copy-start | bytes 393220
  79.2 371.6 %all-to-all-start = ((bf16[64,192,2,256]{1,0,2,3:T(8,128)(2,1)}), bf16[64,192,2,256]{1,0,2,3:T(8,128)(2,1)}, u32[]{:S(2)}, u32[]{:S(2)}) async-start(bf16[64,192,2,256]{1,0,2,3:T(8,128)(2,1)} %copy.120), calls=%async_computation | async-start | bytes 33554432 | tf_op jit(solution)/shard_map/all_to_all | solution.py:57
  86.2 647.0 %all-gather.3.cloned.1.call-start = ((), (), s32[]{:S(2)}) async-start(), calls=%async_computation.3 | async-start | bytes 31457280 | tf_op jit(solution)/shard_map/all_gather | solution.py:65
  535.2 1072.4 %all-gather.5.cloned.1.call-start = ((), (), s32[]{:S(2)}) async-start(), calls=%async_computation.4 | async-start | bytes 188743680 | tf_op jit(solution)/shard_map/all_gather | solution.py:84
  592.8 98.4 %all-to-all-start.1 = ((bf16[4,2,262144]{2,1,0:T(2,128)(2,1)}), bf16[4,2,262144]{2,1,0:T(2,128)(2,1)}, u32[]{:S(2)}, u32[]{:S(2)}) async-start(bf16[4,2,262144]{2,1,0:T(2,128)(2,1)} %reshape.431), calls=%async_computation.1 | async-start | bytes 8388608 | tf_op jit(solution)/shard_map/all_to_all | solution.py:64
  836.5 12.0 copy-start.2
  994.2 280.3 %all-to-all-start.2 = ((bf16[4,2,786432]{2,1,0:T(2,128)(2,1)}), bf16[4,2,786432]{2,1,0:T(2,128)(2,1)}, u32[]{:S(2)}, u32[]{:S(2)}) async-start(bf16[4,2,786432]{2,1,0:T(2,128)(2,1)} %reshape.433), calls=%async_computation.2 | async-start | bytes 25165824 | tf_op jit(solution)/shard_map/all_to_all | solution.py:72
  1669.6 207.9 %copy-start.1 = (bf16[256,256]{1,0:T(8,128)(2,1)S(1)}, bf16[256,256]{1,0:T(8,128)(2,1)}, u32[]{:S(2)}) copy-start(bf16[256,256]{1,0:T(8,128)(2,1)} %param.7) | copy-start | bytes 393220
Sparse Core Ops, SparseCore 0:
  535.4 197.8 all-gather.2
  734.8 872.7 all-gather.4
where the time goes:
time: 1900 us; the launch traced here: 1880 us
  waiting for transfers between devices  984 us (52%)
  matrix products  405 us (21%)
  local copies, waits for them, and re-layouts  389 us (20%)
  other arithmetic  74.5 us (4%)
    all_to_all x1, waiting for transfers between devices, body(): lax.all_to_all(lon_spectrum, 'sp', split_axis=3, concat_axis=1, tiled=True)  360 us
    all_to_all x1, waiting for transfers between devices, body(): lax.all_to_all(lat_field, 'sp', split_axis=3, concat_axis=2, tiled=True)  267 us
    all_gather x1, waiting for transfers between devices, body(): lax.all_gather(state_field, 'ch', axis=0, tiled=True)  265 us
    dot_general x1, matrix products, body(): jnp.einsum('drml,rmx->dlx', band_spectrum, inv_lon, preferred_element_typ...  208 us
    unnamed x12, local copies, waits for them, and re-layouts  141 us
    all_to_all x1, waiting for transfers between devices, body(): lax.all_to_all(spectral_weight, 'ch', split_axis=3, concat_axis=2, tiled=...  88.7 us
    dot_general x1, matrix products, body(): jnp.einsum('cd,clx->dlx', weight_rows, lax.all_gather(state_field, 'ch',...  62 us
    all_to_all x2, local copies, waits for them, and re-layouts, body(): lax.all_to_all(lon_spectrum, 'sp', split_axis=3, concat_axis=1, tiled=True)  50.7 us
  transfers between devices with their start and end apart: 5, of which 5 were waited for; matrix products, arithmetic and copies ran while one was open for 23% of the time, Pallas kernels for 0%

commit v1 on v0

--- a/solution.py
+++ b/solution.py
@@ -1,14 +1,26 @@
+import functools
 import math
 
 import jax
 import jax.numpy as jnp
+import ml_dtypes
+import numpy as np
 from jax import lax
+from jax.experimental import pallas as pl
+from jax.experimental.pallas import tpu as pltpu
 from jax.sharding import PartitionSpec as P
 
 LAT = 768
 LON = 1440
 M = 256
 L = 320
+
+LANES = 128
+ROWS = 16
+KPAD = 384
+VMEM = 56 * 1024 * 1024
+F32 = jnp.float32
+BF16 = jnp.bfloat16
 
 
 def make_tables():
@@ -44,7 +56,7 @@
     return jnp.stack([out_real, out_imag], axis=1)
 
 
-def body(state_field, spectral_weight, mode_gain, bypass_weight):
+def plain_body(state_field, spectral_weight, mode_gain, bypass_weight):
     fwd_lon, inv_lon, fwd_lat, inv_lat = make_tables()
     chan_count = state_field.shape[0]
     band_rows = state_field.shape[1]
@@ -77,10 +89,9 @@
     own_columns = lax.dynamic_slice_in_dim(
         bypass_weight, lax.axis_index("ch") * out_width, out_width, 1
     )
-    weight_rows = own_columns
     bypass = jnp.einsum(
         "cd,clx->dlx",
-        weight_rows,
+        own_columns,
         lax.all_gather(state_field, "ch", axis=0, tiled=True),
         preferred_element_type=jnp.float32,
     ).astype(jnp.bfloat16)
@@ -89,6 +100,497 @@
     )
 
 
+def lon_table(n_sp, modes, transposed):
+    col = np.arange(n_sp * 2 * modes)
+    imag, mode = (col // modes) % 2, col // (2 * modes) * modes + col % modes
+    angle = (np.arange(LON)[:, None] * mode[None, :]) % LON * (2.0 * math.pi / LON)
+    value = np.where(imag == 0, np.cos(angle), -np.sin(angle))
+    if transposed:
+        value = (value * np.where(mode == 0, 1.0, 2.0)).T
+    return jnp.asarray(value.astype(ml_dtypes.bfloat16))
+
+
+def lat_table():
+    k = np.arange(L)
+    kappa = np.where(k < L // 2, k, k - L)
+    angle = (np.arange(LAT)[:, None] * kappa[None, :]) % LAT * (2.0 * math.pi / LAT)
+    value = np.zeros((LAT, 2, KPAD))
+    value[:, 0, :L], value[:, 1, :L] = np.cos(angle), np.sin(angle)
+    return jnp.asarray(value.reshape(LAT, 2 * KPAD).astype(ml_dtypes.bfloat16))
+
+
+MAP_COST = [0, 0, 120, 120, 80, 40]
+FINISH_COST = [0, 0, 0, 0, 0, 0]
+
+
+def call(kernel, name, cost=0, **kwargs):
+    return pl.pallas_call(
+        kernel,
+        name=name,
+        compiler_params=pltpu.CompilerParams(vmem_limit_bytes=VMEM),
+        cost_estimate=pl.CostEstimate(
+            flops=1 + int(cost * 1e9), bytes_accessed=1, transcendentals=0
+        ),
+        **kwargs,
+    )
+
+
+def const_spec(shape):
+    return pl.BlockSpec(shape, lambda *_: (0,) * len(shape))
+
+
+def kron_map(weight):
+    c, d = weight.shape
+    high, wide = d * ROWS, c * ROWS
+
+    def kernel(w_ref, out):
+        iota = functools.partial(lax.broadcasted_iota, jnp.int32)
+        left = (iota((high, d), 0) // ROWS == iota((high, d), 1)).astype(F32).astype(BF16)
+        right = (iota((c, wide), 1) // ROWS == iota((c, wide), 0)).astype(F32).astype(BF16)
+        tall = lax.dot_general(
+            left, w_ref[...], (((1,), (1,)), ((), ())), preferred_element_type=F32
+        ).astype(BF16)
+        value = jnp.dot(tall, right, preferred_element_type=F32)
+        same = iota((high, wide), 0) % ROWS == iota((high, wide), 1) % ROWS
+        out[...] = jnp.where(same, value, 0.0).astype(BF16)
+
+    return call(
+        kernel, "kron_map", out_shape=jax.ShapeDtypeStruct((high, wide), BF16)
+    )(weight)
+
+
+def pick_weights(ch, own, sibling):
+    _, modes, chans, _ = own.shape
+    half = LANES // 2
+    step = modes // 4
+
+    def kernel(ch_ref, a0, a1, b0, b1, out):
+        for parity in range(2):
+
+            @pl.when(ch_ref[0] % 2 == parity)
+            def _():
+                cols = slice(parity * half, (parity + 1) * half)
+                for i, pair in enumerate(((a0, a1), (b0, b1))):
+                    out[:, :, i * chans : (i + 1) * chans, :] = jnp.concatenate(
+                        [ref[:, :, :, cols] for ref in pair], axis=-1
+                    )
+
+    def tile(far):
+        return pl.BlockSpec(
+            (2, step, chans, LANES), lambda i, ch_ref: (0, i, 0, (ch_ref[0] // 2 + far) % 2)
+        )
+
+    return call(
+        kernel,
+        "pick_weights",
+        grid_spec=pltpu.PrefetchScalarGridSpec(
+            num_scalar_prefetch=1,
+            grid=(modes // step,),
+            in_specs=[tile(0), tile(1), tile(0), tile(1)],
+            out_specs=pl.BlockSpec((2, step, 2 * chans, LANES), lambda i, ch_ref: (0, i, 0, 0)),
+        ),
+        out_shape=jax.ShapeDtypeStruct((2, modes, 2 * chans, LANES), BF16),
+    )(ch.reshape(1), own, own, sibling, sibling)
+
+
+def lon_forward(field, table, start, count, n_sp):
+    rows = field.shape[1]
+    step = 4
+
+    def kernel(s_ref, t_ref, out):
+        s = s_ref[...].reshape(step * rows, LON)
+        acc = jnp.dot(s, t_ref[...], preferred_element_type=F32)
+        for k in range(n_sp):
+            part = acc[:, k * LANES : (k + 1) * LANES].astype(BF16)
+            out[k] = part.reshape(step, rows, LANES)
+
+    return call(
+        kernel,
+        "lon_forward",
+        grid=(count // step,),
+        in_specs=[
+            pl.BlockSpec((step, rows, LON), lambda i: (start // step + i, 0, 0)),
+            const_spec(table.shape),
+        ],
+        out_specs=pl.BlockSpec((n_sp, step, rows, LANES), lambda i: (0, i, 0, 0)),
+        out_shape=jax.ShapeDtypeStruct((n_sp, count, rows, LANES), BF16),
+    )(field, table)
+
+
+def lat_forward(bands, table):
+    n_sp, count, rows, _ = bands.shape
+    step = ROWS
+    half = LANES // 2
+
+    def kernel(x_ref, t_ref, out, left, right):
+        for c in range(step):
+            x = x_ref[:, c].reshape(n_sp * rows, LANES)
+            left[c * LANES : (c + 1) * LANES, :] = x.T
+        for c in range(step):
+            g = jnp.dot(
+                left[c * LANES : (c + 1) * LANES, :], t_ref[...], preferred_element_type=F32
+            )
+            right[c, :half, :] = g[:half, :KPAD] + g[half:, KPAD:]
+            right[c, half:, :] = g[half:, :KPAD] - g[:half, KPAD:]
+        out[...] = jnp.transpose(right[...], (1, 0, 2)).astype(BF16)
+
+    return call(
+        kernel,
+        "lat_forward",
+        grid=(count // step,),
+        in_specs=[
+            pl.BlockSpec((n_sp, step, rows, LANES), lambda i: (0, i, 0, 0)),
+            const_spec(table.shape),
+        ],
+        out_specs=pl.BlockSpec((LANES, step, KPAD), lambda i: (0, i, 0)),
+        out_shape=jax.ShapeDtypeStruct((LANES, count, KPAD), BF16),
+        scratch_shapes=[
+            pltpu.VMEM((step * LANES, n_sp * rows), BF16),
+            pltpu.VMEM((step, LANES, KPAD), F32),
+        ],
+    )(bands, table)
+
+
+def mix(weights, spectra, parts):
+    modes, chans, outs2 = weights.shape[1:]
+    outs = outs2 // 2
+    step = ROWS
+    n_in = len(spectra)
+
+    def kernel(w_ref, *refs):
+        ins, own, sends, scratch = refs[:n_in], refs[n_in], refs[n_in + 1 : -1], refs[-1]
+        for m in range(step):
+            y = jnp.concatenate([ref[r, m] for r in range(2) for ref in ins], axis=0)
+            wr, wi = w_ref[0, m], w_ref[1, m]
+            w = jnp.concatenate(
+                [jnp.concatenate([wr, wi], axis=1), jnp.concatenate([-wi, wr], axis=1)], axis=0
+            )
+            scratch[m] = lax.dot_general(
+                w, y, (((0,), (0,)), ((), ())), preferred_element_type=F32
+            )
+        for r in range(2):
+            base = r * outs2
+            own[r] = jnp.transpose(scratch[:, base : base + outs, :], (1, 0, 2))
+        far = [
+            jnp.transpose(scratch[:, r * outs2 + outs : (r + 1) * outs2, :], (1, 0, 2))
+            for r in range(2)
+        ]
+        for i, send in enumerate(sends):
+            block = [f[sum(parts[:i]) : sum(parts[: i + 1])] for f in far]
+            for r in range(2):
+                for t in range(2):
+                    send[2 * r + t] = block[r][:, :, t * LANES : (t + 1) * LANES].astype(BF16)
+            tail = [b[:, :, 2 * LANES : 2 * LANES + LANES // 2] for b in block]
+            send[4] = jnp.concatenate(tail, axis=-1).astype(BF16)
+
+    res = call(
+        kernel,
+        "mix",
+        grid=(modes // step,),
+        in_specs=[pl.BlockSpec((2, step, chans, outs2), lambda i: (0, i, 0, 0))]
+        + [pl.BlockSpec((2, step, s.shape[2], KPAD), lambda i: (0, i, 0, 0)) for s in spectra],
+        out_specs=[pl.BlockSpec((2, outs, step, KPAD), lambda i: (0, 0, i, 0))]
+        + [pl.BlockSpec((5, per, step, LANES), lambda i: (0, 0, i, 0)) for per in parts],
+        out_shape=[jax.ShapeDtypeStruct((2, outs, modes, KPAD), F32)]
+        + [jax.ShapeDtypeStruct((5, per, modes, LANES), BF16) for per in parts],
+        scratch_shapes=[pltpu.VMEM((step, 2 * outs2, KPAD), F32)],
+    )(weights, *spectra)
+    return res[0], res[1:]
+
+
+def lat_backward(own, far, gain, table, start, n_sp):
+    per, modes = far.shape[1:3]
+    rows = LAT // n_sp
+    step = 8
+
+    def kernel(own_ref, far_ref, g_ref, t_ref, result):
+        for pair in range(step // 2):
+            blocks = []
+            for d in (2 * pair, 2 * pair + 1):
+                z = []
+                for r in range(2):
+                    tail = far_ref[4, d][:, r * (LANES // 2) : (r + 1) * (LANES // 2)]
+                    sent = jnp.concatenate(
+                        [
+                            far_ref[2 * r, d].astype(F32),
+                            far_ref[2 * r + 1, d].astype(F32),
+                            tail.astype(F32),
+                            jnp.zeros((modes, LANES // 2), F32),
+                        ],
+                        axis=-1,
+                    )
+                    z.append(((own_ref[r, d] + sent) * g_ref[d]).astype(BF16))
+                blocks.append(jnp.concatenate([z[0], -z[1]], axis=1))
+                blocks.append(jnp.concatenate([z[1], z[0]], axis=1))
+            both = jnp.concatenate(blocks, axis=0)
+            out = lax.dot_general(
+                t_ref[...], both, (((1,), (1,)), ((), ())), preferred_element_type=F32
+            ) * (1.0 / LAT)
+            for k in range(n_sp):
+                for i in range(2):
+                    result[k, 2 * pair + i] = out[
+                        k * rows : (k + 1) * rows, i * LANES : (i + 1) * LANES
+                    ].astype(BF16)
+
+    return call(
+        kernel,
+        "lat_backward",
+        grid=(per // step,),
+        in_specs=[
+            pl.BlockSpec((2, step, modes, KPAD), lambda i: (0, start // step + i, 0, 0)),
+            pl.BlockSpec((5, step, modes, LANES), lambda i: (0, i, 0, 0)),
+            pl.BlockSpec((step, 1, KPAD), lambda i: (start // step + i, 0, 0)),
+            const_spec(table.shape),
+        ],
+        out_specs=pl.BlockSpec((n_sp, step, rows, LANES), lambda i: (0, i, 0, 0)),
+        out_shape=jax.ShapeDtypeStruct((n_sp, per, rows, LANES), BF16),
+    )(own, far, gain, table)
+
+
+WIDE = 2 * LANES
+FULL = LON // WIDE
+REST = LON - FULL * WIDE
+TAIL = REST - LANES
+
+
+def partial_map(field, sibling, kron, start, steps, cost):
+    chans = field.shape[0]
+    outs = kron.shape[0] // ROWS
+    height = outs * ROWS
+    depth = chans * ROWS
+    packed = height * LON // LANES
+    group = LANES // TAIL
+
+    def kernel(a_ref, b_ref, w_ref, out):
+        def product(cols, width):
+            a = a_ref[:, :, cols].reshape(depth, width)
+            b = b_ref[:, :, cols].reshape(depth, width)
+            return jnp.dot(w_ref[:, :depth], a, preferred_element_type=F32) + jnp.dot(
+                w_ref[:, depth:], b, preferred_element_type=F32
+            )
+
+        @pl.loop(0, FULL)
+        def _(n):
+            acc = product(pl.ds(pl.multiple_of(n * WIDE, WIDE), WIDE), WIDE).astype(BF16)
+            base = pl.multiple_of(n * 2 * height, 2 * height)
+            out[0, pl.ds(base, height), :] = acc[:, :LANES]
+            out[0, pl.ds(base + height, height), :] = acc[:, LANES:]
+
+        acc = product(slice(FULL * WIDE, LON), REST)
+        out[0, FULL * 2 * height : (FULL * 2 + 1) * height, :] = acc[:, :LANES].astype(BF16)
+        tail = acc[:, LANES:]
+        size = height // group
+        out[0, (FULL * 2 + 1) * height :, :] = jnp.concatenate(
+            [tail[q * size : (q + 1) * size] for q in range(group)], axis=1
+        ).astype(BF16)
+
+    sib_start = start if sibling.shape[1] == field.shape[1] else 0
+    return call(
+        kernel,
+        "partial_map",
+        cost,
+        grid=(steps,),
+        in_specs=[
+            pl.BlockSpec((chans, ROWS, LON), lambda i: (0, start + i, 0)),
+            pl.BlockSpec((chans, ROWS, LON), lambda i: (0, sib_start + i, 0)),
+            const_spec(kron.shape),
+        ],
+        out_specs=pl.BlockSpec((1, packed, LANES), lambda i: (i, 0, 0)),
+        out_shape=jax.ShapeDtypeStruct((steps, packed, LANES), BF16),
+    )(field, sibling, kron)
+
+
+def gelu(v):
+    return 0.5 * v * (1.0 + lax.erf(v * math.sqrt(0.5)))
+
+
+def finish(previous, field, sibling, kron, spectrum, table, received, start, cost):
+    chans = field.shape[0]
+    outs = kron.shape[0] // ROWS
+    height = outs * ROWS
+    depth = chans * ROWS
+    packed = height * LON // LANES
+    group = LANES // TAIL
+    n_sp = spectrum[0].shape[0]
+    sizes = [part.shape[1] for part in spectrum]
+
+    def kernel(*refs):
+        refs = refs[1:] if previous is not None else refs
+        a_ref, b_ref, w_ref, t_ref, p_ref = refs[:5]
+        lats, out, lat = refs[5:-2], refs[-2], refs[-1]
+        at = 0
+        for ref, per in zip(lats, sizes):
+            for k in range(n_sp):
+                lat[at : at + per * ROWS, k * LANES : (k + 1) * LANES] = ref[k].reshape(
+                    per * ROWS, LANES
+                )
+            at += per * ROWS
+
+        def product(cols, width):
+            a = a_ref[:, :, cols].reshape(depth, width)
+            b = b_ref[:, :, cols].reshape(depth, width)
+            spectral = jnp.dot(lat[...], t_ref[:, cols], preferred_element_type=F32)
+            return (
+                spectral * (1.0 / LON)
+                + jnp.dot(w_ref[:, :depth], a, preferred_element_type=F32)
+                + jnp.dot(w_ref[:, depth:], b, preferred_element_type=F32)
+            )
+
+        @pl.loop(0, FULL)
+        def _(n):
+            cols = pl.ds(pl.multiple_of(n * WIDE, WIDE), WIDE)
+            acc = product(cols, WIDE)
+            base = pl.multiple_of(n * 2 * height, 2 * height)
+            far = jnp.concatenate(
+                [p_ref[0, pl.ds(base, height), :], p_ref[0, pl.ds(base + height, height), :]], axis=1
+            )
+            value = gelu(acc + far.astype(F32)).astype(BF16)
+            out[:, :, cols] = value.reshape(outs, ROWS, WIDE)
+
+        acc = product(slice(FULL * WIDE, LON), REST)
+        size = height // group
+        tails = p_ref[0, (FULL * 2 + 1) * height :, :].astype(F32)
+        tail = jnp.concatenate(
+            [tails[:, q * TAIL : (q + 1) * TAIL] for q in range(group)], axis=0
+        )
+        far = p_ref[0, FULL * 2 * height : (FULL * 2 + 1) * height, :].astype(F32)
+        one = gelu(acc[:, :LANES] + far).astype(BF16)
+        out[:, :, FULL * WIDE : FULL * WIDE + LANES] = one.reshape(outs, ROWS, LANES)
+        two = gelu(acc[:, LANES:] + tail).astype(BF16)
+        out[:, :, FULL * WIDE + LANES :] = two.reshape(outs, ROWS, TAIL)
+
+    steps = received.shape[0]
+    operands = [field, sibling, kron, table, received, *spectrum]
+    specs = [
+        pl.BlockSpec((chans, ROWS, LON), lambda i: (0, start + i, 0)),
+        pl.BlockSpec((chans, ROWS, LON), lambda i: (0, start + i, 0)),
+        const_spec(kron.shape),
+        const_spec(table.shape),
+        pl.BlockSpec((1, packed, LANES), lambda i: (i, 0, 0)),
+    ] + [
+        pl.BlockSpec((n_sp, per, ROWS, LANES), lambda i: (0, 0, start + i, 0)) for per in sizes
+    ]
+    aliases = {}
+    if previous is not None:
+        operands = [previous] + operands
+        specs = [pl.BlockSpec(memory_space=pl.ANY)] + specs
+        aliases = {0: 0}
+    return call(
+        kernel,
+        "finish",
+        cost,
+        grid=(steps,),
+        in_specs=specs,
+        out_specs=pl.BlockSpec((outs, ROWS, LON), lambda i: (0, start + i, 0)),
+        out_shape=jax.ShapeDtypeStruct(field.shape, BF16),
+        input_output_aliases=aliases,
+        scratch_shapes=[pltpu.VMEM((height, n_sp * LANES), BF16)],
+    )(*operands)
+
+
+def after(value, *others):
+    return lax.optimization_barrier((value, *others))[0]
+
+
+def row_plan(total):
+    unit = total // 12
+    return [unit, 2 * unit, 3 * unit, 3 * unit, 2 * unit, total - 11 * unit]
+
+
+def tiled_body(state_field, spectral_weight, mode_gain, bypass_weight):
+    chans, rows, _ = state_field.shape
+    modes = spectral_weight.shape[1]
+    n_sp, n_ch = lax.axis_size("sp"), lax.axis_size("ch")
+    ch = lax.axis_index("ch")
+    near, far = jnp.bitwise_xor(ch, 1), jnp.bitwise_xor(ch, 2)
+
+    def to_near(value):
+        return lax.ppermute(value, "ch", [(i, i ^ 1) for i in range(n_ch)])
+
+    def to_far(value):
+        return lax.ppermute(value, "ch", [(i, i ^ 2) for i in range(n_ch)])
+
+    def across(blocks):
+        return lax.all_to_all(blocks, "sp", 0, 0)
+
+    plan = row_plan(rows // ROWS)
+
+    first = plan[0] * ROWS
+    near_first = to_near(lax.slice_in_dim(state_field, 0, first, axis=1))
+    near_field = to_near(after(state_field, near_first))
+    near_weight = to_near(after(spectral_weight, near_first))
+
+    def rows_of(index):
+        return lax.dynamic_slice_in_dim(bypass_weight, index * chans, chans, 0)
+
+    chip_rows = jnp.concatenate([rows_of(ch), rows_of(near)], axis=0)
+    kron_far = kron_map(lax.dynamic_slice_in_dim(chip_rows, far * chans, chans, 1))
+    kron_own = kron_map(lax.dynamic_slice_in_dim(chip_rows, ch * chans, chans, 1))
+
+    sent, received, starts = [], [], []
+
+    def partial_rows(*others):
+        i = len(sent)
+        starts.append(sum(plan[:i]))
+        sibling = near_field if i else near_first
+        kron = after(kron_far, *others)
+        sent.append(partial_map(state_field, sibling, kron, starts[-1], plan[i], MAP_COST[i]))
+
+    def send_rows(*others):
+        received.append(to_far(after(sent[len(received)], *others)))
+
+    half = chans // 2
+    parts = [half, chans - half]
+    table = lon_table(n_sp, modes, False)
+    lat = lat_table()
+    partial_rows()
+    send_rows()
+    table = after(table, sent[0])
+    bands = [lon_forward(state_field, table, i * half, parts[i], n_sp) for i in range(2)]
+    partial_rows(bands[0])
+    send_rows(received[0])
+    partial_rows(bands[1])
+    send_rows(received[1])
+    bands[1] = after(bands[1], sent[2])
+    weights = pick_weights(ch, spectral_weight, near_weight)
+    spectra = [lat_forward(across(b), lat).reshape(2, modes, -1, KPAD) for b in bands]
+    near_spectra = [to_near(s) for s in spectra]
+
+    own_mixed, sends = mix(weights, spectra + near_spectra, parts)
+    far_mixed = [to_far(after(s, received[2])) for s in sends]
+
+    gain = jnp.pad(mode_gain, ((0, 0), (0, KPAD - L))).reshape(chans, 1, KPAD)
+    back = [lat_backward(own_mixed, far_mixed[i], gain, lat, i * half, n_sp) for i in range(2)]
+    spectrum = [across(b) for b in back]
+    partial_rows(*sends)
+    send_rows(far_mixed[0])
+    partial_rows(*sends)
+    send_rows(received[3])
+    partial_rows(*sends)
+    send_rows(received[3])
+    inverse = lon_table(n_sp, modes, True)
+    out = None
+    for got, start, cost in zip(received, starts, FINISH_COST):
+        out = finish(
+            out, state_field, near_field, kron_own, spectrum, inverse, got, start, cost
+        )
+    return out
+
+
+def body(state_field, spectral_weight, mode_gain, bypass_weight):
+    chans, rows, _ = state_field.shape
+    modes = spectral_weight.shape[1]
+    n_sp, n_ch = lax.axis_size("sp"), lax.axis_size("ch")
+    whole_tiles = (
+        n_ch == 4
+        and 2 * modes == LANES
+        and chans == 64
+        and rows % (12 * ROWS) == 0
+    )
+    run = tiled_body if whole_tiles else plain_body
+    return run(state_field, spectral_weight, mode_gain, bypass_weight)
+
+
 def solution(mesh):
     in_specs = (P(("grp", "ch"), "sp", None), P(None, "sp", "ch", None), P("ch", None), P())
     out_specs = P(("grp", "ch"), "sp", None)

time: 1900 us -> 942 us (0.50)
  waiting for transfers between devices: 984 us -> 494 us
  matrix products: 405 us -> 0 us
  Pallas kernels: 0 us -> 396 us
  local copies, waits for them, and re-layouts: 389 us -> 9.12 us
  other arithmetic: 74.5 us -> 1.1 us
    all_to_all x3 -> x4, waiting for transfers between devices: 716 us -> 307 us  [across(): return lax.all_to_all(blocks, 'sp', 0, 0)]
    dot_general x9 -> x0, matrix products: 405 us -> none  [the longest x1 208 us: body(): jnp.einsum('drml,rmx->dlx', band_spectrum, inv_lon, preferred_element_typ...]
    pallas_call x0 -> x22, Pallas kernels: none -> 396 us  [the longest x6 166 us: finish(): call(kernel, 'finish', cost, grid=(steps,), in_specs=specs, out_specs=pl....]
    all_gather x2 -> x0, waiting for transfers between devices: 268 us -> none  [the longest x1 265 us: body(): lax.all_gather(state_field, 'ch', axis=0, tiled=True)]
    ppermute x0 -> x13, waiting for transfers between devices: none -> 187 us  [the longest x8 182 us: to_far(): return lax.ppermute(value, 'ch', [(i, i ^ 2) for i in range(n_ch)])]
    unnamed x12 -> x16, local copies, waits for them, and re-layouts: 141 us -> 6.27 us
    all_to_all x4 -> x0, local copies, waits for them, and re-layouts: 93.3 us -> none  [the longest x2 50.7 us: body(): lax.all_to_all(lon_spectrum, 'sp', split_axis=3, concat_axis=1, tiled=True)]
    squeeze x5 -> x0, local copies, waits for them, and re-layouts: 74.1 us -> none  [the longest x2 41.9 us: mix_modes(): inputs[:, 1]]
  transfers between devices with their start and end apart: 5 -> 17, of which waited for: 5 -> 11; matrix products, arithmetic and copies ran while one was open for 23% -> 0% of each run, Pallas kernels for 0% -> 40%
where the time goes in v1:
time: 942 us; the launch traced here: 934 us
  waiting for transfers between devices  494 us (52%)
  Pallas kernels  396 us (42%)
  starting transfers between devices  34.1 us (4%)
    all_to_all x4, waiting for transfers between devices, across(): return lax.all_to_all(blocks, 'sp', 0, 0)  307 us
    ppermute x8, waiting for transfers between devices, to_far(): return lax.ppermute(value, 'ch', [(i, i ^ 2) for i in range(n_ch)])  182 us
    pallas_call x6, Pallas kernels, finish(): call(kernel, 'finish', cost, grid=(steps,), in_specs=specs, out_specs=pl....  166 us
    pallas_call x6, Pallas kernels, partial_map(): call(kernel, 'partial_map', cost, grid=(steps,), in_specs=[pl.BlockSpec((...  127 us
    pallas_call x2, Pallas kernels, lon_forward(): call(kernel, 'lon_forward', grid=(count // step,), in_specs=[pl.BlockSpec...  32.3 us
    all_to_all x4, starting transfers between devices, across(): return lax.all_to_all(blocks, 'sp', 0, 0)  21.6 us
    pallas_call x2, Pallas kernels, lat_backward(): call(kernel, 'lat_backward', grid=(per // step,), in_specs=[pl.BlockSpec(...  19.6 us
    pallas_call x2, Pallas kernels, lat_forward(): call(kernel, 'lat_forward', grid=(count // step,), in_specs=[pl.BlockSpec...  19.5 us
  transfers between devices with their start and end apart: 17, of which 11 were waited for; matrix products, arithmetic and copies ran while one was open for 0% of the time, Pallas kernels for 40%

profile of v1, /device:TPU:0, one launch (start us, length us, event | category | flops | bytes accessed | tf_op | source)
XLA Modules:
  0.0 934.5 jit_solution(16853549910260224131)
XLA Ops:
  0.0 2.1 slice.3
  2.1 0.5 collective-permute-start
  2.7 5.3 collective-permute-done.b_ref
  7.9 0.4 collective-permute-start.1
  8.3 1.1 fusion
  9.4 4.3 kron_map.3.w_ref
  13.8 13.4 %partial_map.6 = bf16[1,11520,128]{2,1,0:T(8,128)(2,1)} custom-call(bf16[64,192,1440]{2,1,0:T(8,128)(2,1)} %refs_1_.9, bf16[64,16,1440]{2,1,0:T(8,128)(2,1)} %copy-done, bf16[1024,2048]{1,0:T(8,128)(2,1)} %kron_map.3.w_ref), custom_call_target="tpu_custom_call" | custom-call | flops 1 | bytes 1 | tf_op jit(solution)/shard_map/partial_map/pallas_call | solution.py:388
  27.2 2.5 collective-permute-start.2
  29.7 16.1 %lon_forward.2 = bf16[4,32,192,128]{3,2,1,0:T(8,128)(2,1)} custom-call(bf16[64,192,1440]{2,1,0:T(8,128)(2,1)} %refs_1_.9, bf16[1440,512]{1,0:T(8,128)(2,1)} %constant.22.clone.t_ref), custom_call_target="tpu_custom_call" | custom-call | flops 1 | bytes 1 | tf_op jit(solution)/shard_map/lon_forward/pallas_call | solution.py:207
  45.8 16.2 %lon_forward.3 = bf16[4,32,192,128]{3,2,1,0:T(8,128)(2,1)} custom-call(bf16[64,192,1440]{2,1,0:T(8,128)(2,1)} %refs_1_.9, bf16[1440,512]{1,0:T(8,128)(2,1)} %constant.22.clone.t_ref), custom_call_target="tpu_custom_call" | custom-call | flops 1 | bytes 1 | tf_op jit(solution)/shard_map/lon_forward/pallas_call | solution.py:207
  61.9 5.3 all-to-all-start
  67.2 0.0 collective-permute-done.1.b_ref.refs_1_.refs_2_
  67.2 21.1 %partial_map.8 = bf16[2,11520,128]{2,1,0:T(8,128)(2,1)} custom-call(bf16[64,192,1440]{2,1,0:T(8,128)(2,1)} %refs_1_.9, bf16[64,192,1440]{2,1,0:T(8,128)(2,1)} %collective-permute-done.1.b_ref.refs_1_.refs_2_, bf16[1024,2048]{1,0:T(8,128)(2,1)} %kron_map.3.w_ref), custom_call_target="tpu_custom_call" | custom-call | flops 1 | bytes 1 | tf_op jit(solution)/shard_map/partial_map/pallas_call | solution.py:388
  88.4 6.1 collective-permute-done.2.refs_4_
  94.4 1.7 collective-permute-start.6
  96.2 28.9 %partial_map.7 = bf16[3,11520,128]{2,1,0:T(8,128)(2,1)} custom-call(bf16[64,192,1440]{2,1,0:T(8,128)(2,1)} %refs_1_.9, bf16[64,192,1440]{2,1,0:T(8,128)(2,1)} %collective-permute-done.1.b_ref.refs_1_.refs_2_, bf16[1024,2048]{1,0:T(8,128)(2,1)} %kron_map.3.w_ref), custom_call_target="tpu_custom_call" | custom-call | flops 120000004096 | bytes 1 | tf_op jit(solution)/shard_map/partial_map/pallas_call | solution.py:388
  125.0 0.0 copy-done.3
  125.0 81.0 %all-to-all-done.x_ref = bf16[4,32,192,128]{3,2,1,0:T(8,128)(2,1)} async-done(((bf16[4,32,192,128]{3,2,1,0:T(8,128)(2,1)}), bf16[4,32,192,128]{3,2,1,0:T(8,128)(2,1)}, u32[]{:S(2)}, u32[]{:S(2)}) %all-to-all-start) | async-done | bytes 6291488 | tf_op jit(solution)/shard_map/all_to_all | solution.py:514
  206.0 5.4 all-to-all-start.1
  211.4 12.3 %collective-permute-done.6.refs_5_ = bf16[2,11520,128]{2,1,0:T(8,128)(2,1)} collective-permute-done((bf16[2,11520,128]{2,1,0:T(8,128)(2,1)}, bf16[2,11520,128]{2,1,0:T(8,128)(2,1)}, u32[]{:S(2)}, u32[]{:S(2)}) %collective-permute-start.6) | collective-permute-done | bytes 5898272 | tf_op jit(solution)/shard_map/ppermute | solution.py:511
  223.8 1.5 collective-permute-start.7
  225.3 0.0 collective-permute-start.3
  225.3 9.7 %lat_forward.2 = bf16[128,32,384]{2,1,0:T(8,128)(2,1)} custom-call(bf16[4,32,192,128]{3,2,1,0:T(8,128)(2,1)} %all-to-all-done.x_ref, bf16[768,768]{1,0:T(8,128)(2,1)} %constant.23.clone.t_ref), custom_call_target="tpu_custom_call" | custom-call | flops 1 | bytes 1 | tf_op jit(solution)/shard_map/lat_forward/pallas_call | solution.py:237
  235.1 0.5 collective-permute-start.4
  235.6 113.9 %all-to-all-done.1.x_ref = bf16[4,32,192,128]{3,2,1,0:T(8,128)(2,1)} async-done(((bf16[4,32,192,128]{3,2,1,0:T(8,128)(2,1)}), bf16[4,32,192,128]{3,2,1,0:T(8,128)(2,1)}, u32[]{:S(2)}, u32[]{:S(2)}) %all-to-all-start.1) | async-done | bytes 6291488 | tf_op jit(solution)/shard_map/all_to_all | solution.py:514
  349.4 9.8 %lat_forward.3 = bf16[128,32,384]{2,1,0:T(8,128)(2,1)} custom-call(bf16[4,32,192,128]{3,2,1,0:T(8,128)(2,1)} %all-to-all-done.1.x_ref, bf16[768,768]{1,0:T(8,128)(2,1)} %constant.23.clone.t_ref), custom_call_target="tpu_custom_call" | custom-call | flops 1 | bytes 1 | tf_op jit(solution)/shard_map/lat_forward/pallas_call | solution.py:237
  359.2 0.0 collective-permute-start.5
  359.2 0.0 collective-permute-done.3.b0.b1
  359.2 6.3 pick_weights.1.w_ref
  365.5 0.0 collective-permute-done.4.refs_2_
  365.5 0.0 collective-permute-done.5.refs_3_
  365.5 1.6 copy-done.1
  367.1 1.7 copy-done.2
  368.8 16.5 %mix.1 = (f32[2,64,64,384]{3,2,1,0:T(8,128)}, bf16[5,32,64,128]{3,2,1,0:T(8,128)(2,1)}, bf16[5,32,64,128]{3,2,1,0:T(8,128)(2,1)}) custom-call(bf16[2,64,128,128]{3,2,1,0:T(8,128)(2,1)} %pick_weights.1.w_ref, bf16[2,64,32,384]{3,2,1,0:T(8,128)(2,1)} %bitcast.4, bf16[2,64,32,384]{3,2,1,0:T(8,128)(2,1)} %bitcast.6, bf16[2,64,32,384]{3,2,1,0:T(8,128)(2,1)} %copy-done.1, ...), custom_call_target="tpu_custom_call" | custom-call | flops 1 | bytes 1 | tf_op jit(solution)/shard_map/mix/pallas_call | solution.py:286
  385.3 30.2 %collective-permute-done.7.refs_5_ = bf16[3,11520,128]{2,1,0:T(8,128)(2,1)} collective-permute-done((bf16[3,11520,128]{2,1,0:T(8,128)(2,1)}, bf16[3,11520,128]{2,1,0:T(8,128)(2,1)}, u32[]{:S(2)}, u32[]{:S(2)}) %collective-permute-start.7) | collective-permute-done | bytes 8847392 | tf_op jit(solution)/shard_map/ppermute | solution.py:511
  415.5 1.3 collective-permute-start.8
  416.8 0.7 reshape.15.g_ref
  417.5 0.7 collective-permute-start.9
  418.2 57.3 %collective-permute-done.8.far_ref = bf16[5,32,64,128]{3,2,1,0:T(8,128)(2,1)S(1)} collective-permute-done((bf16[5,32,64,128]{3,2,1,0:T(8,128)(2,1)}, bf16[5,32,64,128]{3,2,1,0:T(8,128)(2,1)S(1)}, u32[]{:S(2)}, u32[]{:S(2)}) %collective-permute-start.8) | collective-permute-done | bytes 2621472 | tf_op jit(solution)/shard_map/ppermute | solution.py:511
  475.5 1.5 copy-done.5
  476.9 9.8 %lat_backward.2 = bf16[4,32,192,128]{3,2,1,0:T(8,128)(2,1)} custom-call(f32[2,64,64,384]{3,2,1,0:T(8,128)} %get-tuple-element.27.own_ref, bf16[5,32,64,128]{3,2,1,0:T(8,128)(2,1)} %copy-done.5, f32[64,1,384]{2,1,0:T(1,128)} %reshape.15.g_ref, bf16[768,768]{1,0:T(8,128)(2,1)} %constant.23.clone.t_ref), custom_call_target="tpu_custom_call" | custom-call | flops 1 | bytes 1 | tf_op jit(solution)/shard_map/lat_backward/pallas_call | solution.py:335
  486.7 5.6 all-to-all-start.2
  492.4 28.9 %partial_map.9 = bf16[3,11520,128]{2,1,0:T(8,128)(2,1)} custom-call(bf16[64,192,1440]{2,1,0:T(8,128)(2,1)} %refs_1_.9, bf16[64,192,1440]{2,1,0:T(8,128)(2,1)} %collective-permute-done.1.b_ref.refs_1_.refs_2_, bf16[1024,2048]{1,0:T(8,128)(2,1)} %kron_map.3.w_ref), custom_call_target="tpu_custom_call" | custom-call | flops 120000004096 | bytes 1 | tf_op jit(solution)/shard_map/partial_map/pallas_call | solution.py:388
  521.3 1.3 collective-permute-start.10
  522.6 9.1 collective-permute-done.9.far_ref
  531.7 1.5 copy-done.4
  533.1 9.8 %lat_backward.3 = bf16[4,32,192,128]{3,2,1,0:T(8,128)(2,1)} custom-call(f32[2,64,64,384]{3,2,1,0:T(8,128)} %get-tuple-element.27.own_ref, bf16[5,32,64,128]{3,2,1,0:T(8,128)(2,1)} %copy-done.4, f32[64,1,384]{2,1,0:T(1,128)} %reshape.15.g_ref, bf16[768,768]{1,0:T(8,128)(2,1)} %constant.23.clone.t_ref), custom_call_target="tpu_custom_call" | custom-call | flops 1 | bytes 1 | tf_op jit(solution)/shard_map/lat_backward/pallas_call | solution.py:335
  542.9 82.6 %all-to-all-done.2.refs_5_.refs_6_ = bf16[4,32,192,128]{3,2,1,0:T(8,128)(2,1)} async-done(((bf16[4,32,192,128]{3,2,1,0:T(8,128)(2,1)}), bf16[4,32,192,128]{3,2,1,0:T(8,128)(2,1)}, u32[]{:S(2)}, u32[]{:S(2)}) %all-to-all-start.2) | async-done | bytes 6291488 | tf_op jit(solution)/shard_map/all_to_all | solution.py:514
  625.5 5.3 all-to-all-start.3
  630.8 21.1 %partial_map.10 = bf16[2,11520,128]{2,1,0:T(8,128)(2,1)} custom-call(bf16[64,192,1440]{2,1,0:T(8,128)(2,1)} %refs_1_.9, bf16[64,192,1440]{2,1,0:T(8,128)(2,1)} %collective-permute-done.1.b_ref.refs_1_.refs_2_, bf16[1024,2048]{1,0:T(8,128)(2,1)} %kron_map.3.w_ref), custom_call_target="tpu_custom_call" | custom-call | flops 80000000000 | bytes 1 | tf_op jit(solution)/shard_map/partial_map/pallas_call | solution.py:388
  651.9 66.7 %collective-permute-done.10.refs_5_ = bf16[3,11520,128]{2,1,0:T(8,128)(2,1)} collective-permute-done((bf16[3,11520,128]{2,1,0:T(8,128)(2,1)}, bf16[3,11520,128]{2,1,0:T(8,128)(2,1)}, u32[]{:S(2)}, u32[]{:S(2)}) %collective-permute-start.10) | collective-permute-done | bytes 8847392 | tf_op jit(solution)/shard_map/ppermute | solution.py:511
  718.6 1.1 collective-permute-start.11
  719.7 13.6 %partial_map.11 = bf16[1,11520,128]{2,1,0:T(8,128)(2,1)} custom-call(bf16[64,192,1440]{2,1,0:T(8,128)(2,1)} %refs_1_.9, bf16[64,192,1440]{2,1,0:T(8,128)(2,1)} %collective-permute-done.1.b_ref.refs_1_.refs_2_, bf16[1024,2048]{1,0:T(8,128)(2,1)} %kron_map.3.w_ref), custom_call_target="tpu_custom_call" | custom-call | flops 40000000000 | bytes 1 | tf_op jit(solution)/shard_map/partial_map/pallas_call | solution.py:388
  733.3 0.9 collective-permute-start.12
  734.2 4.3 kron_map.2.refs_2_.refs_3_
  738.5 29.9 %all-to-all-done.3.refs_6_.refs_7_ = bf16[4,32,192,128]{3,2,1,0:T(8,128)(2,1)} async-done(((bf16[4,32,192,128]{3,2,1,0:T(8,128)(2,1)}), bf16[4,32,192,128]{3,2,1,0:T(8,128)(2,1)}, u32[]{:S(2)}, u32[]{:S(2)}) %all-to-all-start.3) | async-done | bytes 6291488 | tf_op jit(solution)/shard_map/all_to_all | solution.py:514
  768.4 17.4 %finish.6.refs_0_ = bf16[64,192,1440]{2,1,0:T(8,128)(2,1)} custom-call(bf16[64,192,1440]{2,1,0:T(8,128)(2,1)} %refs_1_.9, bf16[64,192,1440]{2,1,0:T(8,128)(2,1)} %collective-permute-done.1.b_ref.refs_1_.refs_2_, bf16[1024,2048]{1,0:T(8,128)(2,1)} %kron_map.2.refs_2_.refs_3_, bf16[512,1440]{1,0:T(8,128)(2,1)} %constant.24.clone.refs_3_.refs_4_, ...), custom_call_target="tpu_custom_call" | custom-call | flops 1 | bytes 1 | tf_op jit(solution)/shard_map/finish/pallas_call | solution.py:478
  785.9 27.7 %finish.7.refs_0_ = bf16[64,192,1440]{2,1,0:T(8,128)(2,1)} custom-call(bf16[64,192,1440]{2,1,0:T(8,128)(2,1)} %finish.6.refs_0_, bf16[64,192,1440]{2,1,0:T(8,128)(2,1)} %refs_1_.9, bf16[64,192,1440]{2,1,0:T(8,128)(2,1)} %collective-permute-done.1.b_ref.refs_1_.refs_2_, bf16[1024,2048]{1,0:T(8,128)(2,1)} %kron_map.2.refs_2_.refs_3_, ...), custom_call_target="tpu_custom_call", output_to_operand_aliasing={{}: (0, {})} | custom-call | flops 1 | bytes 1 | tf_op jit(solution)/shard_map/finish/pallas_call | solution.py:478
  813.6 37.9 %finish.8.refs_0_ = bf16[64,192,1440]{2,1,0:T(8,128)(2,1)} custom-call(bf16[64,192,1440]{2,1,0:T(8,128)(2,1)} %finish.7.refs_0_, bf16[64,192,1440]{2,1,0:T(8,128)(2,1)} %refs_1_.9, bf16[64,192,1440]{2,1,0:T(8,128)(2,1)} %collective-permute-done.1.b_ref.refs_1_.refs_2_, bf16[1024,2048]{1,0:T(8,128)(2,1)} %kron_map.2.refs_2_.refs_3_, ...), custom_call_target="tpu_custom_call", output_to_operand_aliasing={{}: (0, {})} | custom-call | flops 1 | bytes 1 | tf_op jit(solution)/shard_map/finish/pallas_call | solution.py:478
  851.4 37.7 %finish.9.refs_0_ = bf16[64,192,1440]{2,1,0:T(8,128)(2,1)} custom-call(bf16[64,192,1440]{2,1,0:T(8,128)(2,1)} %finish.8.refs_0_, bf16[64,192,1440]{2,1,0:T(8,128)(2,1)} %refs_1_.9, bf16[64,192,1440]{2,1,0:T(8,128)(2,1)} %collective-permute-done.1.b_ref.refs_1_.refs_2_, bf16[1024,2048]{1,0:T(8,128)(2,1)} %kron_map.2.refs_2_.refs_3_, ...), custom_call_target="tpu_custom_call", output_to_operand_aliasing={{}: (0, {})} | custom-call | flops 1 | bytes 1 | tf_op jit(solution)/shard_map/finish/pallas_call | solution.py:478
  889.1 0.0 collective-permute-done.11.refs_5_
  889.1 27.5 %finish.10.refs_0_ = bf16[64,192,1440]{2,1,0:T(8,128)(2,1)} custom-call(bf16[64,192,1440]{2,1,0:T(8,128)(2,1)} %finish.9.refs_0_, bf16[64,192,1440]{2,1,0:T(8,128)(2,1)} %refs_1_.9, bf16[64,192,1440]{2,1,0:T(8,128)(2,1)} %collective-permute-done.1.b_ref.refs_1_.refs_2_, bf16[1024,2048]{1,0:T(8,128)(2,1)} %kron_map.2.refs_2_.refs_3_, ...), custom_call_target="tpu_custom_call", output_to_operand_aliasing={{}: (0, {})} | custom-call | flops 1 | bytes 1 | tf_op jit(solution)/shard_map/finish/pallas_call | solution.py:478
  916.6 0.0 collective-permute-done.12.refs_5_
  916.6 17.7 %finish.11 = bf16[64,192,1440]{2,1,0:T(8,128)(2,1)} custom-call(bf16[64,192,1440]{2,1,0:T(8,128)(2,1)} %finish.10.refs_0_, bf16[64,192,1440]{2,1,0:T(8,128)(2,1)} %refs_1_.9, bf16[64,192,1440]{2,1,0:T(8,128)(2,1)} %collective-permute-done.1.b_ref.refs_1_.refs_2_, bf16[1024,2048]{1,0:T(8,128)(2,1)} %kron_map.2.refs_2_.refs_3_, ...), custom_call_target="tpu_custom_call", output_to_operand_aliasing={{}: (0, {})} | custom-call | flops 1 | bytes 1 | tf_op jit(solution)/shard_map/finish/pallas_call | solution.py:478
  (13 shorter events, 0.0 us)
Async XLA Ops:
  0.0 8.3 copy-start.7
  2.1 5.8 collective-permute-start
  7.9 5.8 copy-start
  7.9 59.3 %collective-permute-start.1 = (bf16[64,192,1440]{2,1,0:T(8,128)(2,1)}, bf16[64,192,1440]{2,1,0:T(8,128)(2,1)}, u32[]{:S(2)}, u32[]{:S(2)}) collective-permute-start(bf16[64,192,1440]{2,1,0:T(8,128)(2,1)} %refs_1_.9), channel_id=1, source_target_pairs={{0,1},{1,0},{2,3},{3,2},{4,5},{5,4},{6,7},{7,6},{8,9},{9,8},{10,11... | collective-permute-start | bytes 106168328 | tf_op jit(solution)/shard_map/ppermute | solution.py:508
  27.2 67.3 %collective-permute-start.2 = (bf16[1,11520,128]{2,1,0:T(8,128)(2,1)}, bf16[1,11520,128]{2,1,0:T(8,128)(2,1)S(1)}, u32[]{:S(2)}, u32[]{:S(2)}) collective-permute-start(bf16[1,11520,128]{2,1,0:T(8,128)(2,1)} %partial_map.6), channel_id=1, source_target_pairs={{0,2},{1,3},{2,0},{3,1},{4,6},{5,7},{6,4},{7,5},{8,10},{9,11},{10,... | collective-permute-start | bytes 8847368 | tf_op jit(solution)/shard_map/ppermute | solution.py:511
  61.9 144.1 %all-to-all-start = ((bf16[4,32,192,128]{3,2,1,0:T(8,128)(2,1)}), bf16[4,32,192,128]{3,2,1,0:T(8,128)(2,1)}, u32[]{:S(2)}, u32[]{:S(2)}) async-start(bf16[4,32,192,128]{3,2,1,0:T(8,128)(2,1)} %lon_forward.2), calls=%async_computation | async-start | bytes 12582912 | tf_op jit(solution)/shard_map/all_to_all | solution.py:514
  94.4 30.6 %copy-start.3 = (bf16[1,11520,128]{2,1,0:T(8,128)(2,1)}, bf16[1,11520,128]{2,1,0:T(8,128)(2,1)S(1)}, u32[]{:S(2)}) copy-start(bf16[1,11520,128]{2,1,0:T(8,128)(2,1)S(1)} %collective-permute-done.2.refs_4_) | copy-start | bytes 8847364
  94.4 129.3 %collective-permute-start.6 = (bf16[2,11520,128]{2,1,0:T(8,128)(2,1)}, bf16[2,11520,128]{2,1,0:T(8,128)(2,1)}, u32[]{:S(2)}, u32[]{:S(2)}) collective-permute-start(bf16[2,11520,128]{2,1,0:T(8,128)(2,1)} %partial_map.8), channel_id=1, source_target_pairs={{0,2},{1,3},{2,0},{3,1},{4,6},{5,7},{6,4},{7,5},{8,10},{9,11},{10,... | collective-permute-start | bytes 17694728 | tf_op jit(solution)/shard_map/ppermute | solution.py:511
  206.0 143.4 %all-to-all-start.1 = ((bf16[4,32,192,128]{3,2,1,0:T(8,128)(2,1)}), bf16[4,32,192,128]{3,2,1,0:T(8,128)(2,1)}, u32[]{:S(2)}, u32[]{:S(2)}) async-start(bf16[4,32,192,128]{3,2,1,0:T(8,128)(2,1)} %lon_forward.3), calls=%async_computation.1 | async-start | bytes 12582912 | tf_op jit(solution)/shard_map/all_to_all | solution.py:514
  223.8 191.7 %collective-permute-start.7 = (bf16[3,11520,128]{2,1,0:T(8,128)(2,1)}, bf16[3,11520,128]{2,1,0:T(8,128)(2,1)}, u32[]{:S(2)}, u32[]{:S(2)}) collective-permute-start(bf16[3,11520,128]{2,1,0:T(8,128)(2,1)} %partial_map.7), channel_id=1, source_target_pairs={{0,2},{1,3},{2,0},{3,1},{4,6},{5,7},{6,4},{7,5},{8,10},{9,11},{10,... | collective-permute-start | bytes 26542088 | tf_op jit(solution)/shard_map/ppermute | solution.py:511
  225.3 133.9 %collective-permute-start.3 = (bf16[2,64,64,256]{3,2,1,0:T(8,128)(2,1)}, bf16[2,64,64,256]{3,2,1,0:T(8,128)(2,1)}, u32[]{:S(2)}, u32[]{:S(2)}) collective-permute-start(bf16[2,64,64,256]{3,2,1,0:T(8,128)(2,1)} %a1.1), channel_id=1, source_target_pairs={{0,1},{1,0},{2,3},{3,2},{4,5},{5,4},{6,7},{7,6},{8,9},{9,8},{10,11... | collective-permute-start | bytes 12582920 | tf_op jit(solution)/shard_map/ppermute | solution.py:508
  235.1 130.4 %collective-permute-start.4 = (bf16[2,64,32,384]{3,2,1,0:T(8,128)(2,1)}, bf16[2,64,32,384]{3,2,1,0:T(8,128)(2,1)S(1)}, u32[]{:S(2)}, u32[]{:S(2)}) collective-permute-start(bf16[2,64,32,384]{3,2,1,0:T(8,128)(2,1)} %bitcast.3), channel_id=1, source_target_pairs={{0,1},{1,0},{2,3},{3,2},{4,5},{5,4},{6,7},{7,6},{8,9},{9,8},{10,11... | collective-permute-start | bytes 9437192 | tf_op jit(solution)/shard_map/ppermute | solution.py:508
  359.2 6.3 collective-permute-start.5
  365.5 51.3 %copy-start.6 = (f32[64,320]{1,0:T(8,128)S(1)}, f32[64,320]{1,0:T(8,128)}, u32[]{:S(2)}) copy-start(f32[64,320]{1,0:T(8,128)} %param.9) | copy-start | bytes 245764
  365.5 1.7 copy-start.1
  367.1 1.7 copy-start.2
  415.5 60.0 %collective-permute-start.8 = (bf16[5,32,64,128]{3,2,1,0:T(8,128)(2,1)}, bf16[5,32,64,128]{3,2,1,0:T(8,128)(2,1)S(1)}, u32[]{:S(2)}, u32[]{:S(2)}) collective-permute-start(bf16[5,32,64,128]{3,2,1,0:T(8,128)(2,1)} %get-tuple-element.32), channel_id=1, source_target_pairs={{0,2},{1,3},{2,0},{3,1},{4,6},{5,7},{6,4},{7,5},{8,10},{9,11},{10,... | collective-permute-start | bytes 7864328 | tf_op jit(solution)/shard_map/ppermute | solution.py:511
  417.5 114.2 %collective-permute-start.9 = (bf16[5,32,64,128]{3,2,1,0:T(8,128)(2,1)}, bf16[5,32,64,128]{3,2,1,0:T(8,128)(2,1)S(1)}, u32[]{:S(2)}, u32[]{:S(2)}) collective-permute-start(bf16[5,32,64,128]{3,2,1,0:T(8,128)(2,1)} %get-tuple-element.34), channel_id=1, source_target_pairs={{0,2},{1,3},{2,0},{3,1},{4,6},{5,7},{6,4},{7,5},{8,10},{9,11},{10,... | collective-permute-start | bytes 7864328 | tf_op jit(solution)/shard_map/ppermute | solution.py:511
  475.5 1.5 copy-start.5
  486.7 138.8 %all-to-all-start.2 = ((bf16[4,32,192,128]{3,2,1,0:T(8,128)(2,1)}), bf16[4,32,192,128]{3,2,1,0:T(8,128)(2,1)}, u32[]{:S(2)}, u32[]{:S(2)}) async-start(bf16[4,32,192,128]{3,2,1,0:T(8,128)(2,1)} %lat_backward.2), calls=%async_computation.2 | async-start | bytes 12582912 | tf_op jit(solution)/shard_map/all_to_all | solution.py:514
  521.3 197.3 %collective-permute-start.10 = (bf16[3,11520,128]{2,1,0:T(8,128)(2,1)}, bf16[3,11520,128]{2,1,0:T(8,128)(2,1)}, u32[]{:S(2)}, u32[]{:S(2)}) collective-permute-start(bf16[3,11520,128]{2,1,0:T(8,128)(2,1)} %partial_map.9), channel_id=1, source_target_pairs={{0,2},{1,3},{2,0},{3,1},{4,6},{5,7},{6,4},{7,5},{8,10},{9,11},{10,... | collective-permute-start | bytes 26542088 | tf_op jit(solution)/shard_map/ppermute | solution.py:511
  531.7 1.5 copy-start.4
  625.5 142.9 %all-to-all-start.3 = ((bf16[4,32,192,128]{3,2,1,0:T(8,128)(2,1)}), bf16[4,32,192,128]{3,2,1,0:T(8,128)(2,1)}, u32[]{:S(2)}, u32[]{:S(2)}) async-start(bf16[4,32,192,128]{3,2,1,0:T(8,128)(2,1)} %lat_backward.3), calls=%async_computation.3 | async-start | bytes 12582912 | tf_op jit(solution)/shard_map/all_to_all | solution.py:514
  718.6 170.5 %collective-permute-start.11 = (bf16[2,11520,128]{2,1,0:T(8,128)(2,1)}, bf16[2,11520,128]{2,1,0:T(8,128)(2,1)}, u32[]{:S(2)}, u32[]{:S(2)}) collective-permute-start(bf16[2,11520,128]{2,1,0:T(8,128)(2,1)} %partial_map.10), channel_id=1, source_target_pairs={{0,2},{1,3},{2,0},{3,1},{4,6},{5,7},{6,4},{7,5},{8,10},{9,11},{10,... | collective-permute-start | bytes 17694728 | tf_op jit(solution)/shard_map/ppermute | solution.py:511
  733.3 183.3 %collective-permute-start.12 = (bf16[1,11520,128]{2,1,0:T(8,128)(2,1)}, bf16[1,11520,128]{2,1,0:T(8,128)(2,1)}, u32[]{:S(2)}, u32[]{:S(2)}) collective-permute-start(bf16[1,11520,128]{2,1,0:T(8,128)(2,1)} %partial_map.11), channel_id=1, source_target_pairs={{0,2},{1,3},{2,0},{3,1},{4,6},{5,7},{6,4},{7,5},{8,10},{9,11},{10,... | collective-permute-start | bytes 8847368 | tf_op jit(solution)/shard_map/ppermute | solution.py:511

commit v2 on v1

--- a/solution.py
+++ b/solution.py
@@ -120,7 +120,6 @@
 
 
 MAP_COST = [0, 0, 120, 120, 80, 40]
-FINISH_COST = [0, 0, 0, 0, 0, 0]
 
 
 def call(kernel, name, cost=0, **kwargs):
@@ -400,15 +399,44 @@
     )(field, sibling, kron)
 
 
+def own_map(field, sibling, kron, start, steps):
+    chans = field.shape[0]
+    outs = kron.shape[0] // ROWS
+    depth = chans * ROWS
+
+    def kernel(a_ref, b_ref, w_ref, out):
+        def product(cols, width):
+            a = a_ref[:, :, cols].reshape(depth, width)
+            b = b_ref[:, :, cols].reshape(depth, width)
+            acc = jnp.dot(w_ref[:, :depth], a, preferred_element_type=F32) + jnp.dot(
+                w_ref[:, depth:], b, preferred_element_type=F32
+            )
+            out[:, :, cols] = acc.reshape(outs, ROWS, width)
+
+        @pl.loop(0, FULL)
+        def _(n):
+            product(pl.ds(pl.multiple_of(n * WIDE, WIDE), WIDE), WIDE)
+
+        product(slice(FULL * WIDE, LON), REST)
+
+    rows = pl.BlockSpec((chans, ROWS, LON), lambda i: (0, start + i, 0))
+    return call(
+        kernel,
+        "own_map",
+        grid=(steps,),
+        in_specs=[rows, rows, const_spec(kron.shape)],
+        out_specs=pl.BlockSpec((outs, ROWS, LON), lambda i: (0, i, 0)),
+        out_shape=jax.ShapeDtypeStruct((outs, steps * ROWS, LON), F32),
+    )(field, sibling, kron)
+
+
 def gelu(v):
     return 0.5 * v * (1.0 + lax.erf(v * math.sqrt(0.5)))
 
 
-def finish(previous, field, sibling, kron, spectrum, table, received, start, cost):
-    chans = field.shape[0]
-    outs = kron.shape[0] // ROWS
+def finish(previous, own, spectrum, table, received, start, own_start, shape, cost):
+    outs = own.shape[0]
     height = outs * ROWS
-    depth = chans * ROWS
     packed = height * LON // LANES
     group = LANES // TAIL
     n_sp = spectrum[0].shape[0]
@@ -416,8 +444,8 @@
 
     def kernel(*refs):
         refs = refs[1:] if previous is not None else refs
-        a_ref, b_ref, w_ref, t_ref, p_ref = refs[:5]
-        lats, out, lat = refs[5:-2], refs[-2], refs[-1]
+        o_ref, t_ref, p_ref = refs[:3]
+        lats, out, lat = refs[3:-2], refs[-2], refs[-1]
         at = 0
         for ref, per in zip(lats, sizes):
             for k in range(n_sp):
@@ -427,14 +455,8 @@
             at += per * ROWS
 
         def product(cols, width):
-            a = a_ref[:, :, cols].reshape(depth, width)
-            b = b_ref[:, :, cols].reshape(depth, width)
             spectral = jnp.dot(lat[...], t_ref[:, cols], preferred_element_type=F32)
-            return (
-                spectral * (1.0 / LON)
-                + jnp.dot(w_ref[:, :depth], a, preferred_element_type=F32)
-                + jnp.dot(w_ref[:, depth:], b, preferred_element_type=F32)
-            )
+            return spectral * (1.0 / LON) + o_ref[:, :, cols].reshape(height, width)
 
         @pl.loop(0, FULL)
         def _(n):
@@ -460,11 +482,9 @@
         out[:, :, FULL * WIDE + LANES :] = two.reshape(outs, ROWS, TAIL)
 
     steps = received.shape[0]
-    operands = [field, sibling, kron, table, received, *spectrum]
+    operands = [own, table, received, *spectrum]
     specs = [
-        pl.BlockSpec((chans, ROWS, LON), lambda i: (0, start + i, 0)),
-        pl.BlockSpec((chans, ROWS, LON), lambda i: (0, start + i, 0)),
-        const_spec(kron.shape),
+        pl.BlockSpec((outs, ROWS, LON), lambda i: (0, own_start + i, 0)),
         const_spec(table.shape),
         pl.BlockSpec((1, packed, LANES), lambda i: (i, 0, 0)),
     ] + [
@@ -482,7 +502,7 @@
         grid=(steps,),
         in_specs=specs,
         out_specs=pl.BlockSpec((outs, ROWS, LON), lambda i: (0, start + i, 0)),
-        out_shape=jax.ShapeDtypeStruct(field.shape, BF16),
+        out_shape=jax.ShapeDtypeStruct(shape, BF16),
         input_output_aliases=aliases,
         scratch_shapes=[pltpu.VMEM((height, n_sp * LANES), BF16)],
     )(*operands)
@@ -517,15 +537,15 @@
 
     first = plan[0] * ROWS
     near_first = to_near(lax.slice_in_dim(state_field, 0, first, axis=1))
-    near_field = to_near(after(state_field, near_first))
-    near_weight = to_near(after(spectral_weight, near_first))
-
     def rows_of(index):
         return lax.dynamic_slice_in_dim(bypass_weight, index * chans, chans, 0)
 
     chip_rows = jnp.concatenate([rows_of(ch), rows_of(near)], axis=0)
     kron_far = kron_map(lax.dynamic_slice_in_dim(chip_rows, far * chans, chans, 1))
     kron_own = kron_map(lax.dynamic_slice_in_dim(chip_rows, ch * chans, chans, 1))
+
+    near_field = to_near(after(state_field, near_first, kron_far))
+    near_weight = to_near(after(spectral_weight, near_first))
 
     sent, received, starts = [], [], []
 
@@ -551,9 +571,15 @@
     send_rows(received[0])
     partial_rows(bands[1])
     send_rows(received[1])
-    bands[1] = after(bands[1], sent[2])
+    middle = sum(plan[:3])
+    own = [own_map(state_field, near_field, after(kron_own, sent[2]), 0, middle)]
+    bands[1] = after(bands[1], sent[2], own[0])
     weights = pick_weights(ch, spectral_weight, near_weight)
-    spectra = [lat_forward(across(b), lat).reshape(2, modes, -1, KPAD) for b in bands]
+    bands = [across(b) for b in bands]
+    spectra = [lat_forward(bands[0], lat)]
+    own.append(own_map(state_field, near_field, after(kron_own, spectra[0]), middle, sum(plan[3:])))
+    spectra.append(lat_forward(bands[1], after(lat, own[1])))
+    spectra = [s.reshape(2, modes, -1, KPAD) for s in spectra]
     near_spectra = [to_near(s) for s in spectra]
 
     own_mixed, sends = mix(weights, spectra + near_spectra, parts)
@@ -570,9 +596,10 @@
     send_rows(received[3])
     inverse = lon_table(n_sp, modes, True)
     out = None
-    for got, start, cost in zip(received, starts, FINISH_COST):
+    for got, start in zip(received, starts):
+        late = start >= middle
         out = finish(
-            out, state_field, near_field, kron_own, spectrum, inverse, got, start, cost
+            out, own[late], spectrum, inverse, got, start, start - late * middle, state_field.shape, 0
         )
     return out
 

time: 942 us -> 921 us (0.978)
  waiting for transfers between devices: 494 us -> 450 us
  Pallas kernels: 396 us -> 417 us
    pallas_call x0 -> x2, Pallas kernels: none -> 104 us  [own_map(): call(kernel, 'own_map', grid=(steps,), in_specs=[rows, rows, const_spec(k...]
    all_to_all x4, waiting for transfers between devices: 307 us -> 215 us  [across(): return lax.all_to_all(blocks, 'sp', 0, 0)]
    pallas_call x6, Pallas kernels: 166 us -> 83.2 us  [finish(): call(kernel, 'finish', cost, grid=(steps,), in_specs=specs, out_specs=pl....]
    ppermute x8, waiting for transfers between devices: 182 us -> 235 us  [to_far(): return lax.ppermute(value, 'ch', [(i, i ^ 2) for i in range(n_ch)])]
  transfers between devices with their start and end apart: 17 -> 17, of which waited for: 11 -> 13; matrix products, arithmetic and copies ran while one was open for 0% -> 0% of each run, Pallas kernels for 40% -> 45%
where the time goes in v2:
time: 921 us; the launch traced here: 915 us
  waiting for transfers between devices  450 us (49%)
  Pallas kernels  417 us (45%)
  starting transfers between devices  33.9 us (4%)
  local copies, waits for them, and re-layouts  12.2 us (1%)
    ppermute x8, waiting for transfers between devices, to_far(): return lax.ppermute(value, 'ch', [(i, i ^ 2) for i in range(n_ch)])  235 us
    all_to_all x4, waiting for transfers between devices, across(): return lax.all_to_all(blocks, 'sp', 0, 0)  215 us
    pallas_call x6, Pallas kernels, partial_map(): call(kernel, 'partial_map', cost, grid=(steps,), in_specs=[pl.BlockSpec((...  127 us
    pallas_call x2, Pallas kernels, own_map(): call(kernel, 'own_map', grid=(steps,), in_specs=[rows, rows, const_spec(k...  104 us
    pallas_call x6, Pallas kernels, finish(): call(kernel, 'finish', cost, grid=(steps,), in_specs=specs, out_specs=pl....  83.2 us
    pallas_call x2, Pallas kernels, lon_forward(): call(kernel, 'lon_forward', grid=(count // step,), in_specs=[pl.BlockSpec...  32.2 us
    all_to_all x4, starting transfers between devices, across(): return lax.all_to_all(blocks, 'sp', 0, 0)  21.4 us
    pallas_call x2, Pallas kernels, lat_forward(): call(kernel, 'lat_forward', grid=(count // step,), in_specs=[pl.BlockSpec...  19.6 us
  transfers between devices with their start and end apart: 17, of which 13 were waited for; matrix products, arithmetic and copies ran while one was open for 0% of the time, Pallas kernels for 45%

profile of v2, /device:TPU:0, one launch (start us, length us, event | category | flops | bytes accessed | tf_op | source)
XLA Modules:
  0.0 914.8 jit_solution(17698571898338802496)
XLA Ops:
  0.0 3.8 slice.3
  3.8 0.5 collective-permute-start
  4.3 0.7 fusion
  5.0 4.2 kron_map.2.w_ref
  9.2 0.6 collective-permute-done.b_ref
  9.8 0.4 collective-permute-start.1
  10.1 1.3 copy-done
  11.4 13.3 %partial_map.6 = bf16[1,11520,128]{2,1,0:T(8,128)(2,1)} custom-call(bf16[64,192,1440]{2,1,0:T(8,128)(2,1)} %a_ref.15, bf16[64,16,1440]{2,1,0:T(8,128)(2,1)} %copy-done, bf16[1024,2048]{1,0:T(8,128)(2,1)} %kron_map.2.w_ref), custom_call_target="tpu_custom_call" | custom-call | flops 1 | bytes 1 | tf_op jit(solution)/shard_map/partial_map/pallas_call | solution.py:387
  24.8 2.9 collective-permute-start.2
  27.6 4.3 kron_map.3.w_ref
  31.9 16.1 %lon_forward.3 = bf16[4,32,192,128]{3,2,1,0:T(8,128)(2,1)} custom-call(bf16[64,192,1440]{2,1,0:T(8,128)(2,1)} %a_ref.15, bf16[1440,512]{1,0:T(8,128)(2,1)} %constant.22.clone.t_ref), custom_call_target="tpu_custom_call" | custom-call | flops 1 | bytes 1 | tf_op jit(solution)/shard_map/lon_forward/pallas_call | solution.py:206
  48.0 16.1 %lon_forward.2 = bf16[4,32,192,128]{3,2,1,0:T(8,128)(2,1)} custom-call(bf16[64,192,1440]{2,1,0:T(8,128)(2,1)} %a_ref.15, bf16[1440,512]{1,0:T(8,128)(2,1)} %constant.22.clone.t_ref), custom_call_target="tpu_custom_call" | custom-call | flops 1 | bytes 1 | tf_op jit(solution)/shard_map/lon_forward/pallas_call | solution.py:206
  64.1 5.4 all-to-all-start
  69.6 0.0 collective-permute-done.1.b_ref
  69.6 21.1 %partial_map.8 = bf16[2,11520,128]{2,1,0:T(8,128)(2,1)} custom-call(bf16[64,192,1440]{2,1,0:T(8,128)(2,1)} %a_ref.15, bf16[64,192,1440]{2,1,0:T(8,128)(2,1)} %collective-permute-done.1.b_ref, bf16[1024,2048]{1,0:T(8,128)(2,1)} %kron_map.2.w_ref), custom_call_target="tpu_custom_call" | custom-call | flops 1 | bytes 1 | tf_op jit(solution)/shard_map/partial_map/pallas_call | solution.py:387
  90.7 1.3 collective-permute-done.2.refs_2_
  92.0 1.7 collective-permute-start.6
  93.8 28.9 %partial_map.7 = bf16[3,11520,128]{2,1,0:T(8,128)(2,1)} custom-call(bf16[64,192,1440]{2,1,0:T(8,128)(2,1)} %a_ref.15, bf16[64,192,1440]{2,1,0:T(8,128)(2,1)} %collective-permute-done.1.b_ref, bf16[1024,2048]{1,0:T(8,128)(2,1)} %kron_map.2.w_ref), custom_call_target="tpu_custom_call" | custom-call | flops 120000004096 | bytes 1 | tf_op jit(solution)/shard_map/partial_map/pallas_call | solution.py:387
  122.7 52.1 %own_map.2.refs_0_.refs_1_ = f32[64,96,1440]{2,1,0:T(8,128)} custom-call(bf16[64,192,1440]{2,1,0:T(8,128)(2,1)} %a_ref.15, bf16[64,192,1440]{2,1,0:T(8,128)(2,1)} %collective-permute-done.1.b_ref, bf16[1024,2048]{1,0:T(8,128)(2,1)} %kron_map.3.w_ref), custom_call_target="tpu_custom_call" | custom-call | flops 1 | bytes 1 | tf_op jit(solution)/shard_map/own_map/pallas_call | solution.py:423
  174.7 33.3 %all-to-all-done.x_ref = bf16[4,32,192,128]{3,2,1,0:T(8,128)(2,1)} async-done(((bf16[4,32,192,128]{3,2,1,0:T(8,128)(2,1)}), bf16[4,32,192,128]{3,2,1,0:T(8,128)(2,1)}, u32[]{:S(2)}, u32[]{:S(2)}) %all-to-all-start) | async-done | bytes 6291488 | tf_op jit(solution)/shard_map/all_to_all | solution.py:534
  208.0 5.5 all-to-all-start.1
  213.5 7.5 collective-permute-done.6.refs_3_
  221.1 1.4 collective-permute-start.7
  222.5 0.0 collective-permute-start.3
  222.5 9.8 %lat_forward.2 = bf16[128,32,384]{2,1,0:T(8,128)(2,1)} custom-call(bf16[4,32,192,128]{3,2,1,0:T(8,128)(2,1)} %all-to-all-done.x_ref, bf16[768,768]{1,0:T(8,128)(2,1)} %constant.23.clone.t_ref), custom_call_target="tpu_custom_call" | custom-call | flops 1 | bytes 1 | tf_op jit(solution)/shard_map/lat_forward/pallas_call | solution.py:236
  232.3 0.5 collective-permute-start.4
  232.8 52.1 %own_map.3.refs_1_ = f32[64,96,1440]{2,1,0:T(8,128)} custom-call(bf16[64,192,1440]{2,1,0:T(8,128)(2,1)} %a_ref.15, bf16[64,192,1440]{2,1,0:T(8,128)(2,1)} %collective-permute-done.1.b_ref, bf16[1024,2048]{1,0:T(8,128)(2,1)} %kron_map.3.w_ref), custom_call_target="tpu_custom_call" | custom-call | flops 1 | bytes 1 | tf_op jit(solution)/shard_map/own_map/pallas_call | solution.py:423
  285.0 66.2 %all-to-all-done.1.x_ref = bf16[4,32,192,128]{3,2,1,0:T(8,128)(2,1)} async-done(((bf16[4,32,192,128]{3,2,1,0:T(8,128)(2,1)}), bf16[4,32,192,128]{3,2,1,0:T(8,128)(2,1)}, u32[]{:S(2)}, u32[]{:S(2)}) %all-to-all-start.1) | async-done | bytes 6291488 | tf_op jit(solution)/shard_map/all_to_all | solution.py:534
  351.2 9.8 %lat_forward.3 = bf16[128,32,384]{2,1,0:T(8,128)(2,1)} custom-call(bf16[4,32,192,128]{3,2,1,0:T(8,128)(2,1)} %all-to-all-done.1.x_ref, bf16[768,768]{1,0:T(8,128)(2,1)} %constant.23.clone.t_ref), custom_call_target="tpu_custom_call" | custom-call | flops 1 | bytes 1 | tf_op jit(solution)/shard_map/lat_forward/pallas_call | solution.py:236
  361.0 0.0 collective-permute-start.5
  361.0 6.3 pick_weights.1.w_ref
  367.3 0.0 collective-permute-done.5.refs_3_
  367.3 1.7 copy-done.1
  369.1 1.6 copy-done.2
  370.7 16.7 %mix.1 = (f32[2,64,64,384]{3,2,1,0:T(8,128)}, bf16[5,32,64,128]{3,2,1,0:T(8,128)(2,1)}, bf16[5,32,64,128]{3,2,1,0:T(8,128)(2,1)}) custom-call(bf16[2,64,128,128]{3,2,1,0:T(8,128)(2,1)} %pick_weights.1.w_ref, bf16[2,64,32,384]{3,2,1,0:T(8,128)(2,1)} %bitcast.4, bf16[2,64,32,384]{3,2,1,0:T(8,128)(2,1)} %bitcast.6, bf16[2,64,32,384]{3,2,1,0:T(8,128)(2,1)} %copy-done.1, ...), custom_call_target="tpu_custom_call" | custom-call | flops 1 | bytes 1 | tf_op jit(solution)/shard_map/mix/pallas_call | solution.py:285
  387.4 25.0 %collective-permute-done.7.refs_3_ = bf16[3,11520,128]{2,1,0:T(8,128)(2,1)} collective-permute-done((bf16[3,11520,128]{2,1,0:T(8,128)(2,1)}, bf16[3,11520,128]{2,1,0:T(8,128)(2,1)}, u32[]{:S(2)}, u32[]{:S(2)}) %collective-permute-start.7) | collective-permute-done | bytes 8847392 | tf_op jit(solution)/shard_map/ppermute | solution.py:531
  412.4 1.1 collective-permute-start.8
  413.5 0.7 reshape.15.g_ref
  414.2 1.0 collective-permute-start.9
  415.2 57.3 %collective-permute-done.8.far_ref = bf16[5,32,64,128]{3,2,1,0:T(8,128)(2,1)S(1)} collective-permute-done((bf16[5,32,64,128]{3,2,1,0:T(8,128)(2,1)}, bf16[5,32,64,128]{3,2,1,0:T(8,128)(2,1)S(1)}, u32[]{:S(2)}, u32[]{:S(2)}) %collective-permute-start.8) | collective-permute-done | bytes 2621472 | tf_op jit(solution)/shard_map/ppermute | solution.py:531
  472.4 1.5 copy-done.5
  473.9 9.8 %lat_backward.2 = bf16[4,32,192,128]{3,2,1,0:T(8,128)(2,1)} custom-call(f32[2,64,64,384]{3,2,1,0:T(8,128)} %get-tuple-element.33.own_ref, bf16[5,32,64,128]{3,2,1,0:T(8,128)(2,1)} %copy-done.5, f32[64,1,384]{2,1,0:T(1,128)} %reshape.15.g_ref, bf16[768,768]{1,0:T(8,128)(2,1)} %constant.23.clone.t_ref), custom_call_target="tpu_custom_call" | custom-call | flops 1 | bytes 1 | tf_op jit(solution)/shard_map/lat_backward/pallas_call | solution.py:334
  483.7 5.2 all-to-all-start.2
  488.9 28.9 %partial_map.9 = bf16[3,11520,128]{2,1,0:T(8,128)(2,1)} custom-call(bf16[64,192,1440]{2,1,0:T(8,128)(2,1)} %a_ref.15, bf16[64,192,1440]{2,1,0:T(8,128)(2,1)} %collective-permute-done.1.b_ref, bf16[1024,2048]{1,0:T(8,128)(2,1)} %kron_map.2.w_ref), custom_call_target="tpu_custom_call" | custom-call | flops 120000004096 | bytes 1 | tf_op jit(solution)/shard_map/partial_map/pallas_call | solution.py:387
  517.8 1.1 collective-permute-start.10
  518.9 9.7 %collective-permute-done.9.far_ref = bf16[5,32,64,128]{3,2,1,0:T(8,128)(2,1)S(1)} collective-permute-done((bf16[5,32,64,128]{3,2,1,0:T(8,128)(2,1)}, bf16[5,32,64,128]{3,2,1,0:T(8,128)(2,1)S(1)}, u32[]{:S(2)}, u32[]{:S(2)}) %collective-permute-start.9) | collective-permute-done | bytes 2621472 | tf_op jit(solution)/shard_map/ppermute | solution.py:531
  528.6 1.5 copy-done.4
  530.1 9.8 %lat_backward.3 = bf16[4,32,192,128]{3,2,1,0:T(8,128)(2,1)} custom-call(f32[2,64,64,384]{3,2,1,0:T(8,128)} %get-tuple-element.33.own_ref, bf16[5,32,64,128]{3,2,1,0:T(8,128)(2,1)} %copy-done.4, f32[64,1,384]{2,1,0:T(1,128)} %reshape.15.g_ref, bf16[768,768]{1,0:T(8,128)(2,1)} %constant.23.clone.t_ref), custom_call_target="tpu_custom_call" | custom-call | flops 1 | bytes 1 | tf_op jit(solution)/shard_map/lat_backward/pallas_call | solution.py:334
  539.9 81.5 %all-to-all-done.2.refs_3_.refs_4_ = bf16[4,32,192,128]{3,2,1,0:T(8,128)(2,1)} async-done(((bf16[4,32,192,128]{3,2,1,0:T(8,128)(2,1)}), bf16[4,32,192,128]{3,2,1,0:T(8,128)(2,1)}, u32[]{:S(2)}, u32[]{:S(2)}) %all-to-all-start.2) | async-done | bytes 6291488 | tf_op jit(solution)/shard_map/all_to_all | solution.py:534
  621.4 5.2 all-to-all-start.3
  626.6 21.1 %partial_map.10 = bf16[2,11520,128]{2,1,0:T(8,128)(2,1)} custom-call(bf16[64,192,1440]{2,1,0:T(8,128)(2,1)} %a_ref.15, bf16[64,192,1440]{2,1,0:T(8,128)(2,1)} %collective-permute-done.1.b_ref, bf16[1024,2048]{1,0:T(8,128)(2,1)} %kron_map.2.w_ref), custom_call_target="tpu_custom_call" | custom-call | flops 80000000000 | bytes 1 | tf_op jit(solution)/shard_map/partial_map/pallas_call | solution.py:387
  647.8 67.4 %collective-permute-done.10.refs_3_ = bf16[3,11520,128]{2,1,0:T(8,128)(2,1)} collective-permute-done((bf16[3,11520,128]{2,1,0:T(8,128)(2,1)}, bf16[3,11520,128]{2,1,0:T(8,128)(2,1)}, u32[]{:S(2)}, u32[]{:S(2)}) %collective-permute-start.10) | collective-permute-done | bytes 8847392 | tf_op jit(solution)/shard_map/ppermute | solution.py:531
  715.2 1.1 collective-permute-start.11
  716.3 13.4 %partial_map.11 = bf16[1,11520,128]{2,1,0:T(8,128)(2,1)} custom-call(bf16[64,192,1440]{2,1,0:T(8,128)(2,1)} %a_ref.15, bf16[64,192,1440]{2,1,0:T(8,128)(2,1)} %collective-permute-done.1.b_ref, bf16[1024,2048]{1,0:T(8,128)(2,1)} %kron_map.2.w_ref), custom_call_target="tpu_custom_call" | custom-call | flops 40000000000 | bytes 1 | tf_op jit(solution)/shard_map/partial_map/pallas_call | solution.py:387
  729.7 1.0 collective-permute-start.12
  730.6 33.7 %all-to-all-done.3.refs_4_.refs_5_ = bf16[4,32,192,128]{3,2,1,0:T(8,128)(2,1)} async-done(((bf16[4,32,192,128]{3,2,1,0:T(8,128)(2,1)}), bf16[4,32,192,128]{3,2,1,0:T(8,128)(2,1)}, u32[]{:S(2)}, u32[]{:S(2)}) %all-to-all-start.3) | async-done | bytes 6291488 | tf_op jit(solution)/shard_map/all_to_all | solution.py:534
  764.3 9.5 %finish.6.refs_0_ = bf16[64,192,1440]{2,1,0:T(8,128)(2,1)} custom-call(f32[64,96,1440]{2,1,0:T(8,128)} %own_map.2.refs_0_.refs_1_, bf16[512,1440]{1,0:T(8,128)(2,1)} %constant.24.clone.refs_1_.refs_2_, bf16[1,11520,128]{2,1,0:T(8,128)(2,1)} %copy-done.3, bf16[4,32,192,128]{3,2,1,0:T(8,128)(2,1)} %all-to-all-done.2.refs_3_.refs_4_, ...), custom_call_target="tpu_custom_call" | custom-call | flops 1 | bytes 1 | tf_op jit(solution)/shard_map/finish/pallas_call | solution.py:498
  773.7 13.0 %finish.7.refs_0_ = bf16[64,192,1440]{2,1,0:T(8,128)(2,1)} custom-call(bf16[64,192,1440]{2,1,0:T(8,128)(2,1)} %finish.6.refs_0_, f32[64,96,1440]{2,1,0:T(8,128)} %own_map.2.refs_0_.refs_1_, bf16[512,1440]{1,0:T(8,128)(2,1)} %constant.24.clone.refs_1_.refs_2_, bf16[2,11520,128]{2,1,0:T(8,128)(2,1)} %collective-permute-done.6.refs_3_, ...), custom_call_target="tpu_custom_call", output_to_operand_aliasing={{}: (0, {})} | custom-call | flops 1 | bytes 1 | tf_op jit(solution)/shard_map/finish/pallas_call | solution.py:498
  786.7 19.1 %finish.8.refs_0_ = bf16[64,192,1440]{2,1,0:T(8,128)(2,1)} custom-call(bf16[64,192,1440]{2,1,0:T(8,128)(2,1)} %finish.7.refs_0_, f32[64,96,1440]{2,1,0:T(8,128)} %own_map.2.refs_0_.refs_1_, bf16[512,1440]{1,0:T(8,128)(2,1)} %constant.24.clone.refs_1_.refs_2_, bf16[3,11520,128]{2,1,0:T(8,128)(2,1)} %collective-permute-done.7.refs_3_, ...), custom_call_target="tpu_custom_call", output_to_operand_aliasing={{}: (0, {})} | custom-call | flops 1 | bytes 1 | tf_op jit(solution)/shard_map/finish/pallas_call | solution.py:498
  805.8 19.1 %finish.9.refs_0_ = bf16[64,192,1440]{2,1,0:T(8,128)(2,1)} custom-call(bf16[64,192,1440]{2,1,0:T(8,128)(2,1)} %finish.8.refs_0_, f32[64,96,1440]{2,1,0:T(8,128)} %own_map.3.refs_1_, bf16[512,1440]{1,0:T(8,128)(2,1)} %constant.24.clone.refs_1_.refs_2_, bf16[3,11520,128]{2,1,0:T(8,128)(2,1)} %collective-permute-done.10.refs_3_, ...), custom_call_target="tpu_custom_call", output_to_operand_aliasing={{}: (0, {})} | custom-call | flops 1 | bytes 1 | tf_op jit(solution)/shard_map/finish/pallas_call | solution.py:498
  825.0 20.6 %collective-permute-done.11.refs_3_ = bf16[2,11520,128]{2,1,0:T(8,128)(2,1)} collective-permute-done((bf16[2,11520,128]{2,1,0:T(8,128)(2,1)}, bf16[2,11520,128]{2,1,0:T(8,128)(2,1)}, u32[]{:S(2)}, u32[]{:S(2)}) %collective-permute-start.11) | collective-permute-done | bytes 5898272 | tf_op jit(solution)/shard_map/ppermute | solution.py:531
  845.6 13.0 %finish.10.refs_0_ = bf16[64,192,1440]{2,1,0:T(8,128)(2,1)} custom-call(bf16[64,192,1440]{2,1,0:T(8,128)(2,1)} %finish.9.refs_0_, f32[64,96,1440]{2,1,0:T(8,128)} %own_map.3.refs_1_, bf16[512,1440]{1,0:T(8,128)(2,1)} %constant.24.clone.refs_1_.refs_2_, bf16[2,11520,128]{2,1,0:T(8,128)(2,1)} %collective-permute-done.11.refs_3_, ...), custom_call_target="tpu_custom_call", output_to_operand_aliasing={{}: (0, {})} | custom-call | flops 1 | bytes 1 | tf_op jit(solution)/shard_map/finish/pallas_call | solution.py:498
  858.5 46.2 %collective-permute-done.12.refs_3_ = bf16[1,11520,128]{2,1,0:T(8,128)(2,1)} collective-permute-done((bf16[1,11520,128]{2,1,0:T(8,128)(2,1)}, bf16[1,11520,128]{2,1,0:T(8,128)(2,1)}, u32[]{:S(2)}, u32[]{:S(2)}) %collective-permute-start.12) | collective-permute-done | bytes 2949152 | tf_op jit(solution)/shard_map/ppermute | solution.py:531
  904.8 9.6 %finish.11 = bf16[64,192,1440]{2,1,0:T(8,128)(2,1)} custom-call(bf16[64,192,1440]{2,1,0:T(8,128)(2,1)} %finish.10.refs_0_, f32[64,96,1440]{2,1,0:T(8,128)} %own_map.3.refs_1_, bf16[512,1440]{1,0:T(8,128)(2,1)} %constant.24.clone.refs_1_.refs_2_, bf16[1,11520,128]{2,1,0:T(8,128)(2,1)} %collective-permute-done.12.refs_3_, ...), custom_call_target="tpu_custom_call", output_to_operand_aliasing={{}: (0, {})} | custom-call | flops 1 | bytes 1 | tf_op jit(solution)/shard_map/finish/pallas_call | solution.py:498
  (15 shorter events, 0.0 us)
Async XLA Ops:
  0.0 4.3 copy-start.7
  3.8 6.0 collective-permute-start
  9.8 1.7 copy-start
  9.8 59.8 %collective-permute-start.1 = (bf16[64,192,1440]{2,1,0:T(8,128)(2,1)}, bf16[64,192,1440]{2,1,0:T(8,128)(2,1)}, u32[]{:S(2)}, u32[]{:S(2)}) collective-permute-start(bf16[64,192,1440]{2,1,0:T(8,128)(2,1)} %a_ref.15), channel_id=1, source_target_pairs={{0,1},{1,0},{2,3},{3,2},{4,5},{5,4},{6,7},{7,6},{8,9},{9,8},{10,11... | collective-permute-start | bytes 106168328 | tf_op jit(solution)/shard_map/ppermute | solution.py:528
  24.8 67.3 %collective-permute-start.2 = (bf16[1,11520,128]{2,1,0:T(8,128)(2,1)}, bf16[1,11520,128]{2,1,0:T(8,128)(2,1)S(1)}, u32[]{:S(2)}, u32[]{:S(2)}) collective-permute-start(bf16[1,11520,128]{2,1,0:T(8,128)(2,1)} %partial_map.6), channel_id=1, source_target_pairs={{0,2},{1,3},{2,0},{3,1},{4,6},{5,7},{6,4},{7,5},{8,10},{9,11},{10,... | collective-permute-start | bytes 8847368 | tf_op jit(solution)/shard_map/ppermute | solution.py:531
  64.1 143.9 %all-to-all-start = ((bf16[4,32,192,128]{3,2,1,0:T(8,128)(2,1)}), bf16[4,32,192,128]{3,2,1,0:T(8,128)(2,1)}, u32[]{:S(2)}, u32[]{:S(2)}) async-start(bf16[4,32,192,128]{3,2,1,0:T(8,128)(2,1)} %lon_forward.3), calls=%async_computation | async-start | bytes 12582912 | tf_op jit(solution)/shard_map/all_to_all | solution.py:534
  92.0 30.6 %copy-start.3 = (bf16[1,11520,128]{2,1,0:T(8,128)(2,1)}, bf16[1,11520,128]{2,1,0:T(8,128)(2,1)S(1)}, u32[]{:S(2)}) copy-start(bf16[1,11520,128]{2,1,0:T(8,128)(2,1)S(1)} %collective-permute-done.2.refs_2_) | copy-start | bytes 8847364
  92.0 129.0 %collective-permute-start.6 = (bf16[2,11520,128]{2,1,0:T(8,128)(2,1)}, bf16[2,11520,128]{2,1,0:T(8,128)(2,1)}, u32[]{:S(2)}, u32[]{:S(2)}) collective-permute-start(bf16[2,11520,128]{2,1,0:T(8,128)(2,1)} %partial_map.8), channel_id=1, source_target_pairs={{0,2},{1,3},{2,0},{3,1},{4,6},{5,7},{6,4},{7,5},{8,10},{9,11},{10,... | collective-permute-start | bytes 17694728 | tf_op jit(solution)/shard_map/ppermute | solution.py:531
  208.0 143.2 %all-to-all-start.1 = ((bf16[4,32,192,128]{3,2,1,0:T(8,128)(2,1)}), bf16[4,32,192,128]{3,2,1,0:T(8,128)(2,1)}, u32[]{:S(2)}, u32[]{:S(2)}) async-start(bf16[4,32,192,128]{3,2,1,0:T(8,128)(2,1)} %lon_forward.2), calls=%async_computation.1 | async-start | bytes 12582912 | tf_op jit(solution)/shard_map/all_to_all | solution.py:534
  221.1 191.3 %collective-permute-start.7 = (bf16[3,11520,128]{2,1,0:T(8,128)(2,1)}, bf16[3,11520,128]{2,1,0:T(8,128)(2,1)}, u32[]{:S(2)}, u32[]{:S(2)}) collective-permute-start(bf16[3,11520,128]{2,1,0:T(8,128)(2,1)} %partial_map.7), channel_id=1, source_target_pairs={{0,2},{1,3},{2,0},{3,1},{4,6},{5,7},{6,4},{7,5},{8,10},{9,11},{10,... | collective-permute-start | bytes 26542088 | tf_op jit(solution)/shard_map/ppermute | solution.py:531
  222.5 138.5 %collective-permute-start.3 = (bf16[2,64,64,256]{3,2,1,0:T(8,128)(2,1)}, bf16[2,64,64,256]{3,2,1,0:T(8,128)(2,1)}, u32[]{:S(2)}, u32[]{:S(2)}) collective-permute-start(bf16[2,64,64,256]{3,2,1,0:T(8,128)(2,1)} %a1.1), channel_id=1, source_target_pairs={{0,1},{1,0},{2,3},{3,2},{4,5},{5,4},{6,7},{7,6},{8,9},{9,8},{10,11... | collective-permute-start | bytes 12582920 | tf_op jit(solution)/shard_map/ppermute | solution.py:528
  232.3 135.0 %collective-permute-start.4 = (bf16[2,64,32,384]{3,2,1,0:T(8,128)(2,1)}, bf16[2,64,32,384]{3,2,1,0:T(8,128)(2,1)S(1)}, u32[]{:S(2)}, u32[]{:S(2)}) collective-permute-start(bf16[2,64,32,384]{3,2,1,0:T(8,128)(2,1)} %bitcast.3), channel_id=1, source_target_pairs={{0,1},{1,0},{2,3},{3,2},{4,5},{5,4},{6,7},{7,6},{8,9},{9,8},{10,11... | collective-permute-start | bytes 9437192 | tf_op jit(solution)/shard_map/ppermute | solution.py:528
  361.0 6.3 collective-permute-start.5
  367.3 46.2 %copy-start.6 = (f32[64,320]{1,0:T(8,128)S(1)}, f32[64,320]{1,0:T(8,128)}, u32[]{:S(2)}) copy-start(f32[64,320]{1,0:T(8,128)} %param.9) | copy-start | bytes 245764
  367.3 1.8 copy-start.1
  369.1 1.6 copy-start.2
  412.4 60.0 %collective-permute-start.8 = (bf16[5,32,64,128]{3,2,1,0:T(8,128)(2,1)}, bf16[5,32,64,128]{3,2,1,0:T(8,128)(2,1)S(1)}, u32[]{:S(2)}, u32[]{:S(2)}) collective-permute-start(bf16[5,32,64,128]{3,2,1,0:T(8,128)(2,1)} %get-tuple-element.38), channel_id=1, source_target_pairs={{0,2},{1,3},{2,0},{3,1},{4,6},{5,7},{6,4},{7,5},{8,10},{9,11},{10,... | collective-permute-start | bytes 7864328 | tf_op jit(solution)/shard_map/ppermute | solution.py:531
  414.2 114.4 %collective-permute-start.9 = (bf16[5,32,64,128]{3,2,1,0:T(8,128)(2,1)}, bf16[5,32,64,128]{3,2,1,0:T(8,128)(2,1)S(1)}, u32[]{:S(2)}, u32[]{:S(2)}) collective-permute-start(bf16[5,32,64,128]{3,2,1,0:T(8,128)(2,1)} %get-tuple-element.40), channel_id=1, source_target_pairs={{0,2},{1,3},{2,0},{3,1},{4,6},{5,7},{6,4},{7,5},{8,10},{9,11},{10,... | collective-permute-start | bytes 7864328 | tf_op jit(solution)/shard_map/ppermute | solution.py:531
  472.4 1.5 copy-start.5
  483.7 137.7 %all-to-all-start.2 = ((bf16[4,32,192,128]{3,2,1,0:T(8,128)(2,1)}), bf16[4,32,192,128]{3,2,1,0:T(8,128)(2,1)}, u32[]{:S(2)}, u32[]{:S(2)}) async-start(bf16[4,32,192,128]{3,2,1,0:T(8,128)(2,1)} %lat_backward.2), calls=%async_computation.2 | async-start | bytes 12582912 | tf_op jit(solution)/shard_map/all_to_all | solution.py:534
  517.8 197.4 %collective-permute-start.10 = (bf16[3,11520,128]{2,1,0:T(8,128)(2,1)}, bf16[3,11520,128]{2,1,0:T(8,128)(2,1)}, u32[]{:S(2)}, u32[]{:S(2)}) collective-permute-start(bf16[3,11520,128]{2,1,0:T(8,128)(2,1)} %partial_map.9), channel_id=1, source_target_pairs={{0,2},{1,3},{2,0},{3,1},{4,6},{5,7},{6,4},{7,5},{8,10},{9,11},{10,... | collective-permute-start | bytes 26542088 | tf_op jit(solution)/shard_map/ppermute | solution.py:531
  528.6 1.5 copy-start.4
  621.4 142.9 %all-to-all-start.3 = ((bf16[4,32,192,128]{3,2,1,0:T(8,128)(2,1)}), bf16[4,32,192,128]{3,2,1,0:T(8,128)(2,1)}, u32[]{:S(2)}, u32[]{:S(2)}) async-start(bf16[4,32,192,128]{3,2,1,0:T(8,128)(2,1)} %lat_backward.3), calls=%async_computation.3 | async-start | bytes 12582912 | tf_op jit(solution)/shard_map/all_to_all | solution.py:534
  715.2 130.3 %collective-permute-start.11 = (bf16[2,11520,128]{2,1,0:T(8,128)(2,1)}, bf16[2,11520,128]{2,1,0:T(8,128)(2,1)}, u32[]{:S(2)}, u32[]{:S(2)}) collective-permute-start(bf16[2,11520,128]{2,1,0:T(8,128)(2,1)} %partial_map.10), channel_id=1, source_target_pairs={{0,2},{1,3},{2,0},{3,1},{4,6},{5,7},{6,4},{7,5},{8,10},{9,11},{10,... | collective-permute-start | bytes 17694728 | tf_op jit(solution)/shard_map/ppermute | solution.py:531
  729.7 175.1 %collective-permute-start.12 = (bf16[1,11520,128]{2,1,0:T(8,128)(2,1)}, bf16[1,11520,128]{2,1,0:T(8,128)(2,1)}, u32[]{:S(2)}, u32[]{:S(2)}) collective-permute-start(bf16[1,11520,128]{2,1,0:T(8,128)(2,1)} %partial_map.11), channel_id=1, source_target_pairs={{0,2},{1,3},{2,0},{3,1},{4,6},{5,7},{6,4},{7,5},{8,10},{9,11},{10,... | collective-permute-start | bytes 8847368 | tf_op jit(solution)/shard_map/ppermute | solution.py:531

commit v3 on v2

--- a/solution.py
+++ b/solution.py
@@ -119,7 +119,11 @@
     return jnp.asarray(value.reshape(LAT, 2 * KPAD).astype(ml_dtypes.bfloat16))
 
 
-MAP_COST = [0, 0, 120, 120, 80, 40]
+MAP_COST = [0, 0, 120, 0, 0]
+CARRIED_COST = [120, 120, 40, 40]
+CARRY = 20
+LAT_COST = 150
+OWN_COST = 50
 
 
 def call(kernel, name, cost=0, **kwargs):
@@ -255,9 +259,11 @@
     outs = outs2 // 2
     step = ROWS
     n_in = len(spectra)
+    carry = outs - sum(parts)
 
     def kernel(w_ref, *refs):
-        ins, own, sends, scratch = refs[:n_in], refs[n_in], refs[n_in + 1 : -1], refs[-1]
+        ins, own, carried, sends = refs[:n_in], refs[n_in], refs[n_in + 1], refs[n_in + 2 : -1]
+        scratch = refs[-1]
         for m in range(step):
             y = jnp.concatenate([ref[r, m] for r in range(2) for ref in ins], axis=0)
             wr, wi = w_ref[0, m], w_ref[1, m]
@@ -274,6 +280,8 @@
             jnp.transpose(scratch[:, r * outs2 + outs : (r + 1) * outs2, :], (1, 0, 2))
             for r in range(2)
         ]
+        for r in range(2):
+            carried[r] = far[r][outs - carry :]
         for i, send in enumerate(sends):
             block = [f[sum(parts[:i]) : sum(parts[: i + 1])] for f in far]
             for r in range(2):
@@ -288,26 +296,31 @@
         grid=(modes // step,),
         in_specs=[pl.BlockSpec((2, step, chans, outs2), lambda i: (0, i, 0, 0))]
         + [pl.BlockSpec((2, step, s.shape[2], KPAD), lambda i: (0, i, 0, 0)) for s in spectra],
-        out_specs=[pl.BlockSpec((2, outs, step, KPAD), lambda i: (0, 0, i, 0))]
+        out_specs=[pl.BlockSpec((2, n, step, KPAD), lambda i: (0, 0, i, 0)) for n in (outs, carry)]
         + [pl.BlockSpec((5, per, step, LANES), lambda i: (0, 0, i, 0)) for per in parts],
-        out_shape=[jax.ShapeDtypeStruct((2, outs, modes, KPAD), F32)]
+        out_shape=[jax.ShapeDtypeStruct((2, n, modes, KPAD), F32) for n in (outs, carry)]
         + [jax.ShapeDtypeStruct((5, per, modes, LANES), BF16) for per in parts],
         scratch_shapes=[pltpu.VMEM((step, 2 * outs2, KPAD), F32)],
     )(weights, *spectra)
-    return res[0], res[1:]
-
-
-def lat_backward(own, far, gain, table, start, n_sp):
-    per, modes = far.shape[1:3]
+    return res[0], res[1], res[2:]
+
+
+def lat_backward(own, far, gain, table, start, per, n_sp, cost=0):
+    modes = own.shape[2]
     rows = LAT // n_sp
-    step = 8
-
-    def kernel(own_ref, far_ref, g_ref, t_ref, result):
+    step = 4
+
+    def kernel(own_ref, *refs):
+        far_ref = refs[0] if far is not None else None
+        g_ref, t_ref, result = refs[-3:]
         for pair in range(step // 2):
             blocks = []
             for d in (2 * pair, 2 * pair + 1):
                 z = []
                 for r in range(2):
+                    if far_ref is None:
+                        z.append((own_ref[r, d] * g_ref[d]).astype(BF16))
+                        continue
                     tail = far_ref[4, d][:, r * (LANES // 2) : (r + 1) * (LANES // 2)]
                     sent = jnp.concatenate(
                         [
@@ -334,16 +347,19 @@
     return call(
         kernel,
         "lat_backward",
+        cost,
         grid=(per // step,),
         in_specs=[
             pl.BlockSpec((2, step, modes, KPAD), lambda i: (0, start // step + i, 0, 0)),
-            pl.BlockSpec((5, step, modes, LANES), lambda i: (0, i, 0, 0)),
+        ]
+        + [pl.BlockSpec((5, step, modes, LANES), lambda i: (0, i, 0, 0))] * (far is not None)
+        + [
             pl.BlockSpec((step, 1, KPAD), lambda i: (start // step + i, 0, 0)),
             const_spec(table.shape),
         ],
         out_specs=pl.BlockSpec((n_sp, step, rows, LANES), lambda i: (0, i, 0, 0)),
         out_shape=jax.ShapeDtypeStruct((n_sp, per, rows, LANES), BF16),
-    )(own, far, gain, table)
+    )(*([own] if far is None else [own, far]), gain, table)
 
 
 WIDE = 2 * LANES
@@ -352,7 +368,7 @@
 TAIL = REST - LANES
 
 
-def partial_map(field, sibling, kron, start, steps, cost):
+def partial_map(field, sibling, kron, start, steps, cost, spectrum=None, table=None):
     chans = field.shape[0]
     outs = kron.shape[0] // ROWS
     height = outs * ROWS
@@ -360,13 +376,25 @@
     packed = height * LON // LANES
     group = LANES // TAIL
 
-    def kernel(a_ref, b_ref, w_ref, out):
+    n_sp = spectrum.shape[0] if spectrum is not None else 0
+
+    def kernel(a_ref, b_ref, w_ref, *refs):
+        out = refs[2] if n_sp else refs[0]
+        if n_sp:
+            s_ref, t_ref, _, lat = refs
+            for k in range(n_sp):
+                lat[:, k * LANES : (k + 1) * LANES] = s_ref[k].reshape(height, LANES)
+
         def product(cols, width):
             a = a_ref[:, :, cols].reshape(depth, width)
             b = b_ref[:, :, cols].reshape(depth, width)
-            return jnp.dot(w_ref[:, :depth], a, preferred_element_type=F32) + jnp.dot(
+            acc = jnp.dot(w_ref[:, :depth], a, preferred_element_type=F32) + jnp.dot(
                 w_ref[:, depth:], b, preferred_element_type=F32
             )
+            if n_sp:
+                spectral = jnp.dot(lat[...], t_ref[:, cols], preferred_element_type=F32)
+                acc = acc + spectral * (1.0 / LON)
+            return acc
 
         @pl.loop(0, FULL)
         def _(n):
@@ -393,13 +421,22 @@
             pl.BlockSpec((chans, ROWS, LON), lambda i: (0, start + i, 0)),
             pl.BlockSpec((chans, ROWS, LON), lambda i: (0, sib_start + i, 0)),
             const_spec(kron.shape),
-        ],
+        ]
+        + (
+            [
+                pl.BlockSpec((n_sp, outs, ROWS, LANES), lambda i: (0, 0, start + i, 0)),
+                const_spec(table.shape),
+            ]
+            if n_sp
+            else []
+        ),
         out_specs=pl.BlockSpec((1, packed, LANES), lambda i: (i, 0, 0)),
         out_shape=jax.ShapeDtypeStruct((steps, packed, LANES), BF16),
-    )(field, sibling, kron)
-
-
-def own_map(field, sibling, kron, start, steps):
+        scratch_shapes=[pltpu.VMEM((height, n_sp * LANES), BF16)] if n_sp else [],
+    )(field, sibling, kron, *([spectrum, table] if n_sp else []))
+
+
+def own_map(field, sibling, kron, start, steps, cost=0):
     chans = field.shape[0]
     outs = kron.shape[0] // ROWS
     depth = chans * ROWS
@@ -423,6 +460,7 @@
     return call(
         kernel,
         "own_map",
+        cost,
         grid=(steps,),
         in_specs=[rows, rows, const_spec(kron.shape)],
         out_specs=pl.BlockSpec((outs, ROWS, LON), lambda i: (0, i, 0)),
@@ -434,18 +472,19 @@
     return 0.5 * v * (1.0 + lax.erf(v * math.sqrt(0.5)))
 
 
-def finish(previous, own, spectrum, table, received, start, own_start, shape, cost):
+def finish(previous, own, spectrum, table, received, start, steps, own_start, shape):
     outs = own.shape[0]
     height = outs * ROWS
-    packed = height * LON // LANES
     group = LANES // TAIL
+    heights = [got.shape[1] * LANES // LON for got, _ in received]
     n_sp = spectrum[0].shape[0]
     sizes = [part.shape[1] for part in spectrum]
 
     def kernel(*refs):
         refs = refs[1:] if previous is not None else refs
-        o_ref, t_ref, p_ref = refs[:3]
-        lats, out, lat = refs[3:-2], refs[-2], refs[-1]
+        o_ref, t_ref = refs[:2]
+        packs, lats = refs[2 : 2 + len(received)], refs[2 + len(received) : -2]
+        out, lat = refs[-2], refs[-1]
         at = 0
         for ref, per in zip(lats, sizes):
             for k in range(n_sp):
@@ -462,31 +501,34 @@
         def _(n):
             cols = pl.ds(pl.multiple_of(n * WIDE, WIDE), WIDE)
             acc = product(cols, WIDE)
-            base = pl.multiple_of(n * 2 * height, 2 * height)
-            far = jnp.concatenate(
-                [p_ref[0, pl.ds(base, height), :], p_ref[0, pl.ds(base + height, height), :]], axis=1
-            )
+            far = []
+            for p_ref, high in zip(packs, heights):
+                base = pl.multiple_of(n * 2 * high, 2 * high)
+                far.append([p_ref[0, pl.ds(base + i * high, high), :] for i in range(2)])
+            far = jnp.concatenate([jnp.concatenate(pair, axis=1) for pair in far], axis=0)
             value = gelu(acc + far.astype(F32)).astype(BF16)
             out[:, :, cols] = value.reshape(outs, ROWS, WIDE)
 
         acc = product(slice(FULL * WIDE, LON), REST)
-        size = height // group
-        tails = p_ref[0, (FULL * 2 + 1) * height :, :].astype(F32)
-        tail = jnp.concatenate(
-            [tails[:, q * TAIL : (q + 1) * TAIL] for q in range(group)], axis=0
-        )
-        far = p_ref[0, FULL * 2 * height : (FULL * 2 + 1) * height, :].astype(F32)
+        far, tail = [], []
+        for p_ref, high in zip(packs, heights):
+            far.append(p_ref[0, FULL * 2 * high : (FULL * 2 + 1) * high, :])
+            tails = p_ref[0, (FULL * 2 + 1) * high :, :].astype(F32)
+            tail += [tails[:, q * TAIL : (q + 1) * TAIL] for q in range(group)]
+        far = jnp.concatenate(far, axis=0).astype(F32)
+        tail = jnp.concatenate(tail, axis=0)
         one = gelu(acc[:, :LANES] + far).astype(BF16)
         out[:, :, FULL * WIDE : FULL * WIDE + LANES] = one.reshape(outs, ROWS, LANES)
         two = gelu(acc[:, LANES:] + tail).astype(BF16)
         out[:, :, FULL * WIDE + LANES :] = two.reshape(outs, ROWS, TAIL)
 
-    steps = received.shape[0]
-    operands = [own, table, received, *spectrum]
+    operands = [own, table, *[got for got, _ in received], *spectrum]
     specs = [
         pl.BlockSpec((outs, ROWS, LON), lambda i: (0, own_start + i, 0)),
         const_spec(table.shape),
-        pl.BlockSpec((1, packed, LANES), lambda i: (i, 0, 0)),
+    ] + [
+        pl.BlockSpec((1, got.shape[1], LANES), functools.partial(lambda first, i: (first + i, 0, 0), first))
+        for got, first in received
     ] + [
         pl.BlockSpec((n_sp, per, ROWS, LANES), lambda i: (0, 0, start + i, 0)) for per in sizes
     ]
@@ -498,7 +540,6 @@
     return call(
         kernel,
         "finish",
-        cost,
         grid=(steps,),
         in_specs=specs,
         out_specs=pl.BlockSpec((outs, ROWS, LON), lambda i: (0, start + i, 0)),
@@ -514,7 +555,8 @@
 
 def row_plan(total):
     unit = total // 12
-    return [unit, 2 * unit, 3 * unit, 3 * unit, 2 * unit, total - 11 * unit]
+    last = total - 11 * unit
+    return [2 * unit, 3 * unit, 3 * unit, 3 * unit, last], [4 * unit, 4 * unit, 3 * unit, last]
 
 
 def tiled_body(state_field, spectral_weight, mode_gain, bypass_weight):
@@ -533,73 +575,98 @@
     def across(blocks):
         return lax.all_to_all(blocks, "sp", 0, 0)
 
-    plan = row_plan(rows // ROWS)
-
-    first = plan[0] * ROWS
-    near_first = to_near(lax.slice_in_dim(state_field, 0, first, axis=1))
+    plan, carried_plan = row_plan(rows // ROWS)
+    plain = chans - CARRY
+
+    near_first = to_near(lax.slice_in_dim(state_field, 0, plan[0] * ROWS, axis=1))
+
     def rows_of(index):
         return lax.dynamic_slice_in_dim(bypass_weight, index * chans, chans, 0)
 
     chip_rows = jnp.concatenate([rows_of(ch), rows_of(near)], axis=0)
-    kron_far = kron_map(lax.dynamic_slice_in_dim(chip_rows, far * chans, chans, 1))
-    kron_own = kron_map(lax.dynamic_slice_in_dim(chip_rows, ch * chans, chans, 1))
-
+    far_columns = lax.dynamic_slice_in_dim(chip_rows, far * chans, chans, 1)
+    kron_far = kron_map(far_columns[:, :plain])
     near_field = to_near(after(state_field, near_first, kron_far))
     near_weight = to_near(after(spectral_weight, near_first))
 
-    sent, received, starts = [], [], []
+    sent, received = [], []
 
     def partial_rows(*others):
         i = len(sent)
-        starts.append(sum(plan[:i]))
         sibling = near_field if i else near_first
         kron = after(kron_far, *others)
-        sent.append(partial_map(state_field, sibling, kron, starts[-1], plan[i], MAP_COST[i]))
+        sent.append(partial_map(state_field, sibling, kron, sum(plan[:i]), plan[i], MAP_COST[i]))
 
     def send_rows(*others):
         received.append(to_far(after(sent[len(received)], *others)))
 
     half = chans // 2
-    parts = [half, chans - half]
     table = lon_table(n_sp, modes, False)
+    inverse = lon_table(n_sp, modes, True)
     lat = lat_table()
+    gain = jnp.pad(mode_gain, ((0, 0), (0, KPAD - L))).reshape(chans, 1, KPAD)
+    far_gain = to_far(gain)
     partial_rows()
-    send_rows()
-    table = after(table, sent[0])
-    bands = [lon_forward(state_field, table, i * half, parts[i], n_sp) for i in range(2)]
+    send_rows(far_gain)
+    bands = [lon_forward(state_field, after(table, sent[0]), 0, half, n_sp)]
     partial_rows(bands[0])
     send_rows(received[0])
-    partial_rows(bands[1])
+    partial_rows(sent[1])
     send_rows(received[1])
-    middle = sum(plan[:3])
+    bands.append(lon_forward(state_field, after(table, sent[2]), half, half, n_sp))
+    kron_own = kron_map(lax.dynamic_slice_in_dim(chip_rows, ch * chans, chans, 1))
+    kron_carried = kron_map(far_columns[:, plain:])
+    middle = plan[0]
     own = [own_map(state_field, near_field, after(kron_own, sent[2]), 0, middle)]
     bands[1] = after(bands[1], sent[2], own[0])
     weights = pick_weights(ch, spectral_weight, near_weight)
+    carried_gain = after(far_gain, weights)[plain:]
     bands = [across(b) for b in bands]
     spectra = [lat_forward(bands[0], lat)]
-    own.append(own_map(state_field, near_field, after(kron_own, spectra[0]), middle, sum(plan[3:])))
-    spectra.append(lat_forward(bands[1], after(lat, own[1])))
+    own.append(own_map(state_field, near_field, after(kron_own, spectra[0]), middle, sum(plan[1:]), OWN_COST))
+    spectra.append(lat_forward(bands[1], after(lat, own[1], weights, kron_carried, carried_gain)))
     spectra = [s.reshape(2, modes, -1, KPAD) for s in spectra]
     near_spectra = [to_near(s) for s in spectra]
 
-    own_mixed, sends = mix(weights, spectra + near_spectra, parts)
+    parts = [plain - 16, 16]
+    own_mixed, carried, sends = mix(weights, spectra + near_spectra, parts)
     far_mixed = [to_far(after(s, received[2])) for s in sends]
-
-    gain = jnp.pad(mode_gain, ((0, 0), (0, KPAD - L))).reshape(chans, 1, KPAD)
-    back = [lat_backward(own_mixed, far_mixed[i], gain, lat, i * half, n_sp) for i in range(2)]
-    spectrum = [across(b) for b in back]
-    partial_rows(*sends)
-    send_rows(far_mixed[0])
-    partial_rows(*sends)
-    send_rows(received[3])
-    partial_rows(*sends)
-    send_rows(received[3])
-    inverse = lon_table(n_sp, modes, True)
+    carried = lat_backward(carried, None, carried_gain, lat, 0, CARRY, n_sp)
+    carried = across(carried)
+
+    back = [
+        lat_backward(own_mixed, None, gain, lat, plain, CARRY, n_sp),
+        lat_backward(own_mixed, far_mixed[0], gain, lat, 0, parts[0], n_sp),
+        lat_backward(own_mixed, far_mixed[1], gain, lat, parts[0], parts[1], n_sp, LAT_COST),
+    ]
+    spectrum = []
+    for b in back:
+        spectrum.append(across(after(b, spectrum[-1] if spectrum else carried)))
+    spectrum = spectrum[1:] + spectrum[:1]
+    for _ in range(2):
+        partial_rows(*sends)
+        send_rows(far_mixed[1])
+
+    kron_carried = after(kron_carried, back[2])
+    late = []
+    for i, steps in enumerate(carried_plan):
+        at = sum(carried_plan[:i])
+        block = partial_map(
+            state_field, near_field, kron_carried, at, steps, CARRIED_COST[i], carried, inverse
+        )
+        late.append(to_far(after(block, late[0] if i > 1 else received[4 - i])))
+
     out = None
-    for got, start in zip(received, starts):
-        late = start >= middle
+    cuts = sorted({sum(p[:i]) for p in (plan, carried_plan) for i in range(len(p) + 1)})
+    for start, end in zip(cuts, cuts[1:]):
+        got = []
+        for blocks, p in ((received, plan), (late, carried_plan)):
+            i = max(i for i in range(len(p)) if sum(p[:i]) <= start)
+            got.append((blocks[i], start - sum(p[:i])))
+        part = start >= middle
         out = finish(
-            out, own[late], spectrum, inverse, got, start, start - late * middle, state_field.shape, 0
+            out, own[part], spectrum, inverse, got, start, end - start, start - part * middle,
+            state_field.shape,
         )
     return out
 

time: 921 us -> 909 us (0.987)
  waiting for transfers between devices: 450 us -> 378 us
  Pallas kernels: 417 us -> 463 us
    ppermute x8 -> x12, waiting for transfers between devices: 235 us -> 120 us  [to_far(): return lax.ppermute(value, 'ch', [(i, i ^ 2) for i in range(n_ch)])]
    pallas_call x6 -> x9, Pallas kernels: 127 us -> 158 us  [partial_map(): call(kernel, 'partial_map', cost, grid=(steps,), in_specs=[pl.BlockSpec((...]
    ppermute x5, waiting for transfers between devices: 0.61 us -> 25.5 us  [to_near(): return lax.ppermute(value, 'ch', [(i, i ^ 1) for i in range(n_ch)])]
    all_to_all x4 -> x6, waiting for transfers between devices: 215 us -> 233 us  [across(): return lax.all_to_all(blocks, 'sp', 0, 0)]
    pallas_call x10 -> x12, Pallas kernels: 207 us -> 220 us  [the longest x2 104 us: own_map(): call(kernel, 'own_map', cost, grid=(steps,), in_specs=[rows, rows, const_...]
    all_to_all x4 -> x6, starting transfers between devices: 21.4 us -> 29.5 us  [across(): return lax.all_to_all(blocks, 'sp', 0, 0)]
  transfers between devices with their start and end apart: 17 -> 23, of which waited for: 13 -> 17; matrix products, arithmetic and copies ran while one was open for 0% -> 0% of each run, Pallas kernels for 45% -> 50%
where the time goes in v3:
time: 909 us; the launch traced here: 899 us
  Pallas kernels  463 us (51%)
  waiting for transfers between devices  378 us (42%)
  starting transfers between devices  42.1 us (5%)
  local copies, waits for them, and re-layouts  14.4 us (2%)
    all_to_all x6, waiting for transfers between devices, across(): return lax.all_to_all(blocks, 'sp', 0, 0)  233 us
    pallas_call x9, Pallas kernels, partial_map(): call(kernel, 'partial_map', cost, grid=(steps,), in_specs=[pl.BlockSpec((...  158 us
    ppermute x12, waiting for transfers between devices, to_far(): return lax.ppermute(value, 'ch', [(i, i ^ 2) for i in range(n_ch)])  120 us
    pallas_call x2, Pallas kernels, own_map(): call(kernel, 'own_map', cost, grid=(steps,), in_specs=[rows, rows, const_...  104 us
    pallas_call x6, Pallas kernels, finish(): call(kernel, 'finish', grid=(steps,), in_specs=specs, out_specs=pl.BlockS...  83.2 us
    pallas_call x4, Pallas kernels, lat_backward(): call(kernel, 'lat_backward', cost, grid=(per // step,), in_specs=[pl.Bloc...  32.6 us
    pallas_call x2, Pallas kernels, lon_forward(): call(kernel, 'lon_forward', grid=(count // step,), in_specs=[pl.BlockSpec...  32.2 us
    all_to_all x6, starting transfers between devices, across(): return lax.all_to_all(blocks, 'sp', 0, 0)  29.5 us
  transfers between devices with their start and end apart: 23, of which 17 were waited for; matrix products, arithmetic and copies ran while one was open for 0% of the time, Pallas kernels for 50%

profile of v3, /device:TPU:0, one launch (start us, length us, event | category | flops | bytes accessed | tf_op | source)
XLA Modules:
  0.0 899.1 jit_solution(6899103340664683002)
XLA Ops:
  0.0 6.3 slice.12
  7.5 3.4 kron_map.3.w_ref
  10.9 6.0 collective-permute-done.b_ref
  17.3 2.7 collective-permute-start.2
  20.0 16.4 %partial_map.9 = bf16[2,7920,128]{2,1,0:T(8,128)(2,1)} custom-call(bf16[64,192,1440]{2,1,0:T(8,128)(2,1)} %a_ref.21, bf16[64,32,1440]{2,1,0:T(8,128)(2,1)} %collective-permute-done.b_ref, bf16[704,2048]{1,0:T(8,128)(2,1)} %kron_map.3.w_ref), custom_call_target="tpu_custom_call" | custom-call | flops 1 | bytes 1 | tf_op jit(solution)/shard_map/partial_map/pallas_call | solution.py:415
  37.1 4.3 kron_map.4.w_ref
  41.3 16.1 %lon_forward.2 = bf16[4,32,192,128]{3,2,1,0:T(8,128)(2,1)} custom-call(bf16[64,192,1440]{2,1,0:T(8,128)(2,1)} %a_ref.21, bf16[1440,512]{1,0:T(8,128)(2,1)} %constant.22.clone.t_ref), custom_call_target="tpu_custom_call" | custom-call | flops 1 | bytes 1 | tf_op jit(solution)/shard_map/lon_forward/pallas_call | solution.py:210
  57.4 5.4 all-to-all-start
  62.8 9.5 %collective-permute-done.1.b_ref = bf16[64,192,1440]{2,1,0:T(8,128)(2,1)} collective-permute-done((bf16[64,192,1440]{2,1,0:T(8,128)(2,1)}, bf16[64,192,1440]{2,1,0:T(8,128)(2,1)}, u32[]{:S(2)}, u32[]{:S(2)}) %collective-permute-start.1) | collective-permute-done | bytes 35389472 | tf_op jit(solution)/shard_map/ppermute | solution.py:570
  72.4 22.0 %partial_map.10 = bf16[3,7920,128]{2,1,0:T(8,128)(2,1)} custom-call(bf16[64,192,1440]{2,1,0:T(8,128)(2,1)} %a_ref.21, bf16[64,192,1440]{2,1,0:T(8,128)(2,1)} %collective-permute-done.1.b_ref, bf16[704,2048]{1,0:T(8,128)(2,1)} %kron_map.3.w_ref), custom_call_target="tpu_custom_call" | custom-call | flops 1 | bytes 1 | tf_op jit(solution)/shard_map/partial_map/pallas_call | solution.py:415
  94.4 32.5 %collective-permute-done.3.refs_2_ = bf16[2,7920,128]{2,1,0:T(8,128)(2,1)} collective-permute-done((bf16[2,7920,128]{2,1,0:T(8,128)(2,1)}, bf16[2,7920,128]{2,1,0:T(8,128)(2,1)}, u32[]{:S(2)}, u32[]{:S(2)}) %collective-permute-start.3) | collective-permute-done | bytes 4055072 | tf_op jit(solution)/shard_map/ppermute | solution.py:573
  127.3 22.1 %partial_map.11 = bf16[3,7920,128]{2,1,0:T(8,128)(2,1)} custom-call(bf16[64,192,1440]{2,1,0:T(8,128)(2,1)} %a_ref.21, bf16[64,192,1440]{2,1,0:T(8,128)(2,1)} %collective-permute-done.1.b_ref, bf16[704,2048]{1,0:T(8,128)(2,1)} %kron_map.3.w_ref), custom_call_target="tpu_custom_call" | custom-call | flops 120000004096 | bytes 1 | tf_op jit(solution)/shard_map/partial_map/pallas_call | solution.py:415
  149.3 16.1 %lon_forward.3 = bf16[4,32,192,128]{3,2,1,0:T(8,128)(2,1)} custom-call(bf16[64,192,1440]{2,1,0:T(8,128)(2,1)} %a_ref.21, bf16[1440,512]{1,0:T(8,128)(2,1)} %constant.22.clone.t_ref), custom_call_target="tpu_custom_call" | custom-call | flops 1 | bytes 1 | tf_op jit(solution)/shard_map/lon_forward/pallas_call | solution.py:210
  165.5 21.7 %own_map.2.refs_0_ = f32[64,32,1440]{2,1,0:T(8,128)} custom-call(bf16[64,192,1440]{2,1,0:T(8,128)(2,1)} %a_ref.21, bf16[64,192,1440]{2,1,0:T(8,128)(2,1)} %collective-permute-done.1.b_ref, bf16[1024,2048]{1,0:T(8,128)(2,1)} %kron_map.4.w_ref), custom_call_target="tpu_custom_call" | custom-call | flops 1 | bytes 1 | tf_op jit(solution)/shard_map/own_map/pallas_call | solution.py:460
  187.2 14.3 %all-to-all-done.x_ref = bf16[4,32,192,128]{3,2,1,0:T(8,128)(2,1)} async-done(((bf16[4,32,192,128]{3,2,1,0:T(8,128)(2,1)}), bf16[4,32,192,128]{3,2,1,0:T(8,128)(2,1)}, u32[]{:S(2)}, u32[]{:S(2)}) %all-to-all-start) | async-done | bytes 6291488 | tf_op jit(solution)/shard_map/all_to_all | solution.py:576
  201.5 5.5 all-to-all-start.1
  207.8 2.5 kron_map.5.w_ref
  210.3 4.2 collective-permute-done.4.b0.b1
  214.4 2.0 copy-done.1
  216.4 6.2 pick_weights.1.w_ref
  222.6 1.4 slice.15.refs_0_
  224.0 9.8 %lat_forward.2 = bf16[128,32,384]{2,1,0:T(8,128)(2,1)} custom-call(bf16[4,32,192,128]{3,2,1,0:T(8,128)(2,1)} %all-to-all-done.x_ref, bf16[768,768]{1,0:T(8,128)(2,1)} %constant.24.clone.t_ref.refs_2_.refs_1_), custom_call_target="tpu_custom_call" | custom-call | flops 1 | bytes 1 | tf_op jit(solution)/shard_map/lat_forward/pallas_call | solution.py:240
  233.9 25.5 %collective-permute-done.7.refs_3_ = bf16[3,7920,128]{2,1,0:T(8,128)(2,1)} collective-permute-done((bf16[3,7920,128]{2,1,0:T(8,128)(2,1)}, bf16[3,7920,128]{2,1,0:T(8,128)(2,1)}, u32[]{:S(2)}, u32[]{:S(2)}) %collective-permute-start.7) | collective-permute-done | bytes 6082592 | tf_op jit(solution)/shard_map/ppermute | solution.py:573
  260.1 82.5 %own_map.3.refs_1_ = f32[64,160,1440]{2,1,0:T(8,128)} custom-call(bf16[64,192,1440]{2,1,0:T(8,128)(2,1)} %a_ref.21, bf16[64,192,1440]{2,1,0:T(8,128)(2,1)} %collective-permute-done.1.b_ref, bf16[1024,2048]{1,0:T(8,128)(2,1)} %kron_map.4.w_ref), custom_call_target="tpu_custom_call" | custom-call | flops 49999998976 | bytes 1 | tf_op jit(solution)/shard_map/own_map/pallas_call | solution.py:460
  342.6 2.2 all-to-all-done.1.x_ref
  344.8 9.8 %lat_forward.3 = bf16[128,32,384]{2,1,0:T(8,128)(2,1)} custom-call(bf16[4,32,192,128]{3,2,1,0:T(8,128)(2,1)} %all-to-all-done.1.x_ref, bf16[768,768]{1,0:T(8,128)(2,1)} %constant.24.clone.t_ref.refs_2_.refs_1_), custom_call_target="tpu_custom_call" | custom-call | flops 1 | bytes 1 | tf_op jit(solution)/shard_map/lat_forward/pallas_call | solution.py:240
  354.6 5.9 collective-permute-done.6.refs_3_
  360.5 1.6 copy-done.3
  362.1 17.4 %mix.1 = (f32[2,64,64,384]{3,2,1,0:T(8,128)}, f32[2,20,64,384]{3,2,1,0:T(8,128)}, bf16[5,28,64,128]{3,2,1,0:T(8,128)(2,1)}, bf16[5,16,64,128]{3,2,1,0:T(8,128)(2,1)}) custom-call(bf16[2,64,128,128]{3,2,1,0:T(8,128)(2,1)} %pick_weights.1.w_ref, bf16[2,64,32,384]{3,2,1,0:T(8,128)(2,1)} %bitcast.5, bf16[2,64,32,384]{3,2,1,0:T(8,128)(2,1)} %bitcast.7, ...), custom_call_target="tpu_custom_call" | custom-call | flops 1 | bytes 1 | tf_op jit(solution)/shard_map/mix/pallas_call | solution.py:293
  379.5 11.5 %collective-permute-done.8.refs_3_ = bf16[3,7920,128]{2,1,0:T(8,128)(2,1)} collective-permute-done((bf16[3,7920,128]{2,1,0:T(8,128)(2,1)}, bf16[3,7920,128]{2,1,0:T(8,128)(2,1)}, u32[]{:S(2)}, u32[]{:S(2)}) %collective-permute-start.8) | collective-permute-done | bytes 6082592 | tf_op jit(solution)/shard_map/ppermute | solution.py:573
  391.0 1.0 collective-permute-start.9
  392.0 7.7 lat_backward.5
  399.7 4.8 all-to-all-start.2
  404.5 1.1 collective-permute-start.12
  405.6 7.7 lat_backward.7
  413.4 10.7 %partial_map.13 = bf16[1,7920,128]{2,1,0:T(8,128)(2,1)} custom-call(bf16[64,192,1440]{2,1,0:T(8,128)(2,1)} %a_ref.21, bf16[64,192,1440]{2,1,0:T(8,128)(2,1)} %collective-permute-done.1.b_ref, bf16[704,2048]{1,0:T(8,128)(2,1)} %kron_map.3.w_ref), custom_call_target="tpu_custom_call" | custom-call | flops 1 | bytes 1 | tf_op jit(solution)/shard_map/partial_map/pallas_call | solution.py:415
  424.0 22.2 %partial_map.15 = bf16[3,7920,128]{2,1,0:T(8,128)(2,1)} custom-call(bf16[64,192,1440]{2,1,0:T(8,128)(2,1)} %a_ref.21, bf16[64,192,1440]{2,1,0:T(8,128)(2,1)} %collective-permute-done.1.b_ref, bf16[704,2048]{1,0:T(8,128)(2,1)} %kron_map.3.w_ref), custom_call_target="tpu_custom_call" | custom-call | flops 1 | bytes 1 | tf_op jit(solution)/shard_map/partial_map/pallas_call | solution.py:415
  446.2 1.0 collective-permute-start.10
  447.3 6.7 lat_backward.4
  453.9 1.0 collective-permute-start.13
  455.0 17.2 %collective-permute-done.12.refs_0_ = bf16[5,28,64,128]{3,2,1,0:T(8,128)(2,1)} collective-permute-done((bf16[5,28,64,128]{3,2,1,0:T(8,128)(2,1)}, bf16[5,28,64,128]{3,2,1,0:T(8,128)(2,1)}, u32[]{:S(2)}, u32[]{:S(2)}) %collective-permute-start.12) | collective-permute-done | bytes 2293792 | tf_op jit(solution)/shard_map/ppermute | solution.py:573
  472.2 10.4 %lat_backward.6 = bf16[4,28,192,128]{3,2,1,0:T(8,128)(2,1)} custom-call(f32[2,64,64,384]{3,2,1,0:T(8,128)} %get-tuple-element.48.own_ref, bf16[5,28,64,128]{3,2,1,0:T(8,128)(2,1)} %collective-permute-done.12.refs_0_, f32[64,1,384]{2,1,0:T(1,128)} %copy-done.4, bf16[768,768]{1,0:T(8,128)(2,1)} %constant.24.clone.t_ref.refs_2_.refs_1_), custom_call_target="tpu_custom_call" | custom-call | flops 1 | bytes 1 | tf_op jit(solution)/shard_map/lat_backward/pallas_call | solution.py:347
  482.6 7.4 all-to-all-done.2.refs_0_
  490.0 4.8 all-to-all-start.3
  494.8 19.9 %partial_map.12 = bf16[4,3600,128]{2,1,0:T(8,128)(2,1)} custom-call(bf16[64,192,1440]{2,1,0:T(8,128)(2,1)} %a_ref.21, bf16[64,192,1440]{2,1,0:T(8,128)(2,1)} %collective-permute-done.1.b_ref, bf16[320,2048]{1,0:T(8,128)(2,1)} %kron_map.5.w_ref, bf16[4,20,192,128]{3,2,1,0:T(8,128)(2,1)} %all-to-all-done.2.refs_0_, ...), custom_call_target="tpu_custom_call" | custom-call | flops 120000004096 | bytes 1 | tf_op jit(solution)/shard_map/partial_map/pallas_call | solution.py:415
  515.6 1.0 collective-permute-start.11
  516.6 65.3 %all-to-all-done.3.refs_6_.refs_7_ = bf16[4,20,192,128]{3,2,1,0:T(8,128)(2,1)} async-done(((bf16[4,20,192,128]{3,2,1,0:T(8,128)(2,1)}), bf16[4,20,192,128]{3,2,1,0:T(8,128)(2,1)}, u32[]{:S(2)}, u32[]{:S(2)}) %all-to-all-start.3) | async-done | bytes 3932192 | tf_op jit(solution)/shard_map/all_to_all | solution.py:576
  581.9 5.1 all-to-all-start.4
  587.0 19.9 %partial_map.14 = bf16[4,3600,128]{2,1,0:T(8,128)(2,1)} custom-call(bf16[64,192,1440]{2,1,0:T(8,128)(2,1)} %a_ref.21, bf16[64,192,1440]{2,1,0:T(8,128)(2,1)} %collective-permute-done.1.b_ref, bf16[320,2048]{1,0:T(8,128)(2,1)} %kron_map.5.w_ref, bf16[4,20,192,128]{3,2,1,0:T(8,128)(2,1)} %all-to-all-done.2.refs_0_, ...), custom_call_target="tpu_custom_call" | custom-call | flops 120000004096 | bytes 1 | tf_op jit(solution)/shard_map/partial_map/pallas_call | solution.py:415
  606.9 100.9 %all-to-all-done.4.refs_4_.refs_5_ = bf16[4,28,192,128]{3,2,1,0:T(8,128)(2,1)} async-done(((bf16[4,28,192,128]{3,2,1,0:T(8,128)(2,1)}), bf16[4,28,192,128]{3,2,1,0:T(8,128)(2,1)}, u32[]{:S(2)}, u32[]{:S(2)}) %all-to-all-start.4) | async-done | bytes 5505056 | tf_op jit(solution)/shard_map/all_to_all | solution.py:576
  707.8 4.0 all-to-all-start.5
  711.8 16.1 %partial_map.16 = bf16[3,3600,128]{2,1,0:T(8,128)(2,1)} custom-call(bf16[64,192,1440]{2,1,0:T(8,128)(2,1)} %a_ref.21, bf16[64,192,1440]{2,1,0:T(8,128)(2,1)} %collective-permute-done.1.b_ref, bf16[320,2048]{1,0:T(8,128)(2,1)} %kron_map.5.w_ref, bf16[4,20,192,128]{3,2,1,0:T(8,128)(2,1)} %all-to-all-done.2.refs_0_, ...), custom_call_target="tpu_custom_call" | custom-call | flops 40000000000 | bytes 1 | tf_op jit(solution)/shard_map/partial_map/pallas_call | solution.py:415
  728.6 1.4 collective-permute-start.15
  729.9 8.4 partial_map.17
  739.0 42.8 %all-to-all-done.5.refs_5_.refs_6_ = bf16[4,16,192,128]{3,2,1,0:T(8,128)(2,1)S(1)} async-done(((bf16[4,16,192,128]{3,2,1,0:T(8,128)(2,1)}), bf16[4,16,192,128]{3,2,1,0:T(8,128)(2,1)S(1)}, u32[]{:S(2)}, u32[]{:S(2)}) %all-to-all-start.5) | async-done | bytes 3145760 | tf_op jit(solution)/shard_map/all_to_all | solution.py:576
  781.9 1.7 copy-done
  783.6 13.0 %finish.6.refs_0_ = bf16[64,192,1440]{2,1,0:T(8,128)(2,1)} custom-call(f32[64,32,1440]{2,1,0:T(8,128)} %own_map.2.refs_0_, bf16[512,1440]{1,0:T(8,128)(2,1)} %constant.23.clone.refs_1_.refs_2_, bf16[2,7920,128]{2,1,0:T(8,128)(2,1)} %collective-permute-done.3.refs_2_, bf16[4,3600,128]{2,1,0:T(8,128)(2,1)} %collective-permute-done.11.refs_3_.refs_4_, ...), custom_call_target="tpu_custom_call" | custom-call | flops 1 | bytes 1 | tf_op jit(solution)/shard_map/finish/pallas_call | solution.py:540
  796.6 13.1 %finish.7.refs_0_ = bf16[64,192,1440]{2,1,0:T(8,128)(2,1)} custom-call(bf16[64,192,1440]{2,1,0:T(8,128)(2,1)} %finish.6.refs_0_, f32[64,160,1440]{2,1,0:T(8,128)} %own_map.3.refs_1_, bf16[512,1440]{1,0:T(8,128)(2,1)} %constant.23.clone.refs_1_.refs_2_, bf16[3,7920,128]{2,1,0:T(8,128)(2,1)} %collective-permute-done.7.refs_3_, ...), custom_call_target="tpu_custom_call", output_to_operand_aliasing={{}: (0, {})} | custom-call | flops 1 | bytes 1 | tf_op jit(solution)/shard_map/finish/pallas_call | solution.py:540
  809.7 1.1 collective-permute-done.14.refs_4_
  810.8 9.4 %finish.8.refs_0_ = bf16[64,192,1440]{2,1,0:T(8,128)(2,1)} custom-call(bf16[64,192,1440]{2,1,0:T(8,128)(2,1)} %finish.7.refs_0_, f32[64,160,1440]{2,1,0:T(8,128)} %own_map.3.refs_1_, bf16[512,1440]{1,0:T(8,128)(2,1)} %constant.23.clone.refs_1_.refs_2_, bf16[3,7920,128]{2,1,0:T(8,128)(2,1)} %collective-permute-done.7.refs_3_, ...), custom_call_target="tpu_custom_call", output_to_operand_aliasing={{}: (0, {})} | custom-call | flops 1 | bytes 1 | tf_op jit(solution)/shard_map/finish/pallas_call | solution.py:540
  820.2 19.1 %finish.9.refs_0_ = bf16[64,192,1440]{2,1,0:T(8,128)(2,1)} custom-call(bf16[64,192,1440]{2,1,0:T(8,128)(2,1)} %finish.8.refs_0_, f32[64,160,1440]{2,1,0:T(8,128)} %own_map.3.refs_1_, bf16[512,1440]{1,0:T(8,128)(2,1)} %constant.23.clone.refs_1_.refs_2_, bf16[3,7920,128]{2,1,0:T(8,128)(2,1)} %collective-permute-done.8.refs_3_, ...), custom_call_target="tpu_custom_call", output_to_operand_aliasing={{}: (0, {})} | custom-call | flops 1 | bytes 1 | tf_op jit(solution)/shard_map/finish/pallas_call | solution.py:540
  839.3 30.7 %collective-permute-done.15.refs_4_ = bf16[3,3600,128]{2,1,0:T(8,128)(2,1)} collective-permute-done((bf16[3,3600,128]{2,1,0:T(8,128)(2,1)}, bf16[3,3600,128]{2,1,0:T(8,128)(2,1)}, u32[]{:S(2)}, u32[]{:S(2)}) %collective-permute-start.15) | collective-permute-done | bytes 2764832 | tf_op jit(solution)/shard_map/ppermute | solution.py:573
  870.1 19.1 %finish.10.refs_0_ = bf16[64,192,1440]{2,1,0:T(8,128)(2,1)} custom-call(bf16[64,192,1440]{2,1,0:T(8,128)(2,1)} %finish.9.refs_0_, f32[64,160,1440]{2,1,0:T(8,128)} %own_map.3.refs_1_, bf16[512,1440]{1,0:T(8,128)(2,1)} %constant.23.clone.refs_1_.refs_2_, bf16[3,7920,128]{2,1,0:T(8,128)(2,1)} %collective-permute-done.13.refs_3_, ...), custom_call_target="tpu_custom_call", output_to_operand_aliasing={{}: (0, {})} | custom-call | flops 1 | bytes 1 | tf_op jit(solution)/shard_map/finish/pallas_call | solution.py:540
  889.2 9.5 %finish.11 = bf16[64,192,1440]{2,1,0:T(8,128)(2,1)} custom-call(bf16[64,192,1440]{2,1,0:T(8,128)(2,1)} %finish.10.refs_0_, f32[64,160,1440]{2,1,0:T(8,128)} %own_map.3.refs_1_, bf16[512,1440]{1,0:T(8,128)(2,1)} %constant.23.clone.refs_1_.refs_2_, bf16[1,7920,128]{2,1,0:T(8,128)(2,1)} %collective-permute-done.10.refs_3_, ...), custom_call_target="tpu_custom_call", output_to_operand_aliasing={{}: (0, {})} | custom-call | flops 1 | bytes 1 | tf_op jit(solution)/shard_map/finish/pallas_call | solution.py:540
  (39 shorter events, 6.4 us)
Async XLA Ops:
  0.0 6.7 copy-start.7
  0.0 17.2 %copy-start.6 = (f32[64,320]{1,0:T(8,128)S(1)}, f32[64,320]{1,0:T(8,128)}, u32[]{:S(2)}) copy-start(f32[64,320]{1,0:T(8,128)} %param.9) | copy-start | bytes 245764
  6.3 10.6 %collective-permute-start = (bf16[64,32,1440]{2,1,0:T(8,128)(2,1)}, bf16[64,32,1440]{2,1,0:T(8,128)(2,1)}, u32[]{:S(2)}, u32[]{:S(2)}) collective-permute-start(bf16[64,32,1440]{2,1,0:T(8,128)(2,1)} %slice.12), channel_id=1, source_target_pairs={{0,1},{1,0},{2,3},{3,2},{4,5},{5,4},{6,7},{7,6},{8,9},{9,8},{10,11... | collective-permute-start | bytes 17694728 | tf_op jit(solution)/shard_map/ppermute | solution.py:570
  16.9 55.5 %collective-permute-start.1 = (bf16[64,192,1440]{2,1,0:T(8,128)(2,1)}, bf16[64,192,1440]{2,1,0:T(8,128)(2,1)}, u32[]{:S(2)}, u32[]{:S(2)}) collective-permute-start(bf16[64,192,1440]{2,1,0:T(8,128)(2,1)} %a_ref.21), channel_id=1, source_target_pairs={{0,1},{1,0},{2,3},{3,2},{4,5},{5,4},{6,7},{7,6},{8,9},{9,8},{10,11... | collective-permute-start | bytes 106168328 | tf_op jit(solution)/shard_map/ppermute | solution.py:570
  17.3 19.1 %copy-start.4 = (f32[64,1,384]{2,1,0:T(1,128)}, f32[64,1,384]{2,1,0:T(1,128)S(1)}, u32[]{:S(2)}) copy-start(f32[64,1,384]{2,1,0:T(1,128)S(1)} %reshape.12.refs_1_.refs_0_) | copy-start | bytes 294916
  17.3 19.1 %collective-permute-start.2 = (f32[64,1,384]{2,1,0:T(1,128)S(1)}, f32[64,1,384]{2,1,0:T(1,128)S(1)}, u32[]{:S(2)}, u32[]{:S(2)}) collective-permute-start(f32[64,1,384]{2,1,0:T(1,128)S(1)} %reshape.12.refs_1_.refs_0_), channel_id=1, source_target_pairs={{0,2},{1,3},{2,0},{3,1},{4,6},{5,7},{6,4},{7,5},{8,10},{9,11},{10,... | collective-permute-start | bytes 294920 | tf_op jit(solution)/shard_map/ppermute | solution.py:573
  36.4 0.6 copy-start.8
  37.0 89.9 %collective-permute-start.3 = (bf16[2,7920,128]{2,1,0:T(8,128)(2,1)}, bf16[2,7920,128]{2,1,0:T(8,128)(2,1)}, u32[]{:S(2)}, u32[]{:S(2)}) collective-permute-start(bf16[2,7920,128]{2,1,0:T(8,128)(2,1)} %partial_map.9), channel_id=1, source_target_pairs={{0,2},{1,3},{2,0},{3,1},{4,6},{5,7},{6,4},{7,5},{8,10},{9,11},{10,... | collective-permute-start | bytes 12165128 | tf_op jit(solution)/shard_map/ppermute | solution.py:573
  57.4 144.1 %all-to-all-start = ((bf16[4,32,192,128]{3,2,1,0:T(8,128)(2,1)}), bf16[4,32,192,128]{3,2,1,0:T(8,128)(2,1)}, u32[]{:S(2)}, u32[]{:S(2)}) async-start(bf16[4,32,192,128]{3,2,1,0:T(8,128)(2,1)} %lon_forward.2), calls=%async_computation | async-start | bytes 12582912 | tf_op jit(solution)/shard_map/all_to_all | solution.py:576
  126.9 132.5 %collective-permute-start.7 = (bf16[3,7920,128]{2,1,0:T(8,128)(2,1)}, bf16[3,7920,128]{2,1,0:T(8,128)(2,1)}, u32[]{:S(2)}, u32[]{:S(2)}) collective-permute-start(bf16[3,7920,128]{2,1,0:T(8,128)(2,1)} %partial_map.10), channel_id=1, source_target_pairs={{0,2},{1,3},{2,0},{3,1},{4,6},{5,7},{6,4},{7,5},{8,10},{9,11},{10,... | collective-permute-start | bytes 18247688 | tf_op jit(solution)/shard_map/ppermute | solution.py:573
  187.2 19.9 %copy-start.5 = (bf16[128,64]{1,0:T(8,128)(2,1)S(1)}, bf16[128,64]{1,0:T(8,128)(2,1)}, u32[]{:S(2)}) copy-start(bf16[128,64]{1,0:T(8,128)(2,1)} %get-tuple-element.70) | copy-start | bytes 49156
  201.5 143.3 %all-to-all-start.1 = ((bf16[4,32,192,128]{3,2,1,0:T(8,128)(2,1)}), bf16[4,32,192,128]{3,2,1,0:T(8,128)(2,1)}, u32[]{:S(2)}, u32[]{:S(2)}) async-start(bf16[4,32,192,128]{3,2,1,0:T(8,128)(2,1)} %lon_forward.3), calls=%async_computation.1 | async-start | bytes 12582912 | tf_op jit(solution)/shard_map/all_to_all | solution.py:576
  207.0 7.4 collective-permute-start.4
  214.4 2.0 copy-start.1
  233.8 120.8 %collective-permute-start.5 = (bf16[2,64,32,384]{3,2,1,0:T(8,128)(2,1)}, bf16[2,64,32,384]{3,2,1,0:T(8,128)(2,1)S(1)}, u32[]{:S(2)}, u32[]{:S(2)}) collective-permute-start(bf16[2,64,32,384]{3,2,1,0:T(8,128)(2,1)} %bitcast.4), channel_id=1, source_target_pairs={{0,1},{1,0},{2,3},{3,2},{4,5},{5,4},{6,7},{7,6},{8,9},{9,8},{10,11... | collective-permute-start | bytes 9437192 | tf_op jit(solution)/shard_map/ppermute | solution.py:570
  259.4 131.6 %collective-permute-start.8 = (bf16[3,7920,128]{2,1,0:T(8,128)(2,1)}, bf16[3,7920,128]{2,1,0:T(8,128)(2,1)}, u32[]{:S(2)}, u32[]{:S(2)}) collective-permute-start(bf16[3,7920,128]{2,1,0:T(8,128)(2,1)} %partial_map.11), channel_id=1, source_target_pairs={{0,2},{1,3},{2,0},{3,1},{4,6},{5,7},{6,4},{7,5},{8,10},{9,11},{10,... | collective-permute-start | bytes 18247688 | tf_op jit(solution)/shard_map/ppermute | solution.py:573
  354.6 5.9 collective-permute-start.6
  354.6 5.9 copy-start.2
  360.5 1.6 copy-start.3
  391.0 55.2 %collective-permute-start.9 = (bf16[5,16,64,128]{3,2,1,0:T(8,128)(2,1)}, bf16[5,16,64,128]{3,2,1,0:T(8,128)(2,1)S(1)}, u32[]{:S(2)}, u32[]{:S(2)}) collective-permute-start(bf16[5,16,64,128]{3,2,1,0:T(8,128)(2,1)} %get-tuple-element.52), channel_id=1, source_target_pairs={{0,2},{1,3},{2,0},{3,1},{4,6},{5,7},{6,4},{7,5},{8,10},{9,11},{10,... | collective-permute-start | bytes 3932168 | tf_op jit(solution)/shard_map/ppermute | solution.py:573
  399.7 90.3 %all-to-all-start.2 = ((bf16[4,20,192,128]{3,2,1,0:T(8,128)(2,1)}), bf16[4,20,192,128]{3,2,1,0:T(8,128)(2,1)}, u32[]{:S(2)}, u32[]{:S(2)}) async-start(bf16[4,20,192,128]{3,2,1,0:T(8,128)(2,1)} %lat_backward.5), calls=%async_computation.2 | async-start | bytes 7864320 | tf_op jit(solution)/shard_map/all_to_all | solution.py:576
  404.5 67.6 %collective-permute-start.12 = (bf16[5,28,64,128]{3,2,1,0:T(8,128)(2,1)}, bf16[5,28,64,128]{3,2,1,0:T(8,128)(2,1)}, u32[]{:S(2)}, u32[]{:S(2)}) collective-permute-start(bf16[5,28,64,128]{3,2,1,0:T(8,128)(2,1)} %get-tuple-element.59), channel_id=1, source_target_pairs={{0,2},{1,3},{2,0},{3,1},{4,6},{5,7},{6,4},{7,5},{8,10},{9,11},{10,... | collective-permute-start | bytes 6881288 | tf_op jit(solution)/shard_map/ppermute | solution.py:573
  446.2 1.1 copy-start.9
  446.2 69.4 %collective-permute-start.10 = (bf16[1,7920,128]{2,1,0:T(8,128)(2,1)}, bf16[1,7920,128]{2,1,0:T(8,128)(2,1)}, u32[]{:S(2)}, u32[]{:S(2)}) collective-permute-start(bf16[1,7920,128]{2,1,0:T(8,128)(2,1)} %partial_map.13), channel_id=1, source_target_pairs={{0,2},{1,3},{2,0},{3,1},{4,6},{5,7},{6,4},{7,5},{8,10},{9,11},{10,... | collective-permute-start | bytes 6082568 | tf_op jit(solution)/shard_map/ppermute | solution.py:573
  453.9 274.0 %collective-permute-start.13 = (bf16[3,7920,128]{2,1,0:T(8,128)(2,1)}, bf16[3,7920,128]{2,1,0:T(8,128)(2,1)}, u32[]{:S(2)}, u32[]{:S(2)}) collective-permute-start(bf16[3,7920,128]{2,1,0:T(8,128)(2,1)} %partial_map.15), channel_id=1, source_target_pairs={{0,2},{1,3},{2,0},{3,1},{4,6},{5,7},{6,4},{7,5},{8,10},{9,11},{10,... | collective-permute-start | bytes 18247688 | tf_op jit(solution)/shard_map/ppermute | solution.py:573
  490.0 91.9 %all-to-all-start.3 = ((bf16[4,20,192,128]{3,2,1,0:T(8,128)(2,1)}), bf16[4,20,192,128]{3,2,1,0:T(8,128)(2,1)}, u32[]{:S(2)}, u32[]{:S(2)}) async-start(bf16[4,20,192,128]{3,2,1,0:T(8,128)(2,1)} %lat_backward.7), calls=%async_computation.3 | async-start | bytes 7864320 | tf_op jit(solution)/shard_map/all_to_all | solution.py:576
  515.6 213.0 %collective-permute-start.11 = (bf16[4,3600,128]{2,1,0:T(8,128)(2,1)}, bf16[4,3600,128]{2,1,0:T(8,128)(2,1)}, u32[]{:S(2)}, u32[]{:S(2)}) collective-permute-start(bf16[4,3600,128]{2,1,0:T(8,128)(2,1)} %partial_map.12), channel_id=1, source_target_pairs={{0,2},{1,3},{2,0},{3,1},{4,6},{5,7},{6,4},{7,5},{8,10},{9,11},{10,... | collective-permute-start | bytes 11059208 | tf_op jit(solution)/shard_map/ppermute | solution.py:573
  581.9 125.9 %all-to-all-start.4 = ((bf16[4,28,192,128]{3,2,1,0:T(8,128)(2,1)}), bf16[4,28,192,128]{3,2,1,0:T(8,128)(2,1)}, u32[]{:S(2)}, u32[]{:S(2)}) async-start(bf16[4,28,192,128]{3,2,1,0:T(8,128)(2,1)} %lat_backward.6), calls=%async_computation.4 | async-start | bytes 11010048 | tf_op jit(solution)/shard_map/all_to_all | solution.py:576
  707.8 74.1 %all-to-all-start.5 = ((bf16[4,16,192,128]{3,2,1,0:T(8,128)(2,1)}), bf16[4,16,192,128]{3,2,1,0:T(8,128)(2,1)S(1)}, u32[]{:S(2)}, u32[]{:S(2)}) async-start(bf16[4,16,192,128]{3,2,1,0:T(8,128)(2,1)} %lat_backward.4), calls=%async_computation.5 | async-start | bytes 6291456 | tf_op jit(solution)/shard_map/all_to_all | solution.py:576
  727.9 82.9 %collective-permute-start.14 = (bf16[4,3600,128]{2,1,0:T(8,128)(2,1)}, bf16[4,3600,128]{2,1,0:T(8,128)(2,1)}, u32[]{:S(2)}, u32[]{:S(2)}) collective-permute-start(bf16[4,3600,128]{2,1,0:T(8,128)(2,1)} %partial_map.14), channel_id=1, source_target_pairs={{0,2},{1,3},{2,0},{3,1},{4,6},{5,7},{6,4},{7,5},{8,10},{9,11},{10,... | collective-permute-start | bytes 11059208 | tf_op jit(solution)/shard_map/ppermute | solution.py:573
  728.6 141.5 %collective-permute-start.15 = (bf16[3,3600,128]{2,1,0:T(8,128)(2,1)}, bf16[3,3600,128]{2,1,0:T(8,128)(2,1)}, u32[]{:S(2)}, u32[]{:S(2)}) collective-permute-start(bf16[3,3600,128]{2,1,0:T(8,128)(2,1)} %partial_map.16), channel_id=1, source_target_pairs={{0,2},{1,3},{2,0},{3,1},{4,6},{5,7},{6,4},{7,5},{8,10},{9,11},{10,... | collective-permute-start | bytes 8294408 | tf_op jit(solution)/shard_map/ppermute | solution.py:573
  738.4 150.8 %collective-permute-start.16 = (bf16[1,3600,128]{2,1,0:T(8,128)(2,1)}, bf16[1,3600,128]{2,1,0:T(8,128)(2,1)}, u32[]{:S(2)}, u32[]{:S(2)}) collective-permute-start(bf16[1,3600,128]{2,1,0:T(8,128)(2,1)} %partial_map.17), channel_id=1, source_target_pairs={{0,2},{1,3},{2,0},{3,1},{4,6},{5,7},{6,4},{7,5},{8,10},{9,11},{10,... | collective-permute-start | bytes 2764808 | tf_op jit(solution)/shard_map/ppermute | solution.py:573
  781.9 1.7 copy-start

commit v4 on v3

--- a/solution.py
+++ b/solution.py
@@ -119,7 +119,7 @@
     return jnp.asarray(value.reshape(LAT, 2 * KPAD).astype(ml_dtypes.bfloat16))
 
 
-MAP_COST = [0, 0, 120, 0, 0]
+MAP_COST = [0, 0, 0, 120, 0, 0]
 CARRIED_COST = [120, 120, 40, 40]
 CARRY = 20
 LAT_COST = 150
@@ -411,7 +411,6 @@
             [tail[q * size : (q + 1) * size] for q in range(group)], axis=1
         ).astype(BF16)
 
-    sib_start = start if sibling.shape[1] == field.shape[1] else 0
     return call(
         kernel,
         "partial_map",
@@ -419,7 +418,7 @@
         grid=(steps,),
         in_specs=[
             pl.BlockSpec((chans, ROWS, LON), lambda i: (0, start + i, 0)),
-            pl.BlockSpec((chans, ROWS, LON), lambda i: (0, sib_start + i, 0)),
+            pl.BlockSpec((chans, ROWS, LON), lambda i: (0, start + i, 0)),
             const_spec(kron.shape),
         ]
         + (
@@ -556,7 +555,7 @@
 def row_plan(total):
     unit = total // 12
     last = total - 11 * unit
-    return [2 * unit, 3 * unit, 3 * unit, 3 * unit, last], [4 * unit, 4 * unit, 3 * unit, last]
+    return [unit, unit, 3 * unit, 3 * unit, 3 * unit, last], [4 * unit, 4 * unit, 3 * unit, last]
 
 
 def tiled_body(state_field, spectral_weight, mode_gain, bypass_weight):
@@ -578,7 +577,7 @@
     plan, carried_plan = row_plan(rows // ROWS)
     plain = chans - CARRY
 
-    near_first = to_near(lax.slice_in_dim(state_field, 0, plan[0] * ROWS, axis=1))
+    near_first = to_near(lax.slice_in_dim(state_field, 0, sum(plan[:2]) * ROWS, axis=1))
 
     def rows_of(index):
         return lax.dynamic_slice_in_dim(bypass_weight, index * chans, chans, 0)
@@ -593,7 +592,7 @@
 
     def partial_rows(*others):
         i = len(sent)
-        sibling = near_field if i else near_first
+        sibling = near_field if i > 1 else near_first
         kron = after(kron_far, *others)
         sent.append(partial_map(state_field, sibling, kron, sum(plan[:i]), plan[i], MAP_COST[i]))
 
@@ -610,27 +609,29 @@
     send_rows(far_gain)
     bands = [lon_forward(state_field, after(table, sent[0]), 0, half, n_sp)]
     partial_rows(bands[0])
-    send_rows(received[0])
+    send_rows(far_gain)
     partial_rows(sent[1])
-    send_rows(received[1])
-    bands.append(lon_forward(state_field, after(table, sent[2]), half, half, n_sp))
+    send_rows(*received[:2])
+    partial_rows(sent[2])
+    send_rows(received[2])
+    bands.append(lon_forward(state_field, after(table, sent[3]), half, half, n_sp))
     kron_own = kron_map(lax.dynamic_slice_in_dim(chip_rows, ch * chans, chans, 1))
     kron_carried = kron_map(far_columns[:, plain:])
-    middle = plan[0]
-    own = [own_map(state_field, near_field, after(kron_own, sent[2]), 0, middle)]
-    bands[1] = after(bands[1], sent[2], own[0])
+    middle = sum(plan[:2])
+    own = [own_map(state_field, near_field, after(kron_own, sent[3]), 0, middle)]
+    bands[1] = after(bands[1], sent[3], own[0])
     weights = pick_weights(ch, spectral_weight, near_weight)
     carried_gain = after(far_gain, weights)[plain:]
     bands = [across(b) for b in bands]
     spectra = [lat_forward(bands[0], lat)]
-    own.append(own_map(state_field, near_field, after(kron_own, spectra[0]), middle, sum(plan[1:]), OWN_COST))
+    own.append(own_map(state_field, near_field, after(kron_own, spectra[0]), middle, sum(plan[2:]), OWN_COST))
     spectra.append(lat_forward(bands[1], after(lat, own[1], weights, kron_carried, carried_gain)))
     spectra = [s.reshape(2, modes, -1, KPAD) for s in spectra]
     near_spectra = [to_near(s) for s in spectra]
 
     parts = [plain - 16, 16]
     own_mixed, carried, sends = mix(weights, spectra + near_spectra, parts)
-    far_mixed = [to_far(after(s, received[2])) for s in sends]
+    far_mixed = [to_far(after(s, received[3])) for s in sends]
     carried = lat_backward(carried, None, carried_gain, lat, 0, CARRY, n_sp)
     carried = across(carried)
 
@@ -654,7 +655,7 @@
         block = partial_map(
             state_field, near_field, kron_carried, at, steps, CARRIED_COST[i], carried, inverse
         )
-        late.append(to_far(after(block, late[0] if i > 1 else received[4 - i])))
+        late.append(to_far(after(block, late[0] if i > 1 else received[5 - i])))
 
     out = None
     cuts = sorted({sum(p[:i]) for p in (plan, carried_plan) for i in range(len(p) + 1)})

time: 909 us -> 903 us (level)
  waiting for transfers between devices: 378 us -> 360 us
  Pallas kernels: 463 us -> 475 us
    ppermute x12 -> x13, waiting for transfers between devices: 120 us -> 82.4 us  [to_far(): return lax.ppermute(value, 'ch', [(i, i ^ 2) for i in range(n_ch)])]
    all_to_all x6, waiting for transfers between devices: 233 us -> 259 us  [across(): return lax.all_to_all(blocks, 'sp', 0, 0)]
    pallas_call x6 -> x7, Pallas kernels: 83.2 us -> 89.3 us  [finish(): call(kernel, 'finish', grid=(steps,), in_specs=specs, out_specs=pl.BlockS...]
    pallas_call x9 -> x10, Pallas kernels: 158 us -> 163 us  [partial_map(): call(kernel, 'partial_map', cost, grid=(steps,), in_specs=[pl.BlockSpec((...]
  transfers between devices with their start and end apart: 23 -> 24, of which waited for: 17 -> 14; matrix products, arithmetic and copies ran while one was open for 0% -> 0% of each run, Pallas kernels for 50% -> 52%
where the time goes in v4:
time: 903 us; the launch traced here: 896 us
  Pallas kernels  475 us (53%)
  waiting for transfers between devices  360 us (40%)
  starting transfers between devices  45.3 us (5%)
  local copies, waits for them, and re-layouts  14.2 us (2%)
    all_to_all x6, waiting for transfers between devices, across(): return lax.all_to_all(blocks, 'sp', 0, 0)  259 us
    pallas_call x10, Pallas kernels, partial_map(): call(kernel, 'partial_map', cost, grid=(steps,), in_specs=[pl.BlockSpec((...  163 us
    pallas_call x2, Pallas kernels, own_map(): call(kernel, 'own_map', cost, grid=(steps,), in_specs=[rows, rows, const_...  104 us
    pallas_call x7, Pallas kernels, finish(): call(kernel, 'finish', grid=(steps,), in_specs=specs, out_specs=pl.BlockS...  89.3 us
    ppermute x13, waiting for transfers between devices, to_far(): return lax.ppermute(value, 'ch', [(i, i ^ 2) for i in range(n_ch)])  82.4 us
    pallas_call x4, Pallas kernels, lat_backward(): call(kernel, 'lat_backward', cost, grid=(per // step,), in_specs=[pl.Bloc...  32.6 us
    pallas_call x2, Pallas kernels, lon_forward(): call(kernel, 'lon_forward', grid=(count // step,), in_specs=[pl.BlockSpec...  32.3 us
    all_to_all x6, starting transfers between devices, across(): return lax.all_to_all(blocks, 'sp', 0, 0)  29.8 us
  transfers between devices with their start and end apart: 24, of which 14 were waited for; matrix products, arithmetic and copies ran while one was open for 0% of the time, Pallas kernels for 52%

profile of v4, /device:TPU:0, one launch (start us, length us, event | category | flops | bytes accessed | tf_op | source)
XLA Modules:
  0.0 895.6 jit_solution(9757410347880478194)
XLA Ops:
  0.0 6.3 slice.12
  7.5 3.4 kron_map.3.w_ref
  10.9 6.0 collective-permute-done.b_ref
  17.3 2.7 collective-permute-start.2
  20.0 10.6 %partial_map.10 = bf16[1,7920,128]{2,1,0:T(8,128)(2,1)} custom-call(bf16[64,192,1440]{2,1,0:T(8,128)(2,1)} %a_ref.23, bf16[64,32,1440]{2,1,0:T(8,128)(2,1)} %collective-permute-done.b_ref, bf16[704,2048]{1,0:T(8,128)(2,1)} %kron_map.3.w_ref), custom_call_target="tpu_custom_call" | custom-call | flops 1 | bytes 1 | tf_op jit(solution)/shard_map/partial_map/pallas_call | solution.py:414
  30.8 16.1 %lon_forward.2 = bf16[4,32,192,128]{3,2,1,0:T(8,128)(2,1)} custom-call(bf16[64,192,1440]{2,1,0:T(8,128)(2,1)} %a_ref.23, bf16[1440,512]{1,0:T(8,128)(2,1)} %constant.22.clone.t_ref), custom_call_target="tpu_custom_call" | custom-call | flops 1 | bytes 1 | tf_op jit(solution)/shard_map/lon_forward/pallas_call | solution.py:210
  46.9 10.6 %partial_map.11 = bf16[1,7920,128]{2,1,0:T(8,128)(2,1)} custom-call(bf16[64,192,1440]{2,1,0:T(8,128)(2,1)} %a_ref.23, bf16[64,32,1440]{2,1,0:T(8,128)(2,1)} %collective-permute-done.b_ref, bf16[704,2048]{1,0:T(8,128)(2,1)} %kron_map.3.w_ref), custom_call_target="tpu_custom_call" | custom-call | flops 1 | bytes 1 | tf_op jit(solution)/shard_map/partial_map/pallas_call | solution.py:414
  57.6 2.0 collective-permute-start.7
  59.5 4.2 kron_map.4.w_ref
  63.8 5.8 all-to-all-start
  69.5 2.8 collective-permute-done.1.b_ref
  72.4 22.0 %partial_map.12 = bf16[3,7920,128]{2,1,0:T(8,128)(2,1)} custom-call(bf16[64,192,1440]{2,1,0:T(8,128)(2,1)} %a_ref.23, bf16[64,192,1440]{2,1,0:T(8,128)(2,1)} %collective-permute-done.1.b_ref, bf16[704,2048]{1,0:T(8,128)(2,1)} %kron_map.3.w_ref), custom_call_target="tpu_custom_call" | custom-call | flops 1 | bytes 1 | tf_op jit(solution)/shard_map/partial_map/pallas_call | solution.py:414
  94.4 26.1 %collective-permute-done.7.refs_3_ = bf16[1,7920,128]{2,1,0:T(8,128)(2,1)S(1)} collective-permute-done((bf16[1,7920,128]{2,1,0:T(8,128)(2,1)}, bf16[1,7920,128]{2,1,0:T(8,128)(2,1)S(1)}, u32[]{:S(2)}, u32[]{:S(2)}) %collective-permute-start.7) | collective-permute-done | bytes 2027552 | tf_op jit(solution)/shard_map/ppermute | solution.py:572
  120.9 22.4 %partial_map.13 = bf16[3,7920,128]{2,1,0:T(8,128)(2,1)} custom-call(bf16[64,192,1440]{2,1,0:T(8,128)(2,1)} %a_ref.23, bf16[64,192,1440]{2,1,0:T(8,128)(2,1)} %collective-permute-done.1.b_ref, bf16[704,2048]{1,0:T(8,128)(2,1)} %kron_map.3.w_ref), custom_call_target="tpu_custom_call" | custom-call | flops 120000004096 | bytes 1 | tf_op jit(solution)/shard_map/partial_map/pallas_call | solution.py:414
  143.3 16.2 %lon_forward.3 = bf16[4,32,192,128]{3,2,1,0:T(8,128)(2,1)} custom-call(bf16[64,192,1440]{2,1,0:T(8,128)(2,1)} %a_ref.23, bf16[1440,512]{1,0:T(8,128)(2,1)} %constant.22.clone.t_ref), custom_call_target="tpu_custom_call" | custom-call | flops 1 | bytes 1 | tf_op jit(solution)/shard_map/lon_forward/pallas_call | solution.py:210
  159.4 21.8 %own_map.2.refs_0_.refs_1_ = f32[64,32,1440]{2,1,0:T(8,128)} custom-call(bf16[64,192,1440]{2,1,0:T(8,128)(2,1)} %a_ref.23, bf16[64,192,1440]{2,1,0:T(8,128)(2,1)} %collective-permute-done.1.b_ref, bf16[1024,2048]{1,0:T(8,128)(2,1)} %kron_map.4.w_ref), custom_call_target="tpu_custom_call" | custom-call | flops 1 | bytes 1 | tf_op jit(solution)/shard_map/own_map/pallas_call | solution.py:459
  181.3 26.4 %all-to-all-done.x_ref = bf16[4,32,192,128]{3,2,1,0:T(8,128)(2,1)} async-done(((bf16[4,32,192,128]{3,2,1,0:T(8,128)(2,1)}), bf16[4,32,192,128]{3,2,1,0:T(8,128)(2,1)}, u32[]{:S(2)}, u32[]{:S(2)}) %all-to-all-start) | async-done | bytes 6291488 | tf_op jit(solution)/shard_map/all_to_all | solution.py:575
  207.6 5.4 all-to-all-start.1
  213.8 2.5 kron_map.5.w_ref
  216.3 4.2 collective-permute-done.4.b0.b1
  220.5 2.0 copy-done.1
  222.5 6.2 pick_weights.1.w_ref
  228.7 1.4 slice.15.refs_0_
  230.1 9.8 %lat_forward.2 = bf16[128,32,384]{2,1,0:T(8,128)(2,1)} custom-call(bf16[4,32,192,128]{3,2,1,0:T(8,128)(2,1)} %all-to-all-done.x_ref, bf16[768,768]{1,0:T(8,128)(2,1)} %constant.24.clone.t_ref.refs_2_.refs_1_), custom_call_target="tpu_custom_call" | custom-call | flops 1 | bytes 1 | tf_op jit(solution)/shard_map/lat_forward/pallas_call | solution.py:240
  240.0 13.1 %collective-permute-done.8.refs_3_ = bf16[3,7920,128]{2,1,0:T(8,128)(2,1)} collective-permute-done((bf16[3,7920,128]{2,1,0:T(8,128)(2,1)}, bf16[3,7920,128]{2,1,0:T(8,128)(2,1)}, u32[]{:S(2)}, u32[]{:S(2)}) %collective-permute-start.8) | collective-permute-done | bytes 6082592 | tf_op jit(solution)/shard_map/ppermute | solution.py:572
  253.8 82.4 %own_map.3.refs_1_ = f32[64,160,1440]{2,1,0:T(8,128)} custom-call(bf16[64,192,1440]{2,1,0:T(8,128)(2,1)} %a_ref.23, bf16[64,192,1440]{2,1,0:T(8,128)(2,1)} %collective-permute-done.1.b_ref, bf16[1024,2048]{1,0:T(8,128)(2,1)} %kron_map.4.w_ref), custom_call_target="tpu_custom_call" | custom-call | flops 49999998976 | bytes 1 | tf_op jit(solution)/shard_map/own_map/pallas_call | solution.py:459
  336.1 14.5 %all-to-all-done.1.x_ref = bf16[4,32,192,128]{3,2,1,0:T(8,128)(2,1)} async-done(((bf16[4,32,192,128]{3,2,1,0:T(8,128)(2,1)}), bf16[4,32,192,128]{3,2,1,0:T(8,128)(2,1)}, u32[]{:S(2)}, u32[]{:S(2)}) %all-to-all-start.1) | async-done | bytes 6291488 | tf_op jit(solution)/shard_map/all_to_all | solution.py:575
  350.6 9.8 %lat_forward.3 = bf16[128,32,384]{2,1,0:T(8,128)(2,1)} custom-call(bf16[4,32,192,128]{3,2,1,0:T(8,128)(2,1)} %all-to-all-done.1.x_ref, bf16[768,768]{1,0:T(8,128)(2,1)} %constant.24.clone.t_ref.refs_2_.refs_1_), custom_call_target="tpu_custom_call" | custom-call | flops 1 | bytes 1 | tf_op jit(solution)/shard_map/lat_forward/pallas_call | solution.py:240
  360.4 5.9 collective-permute-done.6.refs_3_
  366.2 1.6 copy-done.3
  367.9 17.4 %mix.1 = (f32[2,64,64,384]{3,2,1,0:T(8,128)}, f32[2,20,64,384]{3,2,1,0:T(8,128)}, bf16[5,28,64,128]{3,2,1,0:T(8,128)(2,1)}, bf16[5,16,64,128]{3,2,1,0:T(8,128)(2,1)}) custom-call(bf16[2,64,128,128]{3,2,1,0:T(8,128)(2,1)} %pick_weights.1.w_ref, bf16[2,64,32,384]{3,2,1,0:T(8,128)(2,1)} %bitcast.5, bf16[2,64,32,384]{3,2,1,0:T(8,128)(2,1)} %bitcast.7, ...), custom_call_target="tpu_custom_call" | custom-call | flops 1 | bytes 1 | tf_op jit(solution)/shard_map/mix/pallas_call | solution.py:293
  385.9 7.8 lat_backward.5
  393.7 4.8 all-to-all-start.2
  398.5 1.6 collective-permute-start.13
  400.0 7.7 lat_backward.7
  407.8 10.7 %partial_map.15 = bf16[1,7920,128]{2,1,0:T(8,128)(2,1)} custom-call(bf16[64,192,1440]{2,1,0:T(8,128)(2,1)} %a_ref.23, bf16[64,192,1440]{2,1,0:T(8,128)(2,1)} %collective-permute-done.1.b_ref, bf16[704,2048]{1,0:T(8,128)(2,1)} %kron_map.3.w_ref), custom_call_target="tpu_custom_call" | custom-call | flops 1 | bytes 1 | tf_op jit(solution)/shard_map/partial_map/pallas_call | solution.py:414
  418.4 22.0 %partial_map.17 = bf16[3,7920,128]{2,1,0:T(8,128)(2,1)} custom-call(bf16[64,192,1440]{2,1,0:T(8,128)(2,1)} %a_ref.23, bf16[64,192,1440]{2,1,0:T(8,128)(2,1)} %collective-permute-done.1.b_ref, bf16[704,2048]{1,0:T(8,128)(2,1)} %kron_map.3.w_ref), custom_call_target="tpu_custom_call" | custom-call | flops 1 | bytes 1 | tf_op jit(solution)/shard_map/partial_map/pallas_call | solution.py:414
  441.5 6.7 lat_backward.4
  448.2 1.0 collective-permute-start.14
  449.2 17.2 %collective-permute-done.13.refs_0_ = bf16[5,28,64,128]{3,2,1,0:T(8,128)(2,1)} collective-permute-done((bf16[5,28,64,128]{3,2,1,0:T(8,128)(2,1)}, bf16[5,28,64,128]{3,2,1,0:T(8,128)(2,1)}, u32[]{:S(2)}, u32[]{:S(2)}) %collective-permute-start.13) | collective-permute-done | bytes 2293792 | tf_op jit(solution)/shard_map/ppermute | solution.py:572
  466.4 10.5 %lat_backward.6 = bf16[4,28,192,128]{3,2,1,0:T(8,128)(2,1)} custom-call(f32[2,64,64,384]{3,2,1,0:T(8,128)} %get-tuple-element.51.own_ref, bf16[5,28,64,128]{3,2,1,0:T(8,128)(2,1)} %collective-permute-done.13.refs_0_, f32[64,1,384]{2,1,0:T(1,128)} %copy-done.5, bf16[768,768]{1,0:T(8,128)(2,1)} %constant.24.clone.t_ref.refs_2_.refs_1_), custom_call_target="tpu_custom_call" | custom-call | flops 1 | bytes 1 | tf_op jit(solution)/shard_map/lat_backward/pallas_call | solution.py:347
  476.9 9.5 %all-to-all-done.2.refs_0_ = bf16[4,20,192,128]{3,2,1,0:T(8,128)(2,1)} async-done(((bf16[4,20,192,128]{3,2,1,0:T(8,128)(2,1)}), bf16[4,20,192,128]{3,2,1,0:T(8,128)(2,1)}, u32[]{:S(2)}, u32[]{:S(2)}) %all-to-all-start.2) | async-done | bytes 3932192 | tf_op jit(solution)/shard_map/all_to_all | solution.py:575
  486.4 4.8 all-to-all-start.3
  491.2 19.9 %partial_map.14 = bf16[4,3600,128]{2,1,0:T(8,128)(2,1)} custom-call(bf16[64,192,1440]{2,1,0:T(8,128)(2,1)} %a_ref.23, bf16[64,192,1440]{2,1,0:T(8,128)(2,1)} %collective-permute-done.1.b_ref, bf16[320,2048]{1,0:T(8,128)(2,1)} %kron_map.5.w_ref, bf16[4,20,192,128]{3,2,1,0:T(8,128)(2,1)} %all-to-all-done.2.refs_0_, ...), custom_call_target="tpu_custom_call" | custom-call | flops 120000004096 | bytes 1 | tf_op jit(solution)/shard_map/partial_map/pallas_call | solution.py:414
  511.1 1.5 collective-permute-start.12
  512.5 65.8 %all-to-all-done.3.refs_6_.refs_7_ = bf16[4,20,192,128]{3,2,1,0:T(8,128)(2,1)} async-done(((bf16[4,20,192,128]{3,2,1,0:T(8,128)(2,1)}), bf16[4,20,192,128]{3,2,1,0:T(8,128)(2,1)}, u32[]{:S(2)}, u32[]{:S(2)}) %all-to-all-start.3) | async-done | bytes 3932192 | tf_op jit(solution)/shard_map/all_to_all | solution.py:575
  578.3 5.1 all-to-all-start.4
  583.4 19.9 %partial_map.16 = bf16[4,3600,128]{2,1,0:T(8,128)(2,1)} custom-call(bf16[64,192,1440]{2,1,0:T(8,128)(2,1)} %a_ref.23, bf16[64,192,1440]{2,1,0:T(8,128)(2,1)} %collective-permute-done.1.b_ref, bf16[320,2048]{1,0:T(8,128)(2,1)} %kron_map.5.w_ref, bf16[4,20,192,128]{3,2,1,0:T(8,128)(2,1)} %all-to-all-done.2.refs_0_, ...), custom_call_target="tpu_custom_call" | custom-call | flops 120000004096 | bytes 1 | tf_op jit(solution)/shard_map/partial_map/pallas_call | solution.py:414
  603.3 100.8 %all-to-all-done.4.refs_4_.refs_5_ = bf16[4,28,192,128]{3,2,1,0:T(8,128)(2,1)} async-done(((bf16[4,28,192,128]{3,2,1,0:T(8,128)(2,1)}), bf16[4,28,192,128]{3,2,1,0:T(8,128)(2,1)}, u32[]{:S(2)}, u32[]{:S(2)}) %all-to-all-start.4) | async-done | bytes 5505056 | tf_op jit(solution)/shard_map/all_to_all | solution.py:575
  704.2 4.0 all-to-all-start.5
  708.1 16.1 %partial_map.18 = bf16[3,3600,128]{2,1,0:T(8,128)(2,1)} custom-call(bf16[64,192,1440]{2,1,0:T(8,128)(2,1)} %a_ref.23, bf16[64,192,1440]{2,1,0:T(8,128)(2,1)} %collective-permute-done.1.b_ref, bf16[320,2048]{1,0:T(8,128)(2,1)} %kron_map.5.w_ref, bf16[4,20,192,128]{3,2,1,0:T(8,128)(2,1)} %all-to-all-done.2.refs_0_, ...), custom_call_target="tpu_custom_call" | custom-call | flops 40000000000 | bytes 1 | tf_op jit(solution)/shard_map/partial_map/pallas_call | solution.py:414
  724.2 1.5 collective-permute-start.15
  726.3 8.5 partial_map.19
  734.8 1.5 collective-permute-start.17
  736.3 42.0 %all-to-all-done.5.refs_5_.refs_6_ = bf16[4,16,192,128]{3,2,1,0:T(8,128)(2,1)S(1)} async-done(((bf16[4,16,192,128]{3,2,1,0:T(8,128)(2,1)}), bf16[4,16,192,128]{3,2,1,0:T(8,128)(2,1)S(1)}, u32[]{:S(2)}, u32[]{:S(2)}) %all-to-all-start.5) | async-done | bytes 3145760 | tf_op jit(solution)/shard_map/all_to_all | solution.py:575
  778.3 1.6 copy-done
  779.9 9.4 %finish.7.refs_0_ = bf16[64,192,1440]{2,1,0:T(8,128)(2,1)} custom-call(f32[64,32,1440]{2,1,0:T(8,128)} %own_map.2.refs_0_.refs_1_, bf16[512,1440]{1,0:T(8,128)(2,1)} %constant.23.clone.refs_1_.refs_2_, bf16[1,7920,128]{2,1,0:T(8,128)(2,1)} %collective-permute-done.3.refs_2_, bf16[4,3600,128]{2,1,0:T(8,128)(2,1)} %collective-permute-done.12.refs_3_.refs_4_, ...), custom_call_target="tpu_custom_call" | custom-call | flops 1 | bytes 1 | tf_op jit(solution)/shard_map/finish/pallas_call | solution.py:539
  789.3 9.4 %finish.8.refs_0_ = bf16[64,192,1440]{2,1,0:T(8,128)(2,1)} custom-call(bf16[64,192,1440]{2,1,0:T(8,128)(2,1)} %finish.7.refs_0_, f32[64,32,1440]{2,1,0:T(8,128)} %own_map.2.refs_0_.refs_1_, bf16[512,1440]{1,0:T(8,128)(2,1)} %constant.23.clone.refs_1_.refs_2_, bf16[1,7920,128]{2,1,0:T(8,128)(2,1)} %copy-done.4, ...), custom_call_target="tpu_custom_call", output_to_operand_aliasing={{}: (0, {})} | custom-call | flops 1 | bytes 1 | tf_op jit(solution)/shard_map/finish/pallas_call | solution.py:539
  798.7 13.0 %finish.9.refs_0_ = bf16[64,192,1440]{2,1,0:T(8,128)(2,1)} custom-call(bf16[64,192,1440]{2,1,0:T(8,128)(2,1)} %finish.8.refs_0_, f32[64,160,1440]{2,1,0:T(8,128)} %own_map.3.refs_1_, bf16[512,1440]{1,0:T(8,128)(2,1)} %constant.23.clone.refs_1_.refs_2_, bf16[3,7920,128]{2,1,0:T(8,128)(2,1)} %collective-permute-done.8.refs_3_, ...), custom_call_target="tpu_custom_call", output_to_operand_aliasing={{}: (0, {})} | custom-call | flops 1 | bytes 1 | tf_op jit(solution)/shard_map/finish/pallas_call | solution.py:539
  811.7 9.6 %finish.10.refs_0_ = bf16[64,192,1440]{2,1,0:T(8,128)(2,1)} custom-call(bf16[64,192,1440]{2,1,0:T(8,128)(2,1)} %finish.9.refs_0_, f32[64,160,1440]{2,1,0:T(8,128)} %own_map.3.refs_1_, bf16[512,1440]{1,0:T(8,128)(2,1)} %constant.23.clone.refs_1_.refs_2_, bf16[3,7920,128]{2,1,0:T(8,128)(2,1)} %collective-permute-done.8.refs_3_, ...), custom_call_target="tpu_custom_call", output_to_operand_aliasing={{}: (0, {})} | custom-call | flops 1 | bytes 1 | tf_op jit(solution)/shard_map/finish/pallas_call | solution.py:539
  821.3 19.2 %finish.11.refs_0_ = bf16[64,192,1440]{2,1,0:T(8,128)(2,1)} custom-call(bf16[64,192,1440]{2,1,0:T(8,128)(2,1)} %finish.10.refs_0_, f32[64,160,1440]{2,1,0:T(8,128)} %own_map.3.refs_1_, bf16[512,1440]{1,0:T(8,128)(2,1)} %constant.23.clone.refs_1_.refs_2_, bf16[3,7920,128]{2,1,0:T(8,128)(2,1)} %collective-permute-done.9.refs_3_, ...), custom_call_target="tpu_custom_call", output_to_operand_aliasing={{}: (0, {})} | custom-call | flops 1 | bytes 1 | tf_op jit(solution)/shard_map/finish/pallas_call | solution.py:539
  840.5 25.9 %collective-permute-done.16.refs_4_ = bf16[3,3600,128]{2,1,0:T(8,128)(2,1)} collective-permute-done((bf16[3,3600,128]{2,1,0:T(8,128)(2,1)}, bf16[3,3600,128]{2,1,0:T(8,128)(2,1)}, u32[]{:S(2)}, u32[]{:S(2)}) %collective-permute-start.16) | collective-permute-done | bytes 2764832 | tf_op jit(solution)/shard_map/ppermute | solution.py:572
  866.4 19.2 %finish.12.refs_0_ = bf16[64,192,1440]{2,1,0:T(8,128)(2,1)} custom-call(bf16[64,192,1440]{2,1,0:T(8,128)(2,1)} %finish.11.refs_0_, f32[64,160,1440]{2,1,0:T(8,128)} %own_map.3.refs_1_, bf16[512,1440]{1,0:T(8,128)(2,1)} %constant.23.clone.refs_1_.refs_2_, bf16[3,7920,128]{2,1,0:T(8,128)(2,1)} %collective-permute-done.14.refs_3_, ...), custom_call_target="tpu_custom_call", output_to_operand_aliasing={{}: (0, {})} | custom-call | flops 1 | bytes 1 | tf_op jit(solution)/shard_map/finish/pallas_call | solution.py:539
  885.6 9.5 %finish.13 = bf16[64,192,1440]{2,1,0:T(8,128)(2,1)} custom-call(bf16[64,192,1440]{2,1,0:T(8,128)(2,1)} %finish.12.refs_0_, f32[64,160,1440]{2,1,0:T(8,128)} %own_map.3.refs_1_, bf16[512,1440]{1,0:T(8,128)(2,1)} %constant.23.clone.refs_1_.refs_2_, bf16[1,7920,128]{2,1,0:T(8,128)(2,1)} %collective-permute-done.11.refs_3_, ...), custom_call_target="tpu_custom_call", output_to_operand_aliasing={{}: (0, {})} | custom-call | flops 1 | bytes 1 | tf_op jit(solution)/shard_map/finish/pallas_call | solution.py:539
  (45 shorter events, 5.8 us)
Async XLA Ops:
  0.0 6.7 copy-start.8
  0.0 17.2 %copy-start.7 = (f32[64,320]{1,0:T(8,128)S(1)}, f32[64,320]{1,0:T(8,128)}, u32[]{:S(2)}) copy-start(f32[64,320]{1,0:T(8,128)} %param.9) | copy-start | bytes 245764
  6.3 10.6 %collective-permute-start = (bf16[64,32,1440]{2,1,0:T(8,128)(2,1)}, bf16[64,32,1440]{2,1,0:T(8,128)(2,1)}, u32[]{:S(2)}, u32[]{:S(2)}) collective-permute-start(bf16[64,32,1440]{2,1,0:T(8,128)(2,1)} %slice.12), channel_id=1, source_target_pairs={{0,1},{1,0},{2,3},{3,2},{4,5},{5,4},{6,7},{7,6},{8,9},{9,8},{10,11... | collective-permute-start | bytes 17694728 | tf_op jit(solution)/shard_map/ppermute | solution.py:569
  16.9 55.5 %collective-permute-start.1 = (bf16[64,192,1440]{2,1,0:T(8,128)(2,1)}, bf16[64,192,1440]{2,1,0:T(8,128)(2,1)}, u32[]{:S(2)}, u32[]{:S(2)}) collective-permute-start(bf16[64,192,1440]{2,1,0:T(8,128)(2,1)} %a_ref.23), channel_id=1, source_target_pairs={{0,1},{1,0},{2,3},{3,2},{4,5},{5,4},{6,7},{7,6},{8,9},{9,8},{10,11... | collective-permute-start | bytes 106168328 | tf_op jit(solution)/shard_map/ppermute | solution.py:569
  17.3 13.4 %copy-start.5 = (f32[64,1,384]{2,1,0:T(1,128)}, f32[64,1,384]{2,1,0:T(1,128)S(1)}, u32[]{:S(2)}) copy-start(f32[64,1,384]{2,1,0:T(1,128)S(1)} %reshape.12.refs_1_.refs_0_) | copy-start | bytes 294916
  17.3 13.4 %collective-permute-start.2 = (f32[64,1,384]{2,1,0:T(1,128)S(1)}, f32[64,1,384]{2,1,0:T(1,128)S(1)}, u32[]{:S(2)}, u32[]{:S(2)}) collective-permute-start(f32[64,1,384]{2,1,0:T(1,128)S(1)} %reshape.12.refs_1_.refs_0_), channel_id=1, source_target_pairs={{0,2},{1,3},{2,0},{3,1},{4,6},{5,7},{6,4},{7,5},{8,10},{9,11},{10,... | collective-permute-start | bytes 294920 | tf_op jit(solution)/shard_map/ppermute | solution.py:572
  30.7 16.2 %copy-start.9 = (f32[64,1,384]{2,1,0:T(1,128)}, f32[64,1,384]{2,1,0:T(1,128)S(1)}, u32[]{:S(2)}) copy-start(f32[64,1,384]{2,1,0:T(1,128)S(1)} %collective-permute-done.2) | copy-start | bytes 294916
  30.7 63.7 %collective-permute-start.3 = (bf16[1,7920,128]{2,1,0:T(8,128)(2,1)}, bf16[1,7920,128]{2,1,0:T(8,128)(2,1)}, u32[]{:S(2)}, u32[]{:S(2)}) collective-permute-start(bf16[1,7920,128]{2,1,0:T(8,128)(2,1)} %partial_map.10), channel_id=1, source_target_pairs={{0,2},{1,3},{2,0},{3,1},{4,6},{5,7},{6,4},{7,5},{8,10},{9,11},{10,... | collective-permute-start | bytes 6082568 | tf_op jit(solution)/shard_map/ppermute | solution.py:572
  57.6 63.0 %collective-permute-start.7 = (bf16[1,7920,128]{2,1,0:T(8,128)(2,1)}, bf16[1,7920,128]{2,1,0:T(8,128)(2,1)S(1)}, u32[]{:S(2)}, u32[]{:S(2)}) collective-permute-start(bf16[1,7920,128]{2,1,0:T(8,128)(2,1)} %partial_map.11), channel_id=1, source_target_pairs={{0,2},{1,3},{2,0},{3,1},{4,6},{5,7},{6,4},{7,5},{8,10},{9,11},{10,... | collective-permute-start | bytes 6082568 | tf_op jit(solution)/shard_map/ppermute | solution.py:572
  63.8 143.9 %all-to-all-start = ((bf16[4,32,192,128]{3,2,1,0:T(8,128)(2,1)}), bf16[4,32,192,128]{3,2,1,0:T(8,128)(2,1)}, u32[]{:S(2)}, u32[]{:S(2)}) async-start(bf16[4,32,192,128]{3,2,1,0:T(8,128)(2,1)} %lon_forward.2), calls=%async_computation | async-start | bytes 12582912 | tf_op jit(solution)/shard_map/all_to_all | solution.py:575
  120.6 22.7 %copy-start.4 = (bf16[1,7920,128]{2,1,0:T(8,128)(2,1)}, bf16[1,7920,128]{2,1,0:T(8,128)(2,1)S(1)}, u32[]{:S(2)}) copy-start(bf16[1,7920,128]{2,1,0:T(8,128)(2,1)S(1)} %collective-permute-done.7.refs_3_) | copy-start | bytes 6082564
  120.6 132.6 %collective-permute-start.8 = (bf16[3,7920,128]{2,1,0:T(8,128)(2,1)}, bf16[3,7920,128]{2,1,0:T(8,128)(2,1)}, u32[]{:S(2)}, u32[]{:S(2)}) collective-permute-start(bf16[3,7920,128]{2,1,0:T(8,128)(2,1)} %partial_map.12), channel_id=1, source_target_pairs={{0,2},{1,3},{2,0},{3,1},{4,6},{5,7},{6,4},{7,5},{8,10},{9,11},{10,... | collective-permute-start | bytes 18247688 | tf_op jit(solution)/shard_map/ppermute | solution.py:572
  181.3 31.9 %copy-start.6 = (bf16[128,64]{1,0:T(8,128)(2,1)S(1)}, bf16[128,64]{1,0:T(8,128)(2,1)}, u32[]{:S(2)}) copy-start(bf16[128,64]{1,0:T(8,128)(2,1)} %get-tuple-element.74) | copy-start | bytes 49156
  207.6 143.0 %all-to-all-start.1 = ((bf16[4,32,192,128]{3,2,1,0:T(8,128)(2,1)}), bf16[4,32,192,128]{3,2,1,0:T(8,128)(2,1)}, u32[]{:S(2)}, u32[]{:S(2)}) async-start(bf16[4,32,192,128]{3,2,1,0:T(8,128)(2,1)} %lon_forward.3), calls=%async_computation.1 | async-start | bytes 12582912 | tf_op jit(solution)/shard_map/all_to_all | solution.py:575
  213.0 7.4 collective-permute-start.4
  220.5 2.0 copy-start.1
  239.9 120.5 %collective-permute-start.5 = (bf16[2,64,32,384]{3,2,1,0:T(8,128)(2,1)}, bf16[2,64,32,384]{3,2,1,0:T(8,128)(2,1)S(1)}, u32[]{:S(2)}, u32[]{:S(2)}) collective-permute-start(bf16[2,64,32,384]{3,2,1,0:T(8,128)(2,1)} %bitcast.4), channel_id=1, source_target_pairs={{0,1},{1,0},{2,3},{3,2},{4,5},{5,4},{6,7},{7,6},{8,9},{9,8},{10,11... | collective-permute-start | bytes 9437192 | tf_op jit(solution)/shard_map/ppermute | solution.py:569
  253.2 132.1 %collective-permute-start.9 = (bf16[3,7920,128]{2,1,0:T(8,128)(2,1)}, bf16[3,7920,128]{2,1,0:T(8,128)(2,1)}, u32[]{:S(2)}, u32[]{:S(2)}) collective-permute-start(bf16[3,7920,128]{2,1,0:T(8,128)(2,1)} %partial_map.13), channel_id=1, source_target_pairs={{0,2},{1,3},{2,0},{3,1},{4,6},{5,7},{6,4},{7,5},{8,10},{9,11},{10,... | collective-permute-start | bytes 18247688 | tf_op jit(solution)/shard_map/ppermute | solution.py:572
  360.4 5.9 collective-permute-start.6
  360.4 5.9 copy-start.2
  366.2 1.6 copy-start.3
  385.3 55.2 %collective-permute-start.10 = (bf16[5,16,64,128]{3,2,1,0:T(8,128)(2,1)}, bf16[5,16,64,128]{3,2,1,0:T(8,128)(2,1)S(1)}, u32[]{:S(2)}, u32[]{:S(2)}) collective-permute-start(bf16[5,16,64,128]{3,2,1,0:T(8,128)(2,1)} %get-tuple-element.56), channel_id=1, source_target_pairs={{0,2},{1,3},{2,0},{3,1},{4,6},{5,7},{6,4},{7,5},{8,10},{9,11},{10,... | collective-permute-start | bytes 3932168 | tf_op jit(solution)/shard_map/ppermute | solution.py:572
  393.7 92.7 %all-to-all-start.2 = ((bf16[4,20,192,128]{3,2,1,0:T(8,128)(2,1)}), bf16[4,20,192,128]{3,2,1,0:T(8,128)(2,1)}, u32[]{:S(2)}, u32[]{:S(2)}) async-start(bf16[4,20,192,128]{3,2,1,0:T(8,128)(2,1)} %lat_backward.5), calls=%async_computation.2 | async-start | bytes 7864320 | tf_op jit(solution)/shard_map/all_to_all | solution.py:575
  398.5 68.0 %collective-permute-start.13 = (bf16[5,28,64,128]{3,2,1,0:T(8,128)(2,1)}, bf16[5,28,64,128]{3,2,1,0:T(8,128)(2,1)}, u32[]{:S(2)}, u32[]{:S(2)}) collective-permute-start(bf16[5,28,64,128]{3,2,1,0:T(8,128)(2,1)} %get-tuple-element.63), channel_id=1, source_target_pairs={{0,2},{1,3},{2,0},{3,1},{4,6},{5,7},{6,4},{7,5},{8,10},{9,11},{10,... | collective-permute-start | bytes 6881288 | tf_op jit(solution)/shard_map/ppermute | solution.py:572
  440.5 1.1 copy-start.10
  440.5 70.6 %collective-permute-start.11 = (bf16[1,7920,128]{2,1,0:T(8,128)(2,1)}, bf16[1,7920,128]{2,1,0:T(8,128)(2,1)}, u32[]{:S(2)}, u32[]{:S(2)}) collective-permute-start(bf16[1,7920,128]{2,1,0:T(8,128)(2,1)} %partial_map.15), channel_id=1, source_target_pairs={{0,2},{1,3},{2,0},{3,1},{4,6},{5,7},{6,4},{7,5},{8,10},{9,11},{10,... | collective-permute-start | bytes 6082568 | tf_op jit(solution)/shard_map/ppermute | solution.py:572
  448.2 276.0 %collective-permute-start.14 = (bf16[3,7920,128]{2,1,0:T(8,128)(2,1)}, bf16[3,7920,128]{2,1,0:T(8,128)(2,1)}, u32[]{:S(2)}, u32[]{:S(2)}) collective-permute-start(bf16[3,7920,128]{2,1,0:T(8,128)(2,1)} %partial_map.17), channel_id=1, source_target_pairs={{0,2},{1,3},{2,0},{3,1},{4,6},{5,7},{6,4},{7,5},{8,10},{9,11},{10,... | collective-permute-start | bytes 18247688 | tf_op jit(solution)/shard_map/ppermute | solution.py:572
  486.4 92.0 %all-to-all-start.3 = ((bf16[4,20,192,128]{3,2,1,0:T(8,128)(2,1)}), bf16[4,20,192,128]{3,2,1,0:T(8,128)(2,1)}, u32[]{:S(2)}, u32[]{:S(2)}) async-start(bf16[4,20,192,128]{3,2,1,0:T(8,128)(2,1)} %lat_backward.7), calls=%async_computation.3 | async-start | bytes 7864320 | tf_op jit(solution)/shard_map/all_to_all | solution.py:575
  511.1 214.6 %collective-permute-start.12 = (bf16[4,3600,128]{2,1,0:T(8,128)(2,1)}, bf16[4,3600,128]{2,1,0:T(8,128)(2,1)}, u32[]{:S(2)}, u32[]{:S(2)}) collective-permute-start(bf16[4,3600,128]{2,1,0:T(8,128)(2,1)} %partial_map.14), channel_id=1, source_target_pairs={{0,2},{1,3},{2,0},{3,1},{4,6},{5,7},{6,4},{7,5},{8,10},{9,11},{10,... | collective-permute-start | bytes 11059208 | tf_op jit(solution)/shard_map/ppermute | solution.py:572
  578.3 125.9 %all-to-all-start.4 = ((bf16[4,28,192,128]{3,2,1,0:T(8,128)(2,1)}), bf16[4,28,192,128]{3,2,1,0:T(8,128)(2,1)}, u32[]{:S(2)}, u32[]{:S(2)}) async-start(bf16[4,28,192,128]{3,2,1,0:T(8,128)(2,1)} %lat_backward.6), calls=%async_computation.4 | async-start | bytes 11010048 | tf_op jit(solution)/shard_map/all_to_all | solution.py:575
  704.2 74.1 %all-to-all-start.5 = ((bf16[4,16,192,128]{3,2,1,0:T(8,128)(2,1)}), bf16[4,16,192,128]{3,2,1,0:T(8,128)(2,1)S(1)}, u32[]{:S(2)}, u32[]{:S(2)}) async-start(bf16[4,16,192,128]{3,2,1,0:T(8,128)(2,1)} %lat_backward.4), calls=%async_computation.5 | async-start | bytes 6291456 | tf_op jit(solution)/shard_map/all_to_all | solution.py:575
  724.2 87.5 %collective-permute-start.15 = (bf16[4,3600,128]{2,1,0:T(8,128)(2,1)}, bf16[4,3600,128]{2,1,0:T(8,128)(2,1)}, u32[]{:S(2)}, u32[]{:S(2)}) collective-permute-start(bf16[4,3600,128]{2,1,0:T(8,128)(2,1)} %partial_map.16), channel_id=1, source_target_pairs={{0,2},{1,3},{2,0},{3,1},{4,6},{5,7},{6,4},{7,5},{8,10},{9,11},{10,... | collective-permute-start | bytes 11059208 | tf_op jit(solution)/shard_map/ppermute | solution.py:572
  725.7 140.7 %collective-permute-start.16 = (bf16[3,3600,128]{2,1,0:T(8,128)(2,1)}, bf16[3,3600,128]{2,1,0:T(8,128)(2,1)}, u32[]{:S(2)}, u32[]{:S(2)}) collective-permute-start(bf16[3,3600,128]{2,1,0:T(8,128)(2,1)} %partial_map.18), channel_id=1, source_target_pairs={{0,2},{1,3},{2,0},{3,1},{4,6},{5,7},{6,4},{7,5},{8,10},{9,11},{10,... | collective-permute-start | bytes 8294408 | tf_op jit(solution)/shard_map/ppermute | solution.py:572
  734.8 150.8 %collective-permute-start.17 = (bf16[1,3600,128]{2,1,0:T(8,128)(2,1)}, bf16[1,3600,128]{2,1,0:T(8,128)(2,1)}, u32[]{:S(2)}, u32[]{:S(2)}) collective-permute-start(bf16[1,3600,128]{2,1,0:T(8,128)(2,1)} %partial_map.19), channel_id=1, source_target_pairs={{0,2},{1,3},{2,0},{3,1},{4,6},{5,7},{6,4},{7,5},{8,10},{9,11},{10,... | collective-permute-start | bytes 2764808 | tf_op jit(solution)/shard_map/ppermute | solution.py:572
  778.3 1.6 copy-start

commit v5 on v4

--- a/solution.py
+++ b/solution.py
@@ -615,7 +615,8 @@
     partial_rows(sent[2])
     send_rows(received[2])
     bands.append(lon_forward(state_field, after(table, sent[3]), half, half, n_sp))
-    kron_own = kron_map(lax.dynamic_slice_in_dim(chip_rows, ch * chans, chans, 1))
+    own_columns = lax.dynamic_slice_in_dim(chip_rows, ch * chans, chans, 1)
+    kron_own = kron_map(after(own_columns, sent[3]))
     kron_carried = kron_map(far_columns[:, plain:])
     middle = sum(plan[:2])
     own = [own_map(state_field, near_field, after(kron_own, sent[3]), 0, middle)]

time: 903 us -> 899 us (level)
    all_to_all x6, waiting for transfers between devices: 259 us -> 245 us  [across(): return lax.all_to_all(blocks, 'sp', 0, 0)]
  transfers between devices with their start and end apart: 24 -> 24, of which waited for: 14 -> 16; matrix products, arithmetic and copies ran while one was open for 0% -> 0% of each run, Pallas kernels for 52% -> 52%
where the time goes in v5:
time: 899 us; the launch traced here: 893 us
  Pallas kernels  474 us (53%)
  waiting for transfers between devices  359 us (40%)
  starting transfers between devices  44.3 us (5%)
  local copies, waits for them, and re-layouts  13.9 us (2%)
    all_to_all x6, waiting for transfers between devices, across(): return lax.all_to_all(blocks, 'sp', 0, 0)  245 us
    pallas_call x10, Pallas kernels, partial_map(): call(kernel, 'partial_map', cost, grid=(steps,), in_specs=[pl.BlockSpec((...  163 us
    pallas_call x2, Pallas kernels, own_map(): call(kernel, 'own_map', cost, grid=(steps,), in_specs=[rows, rows, const_...  104 us
    ppermute x13, waiting for transfers between devices, to_far(): return lax.ppermute(value, 'ch', [(i, i ^ 2) for i in range(n_ch)])  91.2 us
    pallas_call x7, Pallas kernels, finish(): call(kernel, 'finish', grid=(steps,), in_specs=specs, out_specs=pl.BlockS...  89.3 us
    pallas_call x4, Pallas kernels, lat_backward(): call(kernel, 'lat_backward', cost, grid=(per // step,), in_specs=[pl.Bloc...  32.6 us
    pallas_call x2, Pallas kernels, lon_forward(): call(kernel, 'lon_forward', grid=(count // step,), in_specs=[pl.BlockSpec...  32.3 us
    all_to_all x6, starting transfers between devices, across(): return lax.all_to_all(blocks, 'sp', 0, 0)  29.8 us
  transfers between devices with their start and end apart: 24, of which 16 were waited for; matrix products, arithmetic and copies ran while one was open for 0% of the time, Pallas kernels for 52%

profile of v5, /device:TPU:0, one launch (start us, length us, event | category | flops | bytes accessed | tf_op | source)
XLA Modules:
  0.0 893.1 jit_solution(8165767991613273764)
XLA Ops:
  0.0 6.3 slice.12
  7.5 3.4 kron_map.3.w_ref
  10.9 6.0 collective-permute-done.b_ref
  17.3 2.7 collective-permute-start.2
  20.0 10.7 %partial_map.10 = bf16[1,7920,128]{2,1,0:T(8,128)(2,1)} custom-call(bf16[64,192,1440]{2,1,0:T(8,128)(2,1)} %a_ref.23, bf16[64,32,1440]{2,1,0:T(8,128)(2,1)} %collective-permute-done.b_ref, bf16[704,2048]{1,0:T(8,128)(2,1)} %kron_map.3.w_ref), custom_call_target="tpu_custom_call" | custom-call | flops 1 | bytes 1 | tf_op jit(solution)/shard_map/partial_map/pallas_call | solution.py:414
  30.8 16.1 %lon_forward.2 = bf16[4,32,192,128]{3,2,1,0:T(8,128)(2,1)} custom-call(bf16[64,192,1440]{2,1,0:T(8,128)(2,1)} %a_ref.23, bf16[1440,512]{1,0:T(8,128)(2,1)} %constant.22.clone.t_ref), custom_call_target="tpu_custom_call" | custom-call | flops 1 | bytes 1 | tf_op jit(solution)/shard_map/lon_forward/pallas_call | solution.py:210
  46.9 10.6 %partial_map.11 = bf16[1,7920,128]{2,1,0:T(8,128)(2,1)} custom-call(bf16[64,192,1440]{2,1,0:T(8,128)(2,1)} %a_ref.23, bf16[64,32,1440]{2,1,0:T(8,128)(2,1)} %collective-permute-done.b_ref, bf16[704,2048]{1,0:T(8,128)(2,1)} %kron_map.3.w_ref), custom_call_target="tpu_custom_call" | custom-call | flops 1 | bytes 1 | tf_op jit(solution)/shard_map/partial_map/pallas_call | solution.py:414
  57.6 2.0 collective-permute-start.7
  59.6 5.8 all-to-all-start
  65.3 7.0 collective-permute-done.1.b_ref
  72.4 22.0 %partial_map.12 = bf16[3,7920,128]{2,1,0:T(8,128)(2,1)} custom-call(bf16[64,192,1440]{2,1,0:T(8,128)(2,1)} %a_ref.23, bf16[64,192,1440]{2,1,0:T(8,128)(2,1)} %collective-permute-done.1.b_ref, bf16[704,2048]{1,0:T(8,128)(2,1)} %kron_map.3.w_ref), custom_call_target="tpu_custom_call" | custom-call | flops 1 | bytes 1 | tf_op jit(solution)/shard_map/partial_map/pallas_call | solution.py:414
  94.4 26.2 %collective-permute-done.7.refs_3_ = bf16[1,7920,128]{2,1,0:T(8,128)(2,1)S(1)} collective-permute-done((bf16[1,7920,128]{2,1,0:T(8,128)(2,1)}, bf16[1,7920,128]{2,1,0:T(8,128)(2,1)S(1)}, u32[]{:S(2)}, u32[]{:S(2)}) %collective-permute-start.7) | collective-permute-done | bytes 2027552 | tf_op jit(solution)/shard_map/ppermute | solution.py:572
  120.9 22.4 %partial_map.13 = bf16[3,7920,128]{2,1,0:T(8,128)(2,1)} custom-call(bf16[64,192,1440]{2,1,0:T(8,128)(2,1)} %a_ref.23, bf16[64,192,1440]{2,1,0:T(8,128)(2,1)} %collective-permute-done.1.b_ref, bf16[704,2048]{1,0:T(8,128)(2,1)} %kron_map.3.w_ref), custom_call_target="tpu_custom_call" | custom-call | flops 120000004096 | bytes 1 | tf_op jit(solution)/shard_map/partial_map/pallas_call | solution.py:414
  143.3 4.1 kron_map.4.w_ref
  147.4 16.1 %lon_forward.3 = bf16[4,32,192,128]{3,2,1,0:T(8,128)(2,1)} custom-call(bf16[64,192,1440]{2,1,0:T(8,128)(2,1)} %a_ref.23, bf16[1440,512]{1,0:T(8,128)(2,1)} %constant.22.clone.t_ref), custom_call_target="tpu_custom_call" | custom-call | flops 1 | bytes 1 | tf_op jit(solution)/shard_map/lon_forward/pallas_call | solution.py:210
  163.6 21.8 %own_map.2.refs_0_.refs_1_ = f32[64,32,1440]{2,1,0:T(8,128)} custom-call(bf16[64,192,1440]{2,1,0:T(8,128)(2,1)} %a_ref.23, bf16[64,192,1440]{2,1,0:T(8,128)(2,1)} %collective-permute-done.1.b_ref, bf16[1024,2048]{1,0:T(8,128)(2,1)} %kron_map.4.w_ref), custom_call_target="tpu_custom_call" | custom-call | flops 1 | bytes 1 | tf_op jit(solution)/shard_map/own_map/pallas_call | solution.py:459
  185.4 18.1 %all-to-all-done.x_ref = bf16[4,32,192,128]{3,2,1,0:T(8,128)(2,1)} async-done(((bf16[4,32,192,128]{3,2,1,0:T(8,128)(2,1)}), bf16[4,32,192,128]{3,2,1,0:T(8,128)(2,1)}, u32[]{:S(2)}, u32[]{:S(2)}) %all-to-all-start) | async-done | bytes 6291488 | tf_op jit(solution)/shard_map/all_to_all | solution.py:575
  203.4 5.4 all-to-all-start.1
  209.7 2.5 kron_map.5.w_ref
  212.1 4.2 collective-permute-done.4.b0.b1
  216.3 2.0 copy-done.1
  218.3 6.2 pick_weights.1.w_ref
  224.5 1.4 slice.15.refs_0_
  225.9 9.8 %lat_forward.2 = bf16[128,32,384]{2,1,0:T(8,128)(2,1)} custom-call(bf16[4,32,192,128]{3,2,1,0:T(8,128)(2,1)} %all-to-all-done.x_ref, bf16[768,768]{1,0:T(8,128)(2,1)} %constant.24.clone.t_ref.refs_2_.refs_1_), custom_call_target="tpu_custom_call" | custom-call | flops 1 | bytes 1 | tf_op jit(solution)/shard_map/lat_forward/pallas_call | solution.py:240
  235.7 17.4 %collective-permute-done.8.refs_3_ = bf16[3,7920,128]{2,1,0:T(8,128)(2,1)} collective-permute-done((bf16[3,7920,128]{2,1,0:T(8,128)(2,1)}, bf16[3,7920,128]{2,1,0:T(8,128)(2,1)}, u32[]{:S(2)}, u32[]{:S(2)}) %collective-permute-start.8) | collective-permute-done | bytes 6082592 | tf_op jit(solution)/shard_map/ppermute | solution.py:572
  253.8 82.4 %own_map.3.refs_1_ = f32[64,160,1440]{2,1,0:T(8,128)} custom-call(bf16[64,192,1440]{2,1,0:T(8,128)(2,1)} %a_ref.23, bf16[64,192,1440]{2,1,0:T(8,128)(2,1)} %collective-permute-done.1.b_ref, bf16[1024,2048]{1,0:T(8,128)(2,1)} %kron_map.4.w_ref), custom_call_target="tpu_custom_call" | custom-call | flops 49999998976 | bytes 1 | tf_op jit(solution)/shard_map/own_map/pallas_call | solution.py:459
  336.2 10.3 %all-to-all-done.1.x_ref = bf16[4,32,192,128]{3,2,1,0:T(8,128)(2,1)} async-done(((bf16[4,32,192,128]{3,2,1,0:T(8,128)(2,1)}), bf16[4,32,192,128]{3,2,1,0:T(8,128)(2,1)}, u32[]{:S(2)}, u32[]{:S(2)}) %all-to-all-start.1) | async-done | bytes 6291488 | tf_op jit(solution)/shard_map/all_to_all | solution.py:575
  346.4 9.9 %lat_forward.3 = bf16[128,32,384]{2,1,0:T(8,128)(2,1)} custom-call(bf16[4,32,192,128]{3,2,1,0:T(8,128)(2,1)} %all-to-all-done.1.x_ref, bf16[768,768]{1,0:T(8,128)(2,1)} %constant.24.clone.t_ref.refs_2_.refs_1_), custom_call_target="tpu_custom_call" | custom-call | flops 1 | bytes 1 | tf_op jit(solution)/shard_map/lat_forward/pallas_call | solution.py:240
  356.3 5.9 collective-permute-done.6.refs_3_
  362.2 1.7 copy-done.3
  363.9 17.4 %mix.1 = (f32[2,64,64,384]{3,2,1,0:T(8,128)}, f32[2,20,64,384]{3,2,1,0:T(8,128)}, bf16[5,28,64,128]{3,2,1,0:T(8,128)(2,1)}, bf16[5,16,64,128]{3,2,1,0:T(8,128)(2,1)}) custom-call(bf16[2,64,128,128]{3,2,1,0:T(8,128)(2,1)} %pick_weights.1.w_ref, bf16[2,64,32,384]{3,2,1,0:T(8,128)(2,1)} %bitcast.5, bf16[2,64,32,384]{3,2,1,0:T(8,128)(2,1)} %bitcast.7, ...), custom_call_target="tpu_custom_call" | custom-call | flops 1 | bytes 1 | tf_op jit(solution)/shard_map/mix/pallas_call | solution.py:293
  381.3 3.5 collective-permute-done.9.refs_3_
  385.8 7.8 lat_backward.5
  393.6 4.8 all-to-all-start.2
  398.4 1.1 collective-permute-start.13
  399.5 7.7 lat_backward.7
  407.3 10.7 %partial_map.15 = bf16[1,7920,128]{2,1,0:T(8,128)(2,1)} custom-call(bf16[64,192,1440]{2,1,0:T(8,128)(2,1)} %a_ref.23, bf16[64,192,1440]{2,1,0:T(8,128)(2,1)} %collective-permute-done.1.b_ref, bf16[704,2048]{1,0:T(8,128)(2,1)} %kron_map.3.w_ref), custom_call_target="tpu_custom_call" | custom-call | flops 1 | bytes 1 | tf_op jit(solution)/shard_map/partial_map/pallas_call | solution.py:414
  417.9 22.0 %partial_map.17 = bf16[3,7920,128]{2,1,0:T(8,128)(2,1)} custom-call(bf16[64,192,1440]{2,1,0:T(8,128)(2,1)} %a_ref.23, bf16[64,192,1440]{2,1,0:T(8,128)(2,1)} %collective-permute-done.1.b_ref, bf16[704,2048]{1,0:T(8,128)(2,1)} %kron_map.3.w_ref), custom_call_target="tpu_custom_call" | custom-call | flops 1 | bytes 1 | tf_op jit(solution)/shard_map/partial_map/pallas_call | solution.py:414
  440.0 1.0 collective-permute-start.11
  441.0 6.7 lat_backward.4
  447.7 1.0 collective-permute-start.14
  448.7 17.3 %collective-permute-done.13.refs_0_ = bf16[5,28,64,128]{3,2,1,0:T(8,128)(2,1)} collective-permute-done((bf16[5,28,64,128]{3,2,1,0:T(8,128)(2,1)}, bf16[5,28,64,128]{3,2,1,0:T(8,128)(2,1)}, u32[]{:S(2)}, u32[]{:S(2)}) %collective-permute-start.13) | collective-permute-done | bytes 2293792 | tf_op jit(solution)/shard_map/ppermute | solution.py:572
  466.0 10.4 %lat_backward.6 = bf16[4,28,192,128]{3,2,1,0:T(8,128)(2,1)} custom-call(f32[2,64,64,384]{3,2,1,0:T(8,128)} %get-tuple-element.53.own_ref, bf16[5,28,64,128]{3,2,1,0:T(8,128)(2,1)} %collective-permute-done.13.refs_0_, f32[64,1,384]{2,1,0:T(1,128)} %copy-done.5, bf16[768,768]{1,0:T(8,128)(2,1)} %constant.24.clone.t_ref.refs_2_.refs_1_), custom_call_target="tpu_custom_call" | custom-call | flops 1 | bytes 1 | tf_op jit(solution)/shard_map/lat_backward/pallas_call | solution.py:347
  476.5 7.5 all-to-all-done.2.refs_0_
  484.0 4.8 all-to-all-start.3
  488.8 19.9 %partial_map.14 = bf16[4,3600,128]{2,1,0:T(8,128)(2,1)} custom-call(bf16[64,192,1440]{2,1,0:T(8,128)(2,1)} %a_ref.23, bf16[64,192,1440]{2,1,0:T(8,128)(2,1)} %collective-permute-done.1.b_ref, bf16[320,2048]{1,0:T(8,128)(2,1)} %kron_map.5.w_ref, bf16[4,20,192,128]{3,2,1,0:T(8,128)(2,1)} %all-to-all-done.2.refs_0_, ...), custom_call_target="tpu_custom_call" | custom-call | flops 120000004096 | bytes 1 | tf_op jit(solution)/shard_map/partial_map/pallas_call | solution.py:414
  510.5 65.4 %all-to-all-done.3.refs_6_.refs_7_ = bf16[4,20,192,128]{3,2,1,0:T(8,128)(2,1)} async-done(((bf16[4,20,192,128]{3,2,1,0:T(8,128)(2,1)}), bf16[4,20,192,128]{3,2,1,0:T(8,128)(2,1)}, u32[]{:S(2)}, u32[]{:S(2)}) %all-to-all-start.3) | async-done | bytes 3932192 | tf_op jit(solution)/shard_map/all_to_all | solution.py:575
  575.9 5.1 all-to-all-start.4
  581.0 19.9 %partial_map.16 = bf16[4,3600,128]{2,1,0:T(8,128)(2,1)} custom-call(bf16[64,192,1440]{2,1,0:T(8,128)(2,1)} %a_ref.23, bf16[64,192,1440]{2,1,0:T(8,128)(2,1)} %collective-permute-done.1.b_ref, bf16[320,2048]{1,0:T(8,128)(2,1)} %kron_map.5.w_ref, bf16[4,20,192,128]{3,2,1,0:T(8,128)(2,1)} %all-to-all-done.2.refs_0_, ...), custom_call_target="tpu_custom_call" | custom-call | flops 120000004096 | bytes 1 | tf_op jit(solution)/shard_map/partial_map/pallas_call | solution.py:414
  600.9 100.8 %all-to-all-done.4.refs_4_.refs_5_ = bf16[4,28,192,128]{3,2,1,0:T(8,128)(2,1)} async-done(((bf16[4,28,192,128]{3,2,1,0:T(8,128)(2,1)}), bf16[4,28,192,128]{3,2,1,0:T(8,128)(2,1)}, u32[]{:S(2)}, u32[]{:S(2)}) %all-to-all-start.4) | async-done | bytes 5505056 | tf_op jit(solution)/shard_map/all_to_all | solution.py:575
  701.7 4.0 all-to-all-start.5
  705.7 16.1 %partial_map.18 = bf16[3,3600,128]{2,1,0:T(8,128)(2,1)} custom-call(bf16[64,192,1440]{2,1,0:T(8,128)(2,1)} %a_ref.23, bf16[64,192,1440]{2,1,0:T(8,128)(2,1)} %collective-permute-done.1.b_ref, bf16[320,2048]{1,0:T(8,128)(2,1)} %kron_map.5.w_ref, bf16[4,20,192,128]{3,2,1,0:T(8,128)(2,1)} %all-to-all-done.2.refs_0_, ...), custom_call_target="tpu_custom_call" | custom-call | flops 40000000000 | bytes 1 | tf_op jit(solution)/shard_map/partial_map/pallas_call | solution.py:414
  722.4 1.4 collective-permute-start.16
  723.8 8.5 partial_map.19
  733.0 42.9 %all-to-all-done.5.refs_5_.refs_6_ = bf16[4,16,192,128]{3,2,1,0:T(8,128)(2,1)S(1)} async-done(((bf16[4,16,192,128]{3,2,1,0:T(8,128)(2,1)}), bf16[4,16,192,128]{3,2,1,0:T(8,128)(2,1)S(1)}, u32[]{:S(2)}, u32[]{:S(2)}) %all-to-all-start.5) | async-done | bytes 3145760 | tf_op jit(solution)/shard_map/all_to_all | solution.py:575
  775.8 1.6 copy-done
  777.5 9.4 %finish.7.refs_0_ = bf16[64,192,1440]{2,1,0:T(8,128)(2,1)} custom-call(f32[64,32,1440]{2,1,0:T(8,128)} %own_map.2.refs_0_.refs_1_, bf16[512,1440]{1,0:T(8,128)(2,1)} %constant.23.clone.refs_1_.refs_2_, bf16[1,7920,128]{2,1,0:T(8,128)(2,1)} %collective-permute-done.3.refs_2_, bf16[4,3600,128]{2,1,0:T(8,128)(2,1)} %collective-permute-done.12.refs_3_.refs_4_, ...), custom_call_target="tpu_custom_call" | custom-call | flops 1 | bytes 1 | tf_op jit(solution)/shard_map/finish/pallas_call | solution.py:539
  786.9 9.4 %finish.8.refs_0_ = bf16[64,192,1440]{2,1,0:T(8,128)(2,1)} custom-call(bf16[64,192,1440]{2,1,0:T(8,128)(2,1)} %finish.7.refs_0_, f32[64,32,1440]{2,1,0:T(8,128)} %own_map.2.refs_0_.refs_1_, bf16[512,1440]{1,0:T(8,128)(2,1)} %constant.23.clone.refs_1_.refs_2_, bf16[1,7920,128]{2,1,0:T(8,128)(2,1)} %copy-done.4, ...), custom_call_target="tpu_custom_call", output_to_operand_aliasing={{}: (0, {})} | custom-call | flops 1 | bytes 1 | tf_op jit(solution)/shard_map/finish/pallas_call | solution.py:539
  796.3 13.0 %finish.9.refs_0_ = bf16[64,192,1440]{2,1,0:T(8,128)(2,1)} custom-call(bf16[64,192,1440]{2,1,0:T(8,128)(2,1)} %finish.8.refs_0_, f32[64,160,1440]{2,1,0:T(8,128)} %own_map.3.refs_1_, bf16[512,1440]{1,0:T(8,128)(2,1)} %constant.23.clone.refs_1_.refs_2_, bf16[3,7920,128]{2,1,0:T(8,128)(2,1)} %collective-permute-done.8.refs_3_, ...), custom_call_target="tpu_custom_call", output_to_operand_aliasing={{}: (0, {})} | custom-call | flops 1 | bytes 1 | tf_op jit(solution)/shard_map/finish/pallas_call | solution.py:539
  809.3 9.6 %finish.10.refs_0_ = bf16[64,192,1440]{2,1,0:T(8,128)(2,1)} custom-call(bf16[64,192,1440]{2,1,0:T(8,128)(2,1)} %finish.9.refs_0_, f32[64,160,1440]{2,1,0:T(8,128)} %own_map.3.refs_1_, bf16[512,1440]{1,0:T(8,128)(2,1)} %constant.23.clone.refs_1_.refs_2_, bf16[3,7920,128]{2,1,0:T(8,128)(2,1)} %collective-permute-done.8.refs_3_, ...), custom_call_target="tpu_custom_call", output_to_operand_aliasing={{}: (0, {})} | custom-call | flops 1 | bytes 1 | tf_op jit(solution)/shard_map/finish/pallas_call | solution.py:539
  818.9 19.2 %finish.11.refs_0_ = bf16[64,192,1440]{2,1,0:T(8,128)(2,1)} custom-call(bf16[64,192,1440]{2,1,0:T(8,128)(2,1)} %finish.10.refs_0_, f32[64,160,1440]{2,1,0:T(8,128)} %own_map.3.refs_1_, bf16[512,1440]{1,0:T(8,128)(2,1)} %constant.23.clone.refs_1_.refs_2_, bf16[3,7920,128]{2,1,0:T(8,128)(2,1)} %collective-permute-done.9.refs_3_, ...), custom_call_target="tpu_custom_call", output_to_operand_aliasing={{}: (0, {})} | custom-call | flops 1 | bytes 1 | tf_op jit(solution)/shard_map/finish/pallas_call | solution.py:539
  838.1 25.9 %collective-permute-done.16.refs_4_ = bf16[3,3600,128]{2,1,0:T(8,128)(2,1)} collective-permute-done((bf16[3,3600,128]{2,1,0:T(8,128)(2,1)}, bf16[3,3600,128]{2,1,0:T(8,128)(2,1)}, u32[]{:S(2)}, u32[]{:S(2)}) %collective-permute-start.16) | collective-permute-done | bytes 2764832 | tf_op jit(solution)/shard_map/ppermute | solution.py:572
  864.0 19.2 %finish.12.refs_0_ = bf16[64,192,1440]{2,1,0:T(8,128)(2,1)} custom-call(bf16[64,192,1440]{2,1,0:T(8,128)(2,1)} %finish.11.refs_0_, f32[64,160,1440]{2,1,0:T(8,128)} %own_map.3.refs_1_, bf16[512,1440]{1,0:T(8,128)(2,1)} %constant.23.clone.refs_1_.refs_2_, bf16[3,7920,128]{2,1,0:T(8,128)(2,1)} %collective-permute-done.14.refs_3_, ...), custom_call_target="tpu_custom_call", output_to_operand_aliasing={{}: (0, {})} | custom-call | flops 1 | bytes 1 | tf_op jit(solution)/shard_map/finish/pallas_call | solution.py:539
  883.2 9.5 %finish.13 = bf16[64,192,1440]{2,1,0:T(8,128)(2,1)} custom-call(bf16[64,192,1440]{2,1,0:T(8,128)(2,1)} %finish.12.refs_0_, f32[64,160,1440]{2,1,0:T(8,128)} %own_map.3.refs_1_, bf16[512,1440]{1,0:T(8,128)(2,1)} %constant.23.clone.refs_1_.refs_2_, bf16[1,7920,128]{2,1,0:T(8,128)(2,1)} %collective-permute-done.11.refs_3_, ...), custom_call_target="tpu_custom_call", output_to_operand_aliasing={{}: (0, {})} | custom-call | flops 1 | bytes 1 | tf_op jit(solution)/shard_map/finish/pallas_call | solution.py:539
  (45 shorter events, 7.5 us)
Async XLA Ops:
  0.0 6.7 copy-start.8
  0.0 17.2 %copy-start.7 = (f32[64,320]{1,0:T(8,128)S(1)}, f32[64,320]{1,0:T(8,128)}, u32[]{:S(2)}) copy-start(f32[64,320]{1,0:T(8,128)} %param.9) | copy-start | bytes 245764
  6.3 10.6 %collective-permute-start = (bf16[64,32,1440]{2,1,0:T(8,128)(2,1)}, bf16[64,32,1440]{2,1,0:T(8,128)(2,1)}, u32[]{:S(2)}, u32[]{:S(2)}) collective-permute-start(bf16[64,32,1440]{2,1,0:T(8,128)(2,1)} %slice.12), channel_id=1, source_target_pairs={{0,1},{1,0},{2,3},{3,2},{4,5},{5,4},{6,7},{7,6},{8,9},{9,8},{10,11... | collective-permute-start | bytes 17694728 | tf_op jit(solution)/shard_map/ppermute | solution.py:569
  16.9 55.5 %collective-permute-start.1 = (bf16[64,192,1440]{2,1,0:T(8,128)(2,1)}, bf16[64,192,1440]{2,1,0:T(8,128)(2,1)}, u32[]{:S(2)}, u32[]{:S(2)}) collective-permute-start(bf16[64,192,1440]{2,1,0:T(8,128)(2,1)} %a_ref.23), channel_id=1, source_target_pairs={{0,1},{1,0},{2,3},{3,2},{4,5},{5,4},{6,7},{7,6},{8,9},{9,8},{10,11... | collective-permute-start | bytes 106168328 | tf_op jit(solution)/shard_map/ppermute | solution.py:569
  17.3 13.4 %copy-start.5 = (f32[64,1,384]{2,1,0:T(1,128)}, f32[64,1,384]{2,1,0:T(1,128)S(1)}, u32[]{:S(2)}) copy-start(f32[64,1,384]{2,1,0:T(1,128)S(1)} %reshape.12.refs_1_.refs_0_) | copy-start | bytes 294916
  17.3 13.4 %collective-permute-start.2 = (f32[64,1,384]{2,1,0:T(1,128)S(1)}, f32[64,1,384]{2,1,0:T(1,128)S(1)}, u32[]{:S(2)}, u32[]{:S(2)}) collective-permute-start(f32[64,1,384]{2,1,0:T(1,128)S(1)} %reshape.12.refs_1_.refs_0_), channel_id=1, source_target_pairs={{0,2},{1,3},{2,0},{3,1},{4,6},{5,7},{6,4},{7,5},{8,10},{9,11},{10,... | collective-permute-start | bytes 294920 | tf_op jit(solution)/shard_map/ppermute | solution.py:572
  30.7 16.2 %copy-start.9 = (f32[64,1,384]{2,1,0:T(1,128)}, f32[64,1,384]{2,1,0:T(1,128)S(1)}, u32[]{:S(2)}) copy-start(f32[64,1,384]{2,1,0:T(1,128)S(1)} %collective-permute-done.2) | copy-start | bytes 294916
  30.7 63.7 %collective-permute-start.3 = (bf16[1,7920,128]{2,1,0:T(8,128)(2,1)}, bf16[1,7920,128]{2,1,0:T(8,128)(2,1)}, u32[]{:S(2)}, u32[]{:S(2)}) collective-permute-start(bf16[1,7920,128]{2,1,0:T(8,128)(2,1)} %partial_map.10), channel_id=1, source_target_pairs={{0,2},{1,3},{2,0},{3,1},{4,6},{5,7},{6,4},{7,5},{8,10},{9,11},{10,... | collective-permute-start | bytes 6082568 | tf_op jit(solution)/shard_map/ppermute | solution.py:572
  57.6 63.0 %collective-permute-start.7 = (bf16[1,7920,128]{2,1,0:T(8,128)(2,1)}, bf16[1,7920,128]{2,1,0:T(8,128)(2,1)S(1)}, u32[]{:S(2)}, u32[]{:S(2)}) collective-permute-start(bf16[1,7920,128]{2,1,0:T(8,128)(2,1)} %partial_map.11), channel_id=1, source_target_pairs={{0,2},{1,3},{2,0},{3,1},{4,6},{5,7},{6,4},{7,5},{8,10},{9,11},{10,... | collective-permute-start | bytes 6082568 | tf_op jit(solution)/shard_map/ppermute | solution.py:572
  59.6 143.9 %all-to-all-start = ((bf16[4,32,192,128]{3,2,1,0:T(8,128)(2,1)}), bf16[4,32,192,128]{3,2,1,0:T(8,128)(2,1)}, u32[]{:S(2)}, u32[]{:S(2)}) async-start(bf16[4,32,192,128]{3,2,1,0:T(8,128)(2,1)} %lon_forward.2), calls=%async_computation | async-start | bytes 12582912 | tf_op jit(solution)/shard_map/all_to_all | solution.py:575
  120.6 22.7 %copy-start.4 = (bf16[1,7920,128]{2,1,0:T(8,128)(2,1)}, bf16[1,7920,128]{2,1,0:T(8,128)(2,1)S(1)}, u32[]{:S(2)}) copy-start(bf16[1,7920,128]{2,1,0:T(8,128)(2,1)S(1)} %collective-permute-done.7.refs_3_) | copy-start | bytes 6082564
  120.6 132.6 %collective-permute-start.8 = (bf16[3,7920,128]{2,1,0:T(8,128)(2,1)}, bf16[3,7920,128]{2,1,0:T(8,128)(2,1)}, u32[]{:S(2)}, u32[]{:S(2)}) collective-permute-start(bf16[3,7920,128]{2,1,0:T(8,128)(2,1)} %partial_map.12), channel_id=1, source_target_pairs={{0,2},{1,3},{2,0},{3,1},{4,6},{5,7},{6,4},{7,5},{8,10},{9,11},{10,... | collective-permute-start | bytes 18247688 | tf_op jit(solution)/shard_map/ppermute | solution.py:572
  185.4 23.6 %copy-start.6 = (bf16[128,64]{1,0:T(8,128)(2,1)S(1)}, bf16[128,64]{1,0:T(8,128)(2,1)}, u32[]{:S(2)}) copy-start(bf16[128,64]{1,0:T(8,128)(2,1)} %get-tuple-element.76) | copy-start | bytes 49156
  203.4 143.0 %all-to-all-start.1 = ((bf16[4,32,192,128]{3,2,1,0:T(8,128)(2,1)}), bf16[4,32,192,128]{3,2,1,0:T(8,128)(2,1)}, u32[]{:S(2)}, u32[]{:S(2)}) async-start(bf16[4,32,192,128]{3,2,1,0:T(8,128)(2,1)} %lon_forward.3), calls=%async_computation.1 | async-start | bytes 12582912 | tf_op jit(solution)/shard_map/all_to_all | solution.py:575
  208.9 7.4 collective-permute-start.4
  216.3 2.0 copy-start.1
  235.6 120.7 %collective-permute-start.5 = (bf16[2,64,32,384]{3,2,1,0:T(8,128)(2,1)}, bf16[2,64,32,384]{3,2,1,0:T(8,128)(2,1)S(1)}, u32[]{:S(2)}, u32[]{:S(2)}) collective-permute-start(bf16[2,64,32,384]{3,2,1,0:T(8,128)(2,1)} %bitcast.4), channel_id=1, source_target_pairs={{0,1},{1,0},{2,3},{3,2},{4,5},{5,4},{6,7},{7,6},{8,9},{9,8},{10,11... | collective-permute-start | bytes 9437192 | tf_op jit(solution)/shard_map/ppermute | solution.py:569
  253.2 131.7 %collective-permute-start.9 = (bf16[3,7920,128]{2,1,0:T(8,128)(2,1)}, bf16[3,7920,128]{2,1,0:T(8,128)(2,1)}, u32[]{:S(2)}, u32[]{:S(2)}) collective-permute-start(bf16[3,7920,128]{2,1,0:T(8,128)(2,1)} %partial_map.13), channel_id=1, source_target_pairs={{0,2},{1,3},{2,0},{3,1},{4,6},{5,7},{6,4},{7,5},{8,10},{9,11},{10,... | collective-permute-start | bytes 18247688 | tf_op jit(solution)/shard_map/ppermute | solution.py:572
  356.3 5.9 collective-permute-start.6
  356.3 5.9 copy-start.2
  362.2 1.7 copy-start.3
  384.9 55.1 %collective-permute-start.10 = (bf16[5,16,64,128]{3,2,1,0:T(8,128)(2,1)}, bf16[5,16,64,128]{3,2,1,0:T(8,128)(2,1)S(1)}, u32[]{:S(2)}, u32[]{:S(2)}) collective-permute-start(bf16[5,16,64,128]{3,2,1,0:T(8,128)(2,1)} %get-tuple-element.58), channel_id=1, source_target_pairs={{0,2},{1,3},{2,0},{3,1},{4,6},{5,7},{6,4},{7,5},{8,10},{9,11},{10,... | collective-permute-start | bytes 3932168 | tf_op jit(solution)/shard_map/ppermute | solution.py:572
  393.6 90.4 %all-to-all-start.2 = ((bf16[4,20,192,128]{3,2,1,0:T(8,128)(2,1)}), bf16[4,20,192,128]{3,2,1,0:T(8,128)(2,1)}, u32[]{:S(2)}, u32[]{:S(2)}) async-start(bf16[4,20,192,128]{3,2,1,0:T(8,128)(2,1)} %lat_backward.5), calls=%async_computation.2 | async-start | bytes 7864320 | tf_op jit(solution)/shard_map/all_to_all | solution.py:575
  398.4 67.7 %collective-permute-start.13 = (bf16[5,28,64,128]{3,2,1,0:T(8,128)(2,1)}, bf16[5,28,64,128]{3,2,1,0:T(8,128)(2,1)}, u32[]{:S(2)}, u32[]{:S(2)}) collective-permute-start(bf16[5,28,64,128]{3,2,1,0:T(8,128)(2,1)} %get-tuple-element.65), channel_id=1, source_target_pairs={{0,2},{1,3},{2,0},{3,1},{4,6},{5,7},{6,4},{7,5},{8,10},{9,11},{10,... | collective-permute-start | bytes 6881288 | tf_op jit(solution)/shard_map/ppermute | solution.py:572
  440.0 1.1 copy-start.10
  440.0 69.5 %collective-permute-start.11 = (bf16[1,7920,128]{2,1,0:T(8,128)(2,1)}, bf16[1,7920,128]{2,1,0:T(8,128)(2,1)}, u32[]{:S(2)}, u32[]{:S(2)}) collective-permute-start(bf16[1,7920,128]{2,1,0:T(8,128)(2,1)} %partial_map.15), channel_id=1, source_target_pairs={{0,2},{1,3},{2,0},{3,1},{4,6},{5,7},{6,4},{7,5},{8,10},{9,11},{10,... | collective-permute-start | bytes 6082568 | tf_op jit(solution)/shard_map/ppermute | solution.py:572
  447.7 274.1 %collective-permute-start.14 = (bf16[3,7920,128]{2,1,0:T(8,128)(2,1)}, bf16[3,7920,128]{2,1,0:T(8,128)(2,1)}, u32[]{:S(2)}, u32[]{:S(2)}) collective-permute-start(bf16[3,7920,128]{2,1,0:T(8,128)(2,1)} %partial_map.17), channel_id=1, source_target_pairs={{0,2},{1,3},{2,0},{3,1},{4,6},{5,7},{6,4},{7,5},{8,10},{9,11},{10,... | collective-permute-start | bytes 18247688 | tf_op jit(solution)/shard_map/ppermute | solution.py:572
  484.0 91.9 %all-to-all-start.3 = ((bf16[4,20,192,128]{3,2,1,0:T(8,128)(2,1)}), bf16[4,20,192,128]{3,2,1,0:T(8,128)(2,1)}, u32[]{:S(2)}, u32[]{:S(2)}) async-start(bf16[4,20,192,128]{3,2,1,0:T(8,128)(2,1)} %lat_backward.7), calls=%async_computation.3 | async-start | bytes 7864320 | tf_op jit(solution)/shard_map/all_to_all | solution.py:575
  509.5 212.9 %collective-permute-start.12 = (bf16[4,3600,128]{2,1,0:T(8,128)(2,1)}, bf16[4,3600,128]{2,1,0:T(8,128)(2,1)}, u32[]{:S(2)}, u32[]{:S(2)}) collective-permute-start(bf16[4,3600,128]{2,1,0:T(8,128)(2,1)} %partial_map.14), channel_id=1, source_target_pairs={{0,2},{1,3},{2,0},{3,1},{4,6},{5,7},{6,4},{7,5},{8,10},{9,11},{10,... | collective-permute-start | bytes 11059208 | tf_op jit(solution)/shard_map/ppermute | solution.py:572
  575.9 125.9 %all-to-all-start.4 = ((bf16[4,28,192,128]{3,2,1,0:T(8,128)(2,1)}), bf16[4,28,192,128]{3,2,1,0:T(8,128)(2,1)}, u32[]{:S(2)}, u32[]{:S(2)}) async-start(bf16[4,28,192,128]{3,2,1,0:T(8,128)(2,1)} %lat_backward.6), calls=%async_computation.4 | async-start | bytes 11010048 | tf_op jit(solution)/shard_map/all_to_all | solution.py:575
  701.7 74.1 %all-to-all-start.5 = ((bf16[4,16,192,128]{3,2,1,0:T(8,128)(2,1)}), bf16[4,16,192,128]{3,2,1,0:T(8,128)(2,1)S(1)}, u32[]{:S(2)}, u32[]{:S(2)}) async-start(bf16[4,16,192,128]{3,2,1,0:T(8,128)(2,1)} %lat_backward.4), calls=%async_computation.5 | async-start | bytes 6291456 | tf_op jit(solution)/shard_map/all_to_all | solution.py:575
  721.8 87.5 %collective-permute-start.15 = (bf16[4,3600,128]{2,1,0:T(8,128)(2,1)}, bf16[4,3600,128]{2,1,0:T(8,128)(2,1)}, u32[]{:S(2)}, u32[]{:S(2)}) collective-permute-start(bf16[4,3600,128]{2,1,0:T(8,128)(2,1)} %partial_map.16), channel_id=1, source_target_pairs={{0,2},{1,3},{2,0},{3,1},{4,6},{5,7},{6,4},{7,5},{8,10},{9,11},{10,... | collective-permute-start | bytes 11059208 | tf_op jit(solution)/shard_map/ppermute | solution.py:572
  722.4 141.6 %collective-permute-start.16 = (bf16[3,3600,128]{2,1,0:T(8,128)(2,1)}, bf16[3,3600,128]{2,1,0:T(8,128)(2,1)}, u32[]{:S(2)}, u32[]{:S(2)}) collective-permute-start(bf16[3,3600,128]{2,1,0:T(8,128)(2,1)} %partial_map.18), channel_id=1, source_target_pairs={{0,2},{1,3},{2,0},{3,1},{4,6},{5,7},{6,4},{7,5},{8,10},{9,11},{10,... | collective-permute-start | bytes 8294408 | tf_op jit(solution)/shard_map/ppermute | solution.py:572
  732.4 150.8 %collective-permute-start.17 = (bf16[1,3600,128]{2,1,0:T(8,128)(2,1)}, bf16[1,3600,128]{2,1,0:T(8,128)(2,1)}, u32[]{:S(2)}, u32[]{:S(2)}) collective-permute-start(bf16[1,3600,128]{2,1,0:T(8,128)(2,1)} %partial_map.19), channel_id=1, source_target_pairs={{0,2},{1,3},{2,0},{3,1},{4,6},{5,7},{6,4},{7,5},{8,10},{9,11},{10,... | collective-permute-start | bytes 2764808 | tf_op jit(solution)/shard_map/ppermute | solution.py:572
  775.8 1.6 copy-start
